TPU v7x, 32 devices: a whole 2x2x4 slice. The times are simulated.
32 devices in a mesh: req: 4 (over z), seq: 8 (over y, x, core).
Axes of the slice: x: 2, y: 2, z: 4, core: 2. Of those that a mesh axis runs over, the one named last changes fastest.
Arguments:
- queries: bfloat16 [4, 128, 4096], P('req', 'seq'), may hold values from -160 to 160
- kv_cache: bfloat16 [4, 4096, 2, 256], P('req', 'seq'), may hold values from -6 to 6
- tree_kv: bfloat16 [4, 128, 2, 256], P('req', 'seq'), may hold values from -14 to 14
- context_lengths: int32 [4], P('req'), may hold values from 512 to 4096, as said below
- tree_parents: int32 [4, 128], P('req'), may hold values from -1 to 126, as said below
- resid: bfloat16 [4, 128, 4096], P('req', 'seq'), may hold values from -6 to 6
- out_weight: bfloat16 [4096, 4096], P('seq'), may hold values from -0.5 to 0.5
- norm_gain: bfloat16 [4096], replicated, may hold values from 0.099609375 to 1.8984375
- expert_ids: int32 [4, 128, 8], P('req'), may hold values from 0 to 63, all different within a row; in each aligned block of 128 rows (0 to 127, 128 to 255, ..., all dimensions but the last counted through in order) at most 32 rows name the same one
- gate_weights: bfloat16 [4, 128, 8], P('req'), may hold values from 0.049804688 to 0.5
- w_gate: bfloat16 [512, 4096, 128], P(('req', 'seq')), may hold values from -0.09375 to 0.09375
- w_up: bfloat16 [512, 4096, 128], P(('req', 'seq')), may hold values from -0.09375 to 0.09375
- w_down: bfloat16 [512, 128, 4096], P(('req', 'seq')), may hold values from -0.375 to 0.375
Outputs:
- attended: bfloat16 [4, 128, 4096], P('req', 'seq')
- expert_sum: bfloat16 [4, 128, 4096], P('req', 'seq')
Inputs may be any that keep to these rules, and one draw needn't show every extreme that they name: `expert_ids`: each row names 8 different experts; among the rows of one request no expert is named by more than 32 rows. `tree_parents`: each request holds 4 trees of 32 nodes in a row; a tree's first node has parent -1, every other node's parent is an earlier node of the same tree; the request's last node has parent 128 - 2. `context_lengths`: at least one request uses all 4096 positions.
All inputs are finite; a program needn't handle non-finite values.
Results may differ from a plain program's by a relative error of at most 0.01615.
Values may be sent and summed in bfloat16 or wider, within the bound.
No kernel may reach another device: no remote copies, remote signals or barrier semaphores. Data moves between devices by JAX's collectives and lax.ppermute only.
A program may use at most 128 MiB of HBM per device.

v0:
```python
import jax
import jax.numpy as jnp
from jax import lax
from jax.sharding import PartitionSpec as P

DH = 128
HQ = 32
KVH = 2
EXPERTS = 64
CAP = 32
SPLIT = 8


NEG = -1e30
EPS = 1e-06


def ancestry(parents):
    count = parents.shape[0]
    node = jnp.arange(count, dtype=jnp.int32)
    linked = (parents[:, None] == node[None, :]) | (node[:, None] == node[None, :])
    reach = linked.astype(jnp.bfloat16)
    hops = 1
    while hops < count:
        paths = jnp.dot(reach, reach, preferred_element_type=jnp.float32)
        reach = jnp.minimum(paths, 1.0).astype(jnp.bfloat16)
        hops = hops * 2
    return reach > 0.5


def shard_partial(query, block, length, first):
    rows = query.shape[0]
    group = HQ // KVH
    span = block.shape[0]
    keys = block[:, 0].reshape(span, KVH, DH)
    values = block[:, 1].reshape(span, KVH, DH)
    heads = query.reshape(rows, KVH, group, DH)
    scores = jnp.einsum("rkgd,tkd->rkgt", heads, keys, preferred_element_type=jnp.float32) * DH ** (
        -0.5
    )
    valid = first + jnp.arange(span, dtype=jnp.int32) < length
    top = jnp.max(jnp.where(valid, scores, NEG), axis=-1)
    weights = jnp.where(valid, jnp.exp(scores - top[..., None]), 0.0)
    total = jnp.sum(weights, axis=-1)
    out = jnp.einsum(
        "rkgt,tkd->rkgd", weights.astype(jnp.bfloat16), values, preferred_element_type=jnp.float32
    )
    return (out.reshape(rows, HQ * DH), top.reshape(rows, HQ), total.reshape(rows, HQ))


def normalize(base, attended, gain):
    mid = (base.astype(jnp.float32) + attended.astype(jnp.float32)).astype(jnp.bfloat16)
    midf = lax.optimization_barrier(mid).astype(jnp.float32)
    factor = lax.rsqrt(jnp.mean(midf * midf, axis=-1, keepdims=True) + EPS)
    return (midf * factor * gain.astype(jnp.float32)).astype(jnp.bfloat16)


def body(
    queries,
    kv_cache,
    tree_kv,
    context_lengths,
    tree_parents,
    resid,
    out_weight,
    norm_gain,
    expert_ids,
    gate_weights,
    w_gate,
    w_up,
    w_down,
):
    here = lax.axis_index("seq")
    parts = lax.axis_size("seq")
    own_rows = queries.shape[1]
    query_all, tree_all, resid_all = (
        lax.all_gather(queries, "seq", axis=1, tiled=True),
        lax.all_gather(tree_kv, "seq", axis=1, tiled=True),
        lax.all_gather(resid, "seq", axis=1, tiled=True),
    )
    query = query_all[0]
    rows = query.shape[0]
    length = context_lengths[0]
    block = kv_cache[0]
    span = block.shape[0]
    out, top, total = shard_partial(query, block, length, here * span)
    got_out, got_top, got_total = (
        lax.all_to_all(out, "seq", split_axis=1, concat_axis=0, tiled=True),
        lax.all_to_all(top, "seq", split_axis=1, concat_axis=0, tiled=True),
        lax.all_to_all(total, "seq", split_axis=1, concat_axis=0, tiled=True),
    )
    mine = HQ // parts
    group = HQ // KVH
    got_out = got_out.reshape(parts, rows, mine, DH)
    got_top = got_top.reshape(parts, rows, mine)
    got_total = got_total.reshape(parts, rows, mine)
    head_ids = here * mine + jnp.arange(mine, dtype=jnp.int32)
    head_pick = ((head_ids // group)[:, None] == jnp.arange(KVH, dtype=jnp.int32)[None, :]).astype(
        jnp.bfloat16
    )
    tree = tree_all[0]
    tree_keys = tree[:, 0].reshape(rows, KVH, DH)
    tree_vals = tree[:, 1].reshape(rows, KVH, DH)
    my_keys = jnp.einsum(
        "nkd,ak->nad", tree_keys, head_pick, preferred_element_type=jnp.float32
    ).astype(jnp.bfloat16)
    my_vals = jnp.einsum(
        "nkd,ak->nad", tree_vals, head_pick, preferred_element_type=jnp.float32
    ).astype(jnp.bfloat16)
    my_query = lax.dynamic_slice_in_dim(query, here * mine * DH, mine * DH, 1).reshape(
        rows, mine, DH
    )
    tree_scores = jnp.einsum(
        "rad,nad->ran", my_query, my_keys, preferred_element_type=jnp.float32
    ) * DH ** (-0.5)
    linked = ancestry(tree_parents[0])[:, None, :]
    tree_top = jnp.max(jnp.where(linked, tree_scores, NEG), axis=-1)
    tree_weights = jnp.where(linked, jnp.exp(tree_scores - tree_top[..., None]), 0.0)
    tree_total = jnp.sum(tree_weights, axis=-1)
    tree_out = jnp.einsum(
        "ran,nad->rad",
        tree_weights.astype(jnp.bfloat16),
        my_vals,
        preferred_element_type=jnp.float32,
    )
    peak = jnp.maximum(jnp.max(got_top, axis=0), tree_top)
    factor = jnp.exp(got_top - peak[None])
    tree_factor = jnp.exp(tree_top - peak)
    numer = jnp.sum(factor[..., None] * got_out, axis=0) + tree_factor[..., None] * tree_out
    denom = jnp.sum(factor * got_total, axis=0) + tree_factor * tree_total
    attention = (numer / denom[..., None]).astype(jnp.bfloat16).reshape(rows, mine * DH)
    projected = jnp.dot(attention, out_weight, preferred_element_type=jnp.float32)
    summed = lax.psum(projected, "seq")
    attended_all = summed.astype(jnp.bfloat16)
    normed = normalize(resid_all[0], attended_all, norm_gain)
    attended = lax.dynamic_slice_in_dim(attended_all, here * own_rows, own_rows, 0)
    ids = expert_ids[0]
    gates = gate_weights[0]
    table = jnp.arange(EXPERTS, dtype=jnp.int32)
    hits = ids[:, :, None] == table[None, None, :]
    choose = jnp.sum(hits.astype(jnp.int32), axis=1)
    weight = jnp.sum(jnp.where(hits, gates[:, :, None], jnp.zeros((), jnp.bfloat16)), axis=1)
    slot = jnp.cumsum(choose, axis=0) - choose
    groups = lax.axis_size("req")
    held = w_gate.shape[0]
    target = jnp.arange(groups, dtype=jnp.int32)[:, None]
    local = jnp.arange(held, dtype=jnp.int32)[None, :]
    owner = ((target * parts + here) * held + local) // SPLIT
    owned = (owner[:, :, None] == table[None, None, :])[..., None]
    chosen = jnp.sum(jnp.where(owned, choose.T[None, None], 0), axis=2)
    seated = jnp.sum(jnp.where(owned, slot.T[None, None], 0), axis=2)
    rate = jnp.sum(jnp.where(owned, weight.T[None, None], jnp.zeros((), jnp.bfloat16)), axis=2)
    seats = jnp.arange(CAP, dtype=jnp.int32)
    select = (chosen[:, :, None, :] > 0) & (seated[:, :, None, :] == seats[None, None, :, None])
    select_b = select.astype(jnp.bfloat16)
    send_rows = jnp.einsum(
        "ghci,id->ghcd", select_b, normed, preferred_element_type=jnp.float32
    ).astype(jnp.bfloat16)
    send_rate = jnp.einsum(
        "ghci,ghi->ghc", select_b, rate, preferred_element_type=jnp.float32
    ).astype(jnp.bfloat16)
    got_rows = lax.all_to_all(send_rows, "req", split_axis=0, concat_axis=0, tiled=True)
    got_rate = lax.all_to_all(send_rate, "req", split_axis=0, concat_axis=0, tiled=True)
    gate = jnp.einsum("shcd,hdf->shcf", got_rows, w_gate, preferred_element_type=jnp.float32)
    up = jnp.einsum("shcd,hdf->shcf", got_rows, w_up, preferred_element_type=jnp.float32)
    hidden = (jax.nn.silu(gate) * up * got_rate[..., None].astype(jnp.float32)).astype(jnp.bfloat16)
    part = jnp.einsum("shcf,hfd->shcd", hidden, w_down, preferred_element_type=jnp.float32).astype(
        jnp.bfloat16
    )
    back = lax.all_to_all(part, "req", split_axis=0, concat_axis=0, tiled=True)
    mixed = jnp.einsum("ghci,ghcd->id", select_b, back, preferred_element_type=jnp.float32)
    expert_rows = lax.psum_scatter(
        mixed.astype(jnp.bfloat16), "seq", scatter_dimension=0, tiled=True
    )
    return (attended[None], expert_rows[None])


def solution(mesh):
    placed = (
        P("req", "seq", None),
        P("req", "seq", None, None),
        P("req", "seq", None, None),
        P("req"),
        P("req", None),
        P("req", "seq", None),
        P("seq", None),
        P(),
        P("req", None, None),
        P("req", None, None),
        P(("req", "seq"), None, None),
        P(("req", "seq"), None, None),
        P(("req", "seq"), None, None),
    )
    return jax.shard_map(
        body,
        mesh=mesh,
        in_specs=placed,
        out_specs=(P("req", "seq", None), P("req", "seq", None)),
        check_vma=False,
    )
```

profile of v0, /device:TPU:0, one launch (start us, length us, event | category | flops | bytes accessed | tf_op | source)
XLA Modules:
  0.0 987.3 jit_solution(15870105660192158869)
XLA Ops:
  8.7 1.3 copy.61
  10.7 1.2 fusion.57
  12.6 10.8 %all_gather.10 = bf16[1,128,2,256]{3,2,0,1:T(2,128)(2,1)S(1)} all-gather(bf16[1,16,2,256]{3,2,0,1:T(2,128)(2,1)} %bitcast.172), channel_id=1, replica_groups=mesh['req'=4,'seq'=8] {'seq'}, dimensions={1}, use_global_device_ids=true | all-gather | bytes 147456 | tf_op jit(solution)/shard_map/all_gather | solution.py:78
  23.6 0.7 convert_reduce_fusion
  24.8 1.0 select_reduce_fusion.1
  25.8 0.7 fusion.84
  26.6 9.7 all-gather.3.cloned.1.call-done
  36.2 1.6 copy.62
  37.9 2.1 fusion.10
  40.0 3.2 copy-done
  43.2 3.4 fusion.13
  46.6 3.3 all-to-all-start.2
  49.9 0.8 select_reduce_fusion.2
  51.1 3.5 all-to-all-done.2
  54.6 3.3 all-to-all-start
  58.0 6.6 fusion.16
  64.5 4.1 all-to-all-start.1
  69.0 0.7 reshape.164
  70.7 24.6 %all-to-all-done.1 = f32[128,8,512]{0,2,1:T(8,128)S(1)} async-done(((f32[128,8,512]{0,2,1:T(8,128)}), f32[128,8,512]{0,2,1:T(8,128)S(1)}, u32[]{:S(2)}, u32[]{:S(2)}) %all-to-all-start.1) | async-done | bytes 2097184 | tf_op jit(solution)/shard_map/all_to_all | solution.py:88
  95.3 4.6 all-to-all-start.4
  100.3 2.9 fusion.117
  103.2 55.6 %all-reduce.1 = bf16[128,4096]{1,0:T(8,128)(2,1)S(1)} all-reduce(f32[128,4096]{1,0:T(8,128)S(1)} %fusion.117), channel_id=1, replica_groups=mesh['req'=4,'seq'=8] {'seq'}, use_global_device_ids=true, to_apply=%region_7.8 | all-reduce | flops 524288 | bytes 3145728 | tf_op jit(solution)/shard_map/psum | solution.py:133
  158.8 1.5 fusion.22
  160.6 8.1 convolution_convert_fusion
  168.8 7.0 all-to-all-start.3
  175.9 361.5 %all-to-all-done.3 = bf16[4,16,32,4096]{3,2,1,0:T(8,128)(2,1)} async-done(((bf16[4,16,32,4096]{3,2,1,0:T(8,128)(2,1)}), bf16[4,16,32,4096]{3,2,1,0:T(8,128)(2,1)}, u32[]{:S(2)}, u32[]{:S(2)}) %all-to-all-start.3) | async-done | bytes 16777248 | tf_op jit(solution)/shard_map/all_to_all | solution.py:162
  537.4 12.9 %fusion.24 = f32[4,16,32,128]{3,2,0,1:T(8,128)S(1)} fusion(bf16[16,4096,128]{2,1,0:T(8,128)(2,1)} %param.23, bf16[4,16,32,4096]{3,2,1,0:T(8,128)(2,1)} %all-to-all-done.3), kind=kOutput, calls=%fused_computation.32 | convolution fusion | flops 2147483648 | bytes 34603008 | tf_op jit(solution)/shard_map/shcd,hdf->shcf/dot_general | solution.py:164
  550.3 12.9 %fusion.44 = bf16[4,16,32,128]{3,2,0,1:T(8,128)(2,1)S(1)} fusion(bf16[16,4096,128]{2,1,0:T(8,128)(2,1)} %param.24, bf16[4,16,32,4096]{3,2,1,0:T(8,128)(2,1)} %all-to-all-done.3, f32[4,16,32,128]{3,2,0,1:T(8,128)S(1)} %fusion.24, f32[4,16,32]{2,0,1:T(4,128)S(1)} %copy.82), kind=kOutput, calls=%fused_computation.36 | convolution fusion | flops 2149318656 | bytes 35135488 | tf_op jit(solution)/shard_map/shcd,hdf->shcf/dot_general | solution.py:165
  563.2 11.4 %convert_bitcast_fusion = bf16[4,16,32,4096]{3,2,1,0:T(8,128)(2,1)} fusion(bf16[16,128,4096]{2,1,0:T(8,128)(2,1)} %param.25, bf16[4,16,32,128]{3,2,0,1:T(8,128)(2,1)S(1)} %fusion.44), kind=kOutput, calls=%fused_computation.6 | convolution fusion | flops 2155872256 | bytes 34078720 | tf_op jit(solution)/shard_map/shcf,hfd->shcd/dot_general | solution.py:167
  574.7 367.6 %all_to_all.63 = bf16[4,16,32,4096]{3,2,1,0:T(8,128)(2,1)S(1)} all-to-all(bf16[4,16,32,4096]{3,2,1,0:T(8,128)(2,1)} %convert_bitcast_fusion), channel_id=1, replica_groups=mesh['req'=4,'seq'=8] {'req'}, dimensions={0} | all-to-all | bytes 33554432 | tf_op jit(solution)/shard_map/all_to_all | solution.py:170
  942.3 3.4 fusion.15
  946.4 34.4 %reduce-scatter.2.cloned.1.call-done = bf16[16,4096]{1,0:T(8,128)(2,1)} async-done(((bf16[128,4096]{1,0:T(8,128)(2,1)}), bf16[16,4096]{1,0:T(8,128)(2,1)}) %reduce-scatter.2.cloned.1.call-update) | async-done | bytes 131088 | tf_op jit(solution)/shard_map/reduce_scatter | solution.py:172
  (50 shorter events, 6.1 us)
Async XLA Ops:
  7.2 29.1 %all-gather.3.cloned.1.call-start = ((), (), s32[]{:S(2)}) async-start(), calls=%async_computation.7 | async-start | bytes 1179648 | tf_op jit(solution)/shard_map/all_gather | solution.py:77
  7.9 150.9 %all-gather.5.cloned.1.call-start = ((), (), s32[]{:S(2)}) async-start(), calls=%async_computation.8 | async-start | bytes 1179648 | tf_op jit(solution)/shard_map/all_gather | solution.py:79
  37.9 13.2 %copy-start.1 = (bf16[4096]{0:T(1024)(128)(2,1)S(1)}, bf16[4096]{0:T(1024)(128)(2,1)}, u32[]{:S(2)}) copy-start(bf16[4096]{0:T(1024)(128)(2,1)} %param.20) | copy-start | bytes 24580
  40.0 3.2 copy-start
  46.6 8.0 all-to-all-start.2
  54.6 9.9 %all-to-all-start = ((f32[128,8,4]{0,2,1:T(4,128)}), f32[128,8,4]{0,2,1:T(4,128)S(1)}, u32[]{:S(2)}, u32[]{:S(2)}) async-start(f32[128,8,4]{0,2,1:T(4,128)} %bitcast.6), calls=%async_computation | async-start | bytes 32768 | tf_op jit(solution)/shard_map/all_to_all | solution.py:89
  64.5 30.7 %all-to-all-start.1 = ((f32[128,8,512]{0,2,1:T(8,128)}), f32[128,8,512]{0,2,1:T(8,128)S(1)}, u32[]{:S(2)}, u32[]{:S(2)}) async-start(f32[128,8,512]{0,2,1:T(8,128)} %bitcast.159), calls=%async_computation.1 | async-start | bytes 4194304 | tf_op jit(solution)/shard_map/all_to_all | solution.py:88
  95.3 73.5 %all-to-all-start.4 = ((bf16[4,2,256]{2,1,0:T(2,128)(2,1)}), bf16[4,2,256]{2,1,0:T(2,128)(2,1)S(1)}, u32[]{:S(2)}, u32[]{:S(2)}) async-start(bf16[4,2,256]{2,1,0:T(2,128)(2,1)} %reshape.164), calls=%async_computation.4 | async-start | bytes 8192 | tf_op jit(solution)/shard_map/all_to_all | solution.py:163
  168.8 368.6 %all-to-all-start.3 = ((bf16[4,16,32,4096]{3,2,1,0:T(8,128)(2,1)}), bf16[4,16,32,4096]{3,2,1,0:T(8,128)(2,1)}, u32[]{:S(2)}, u32[]{:S(2)}) async-start(bf16[4,16,32,4096]{3,2,1,0:T(8,128)(2,1)} %convolution_convert_fusion), calls=%async_computation.3 | async-start | bytes 33554432 | tf_op jit(solution)/shard_map/all_to_all | solution.py:162
  175.7 805.1 %reduce-scatter.2.cloned.1.call-start = ((), (), s32[]{:S(2)}) async-start(), calls=%async_computation.9 | async-start | bytes 1179648 | tf_op jit(solution)/shard_map/reduce_scatter | solution.py:172
Sparse Core Ops, SparseCore 0:
  9.9 26.3 all-gather.2
  38.1 23.4 all-gather.4
  945.9 34.8 reduce-scatter.1
where the time goes:
time: 988 us; the launch traced here: 987 us
  waiting for transfers between devices  435 us (44%)
  blocking collectives  434 us (44%)
  matrix products  63.7 us (6%)
  starting transfers between devices  22.4 us (2%)
  between operations  14.7 us (1%)
    all_to_all x1, blocking collectives, body(): back = lax.all_to_all(part, 'req', split_axis=0, concat_axis=0, tiled=True)  368 us
    all_to_all x1, waiting for transfers between devices, body(): lax.all_to_all(send_rows, 'req', split_axis=0, concat_axis=0, tiled=True)  362 us
    psum x1, blocking collectives, body(): summed = lax.psum(projected, 'seq')  55.6 us
    reduce_scatter x1, waiting for transfers between devices, body(): lax.psum_scatter(mixed.astype(jnp.bfloat16), 'seq', scatter_dimension=0,...  34.4 us
    all_to_all x1, waiting for transfers between devices, body(): lax.all_to_all(out, 'seq', split_axis=1, concat_axis=0, tiled=True)  24.6 us
  transfers between devices with their start and end apart: 8, of which 5 were waited for; matrix products, arithmetic and copies ran while one was open for 4% of the time, Pallas kernels for 0%

commit v1 on v0

v1 whole, which is shorter than its diff:
```python
import functools

import jax
import jax.numpy as jnp
from jax import lax
from jax.experimental import pallas as pl
from jax.experimental.pallas import tpu as pltpu
from jax.sharding import PartitionSpec as P

DH = 128
HQ = 32
KVH = 2
EXPERTS = 64
CAP = 32
SPLIT = 8


NEG = -1e30
EPS = 1e-06
CHUNKS = 2
VMEM_LIMIT = 48 * 1024 * 1024


def hop(value, mask):
    count = lax.axis_size("seq")
    return lax.ppermute(value, "seq", [(i, i ^ mask) for i in range(count)])


def turn(value, step):
    count = lax.axis_size("req")
    return lax.ppermute(value, "req", [(i, (i + step) % count) for i in range(count)])


def block_order(parts):
    bits = parts.bit_length() - 1
    return [int(format(p, "b").zfill(bits)[::-1], 2) if bits else 0 for p in range(parts)]


def ancestry(parents):
    count = parents.shape[0]
    node = jnp.arange(count, dtype=jnp.int32)
    linked = (parents[:, None] == node[None, :]) | (node[:, None] == node[None, :])
    reach = linked.astype(jnp.bfloat16)
    hops = 1
    while hops < count:
        paths = jnp.dot(reach, reach, preferred_element_type=jnp.float32)
        reach = jnp.minimum(paths, 1.0).astype(jnp.bfloat16)
        hops = hops * 2
    return reach


def attend_kernel(parts, mine, valid_ref, q_ref, mask_ref, tree_ref, *refs):
    kv_refs = refs[:parts]
    w_ref, keep_ref, send_ref = refs[parts : parts + 3]
    rows = q_ref.shape[0]
    scale = DH ** (-0.5)
    q = jnp.concatenate([q_ref[:, a * DH : (a + 1) * DH] for a in range(mine)], axis=0)

    def scores(keys):
        return (
            lax.dot_general(q, keys, (((1,), (1,)), ((), ())), preferred_element_type=jnp.float32)
            * scale
        )

    linked = jnp.concatenate([mask_ref[...]] * mine, axis=0) > 0.5
    s = jnp.where(linked, scores(tree_ref[:, :DH]), NEG)
    top = jnp.max(s, axis=-1, keepdims=True)
    weights = jnp.exp(s - top)
    total = jnp.sum(weights, axis=-1, keepdims=True)
    out = jnp.dot(
        weights.astype(jnp.bfloat16), tree_ref[:, DH:], preferred_element_type=jnp.float32
    )
    for part in range(parts):
        kv = kv_refs[part]
        s = scores(kv[:, :DH])
        place = lax.broadcasted_iota(jnp.int32, s.shape, 1)
        s = jnp.where(place < valid_ref[part], s, NEG)
        peak = jnp.maximum(top, jnp.max(s, axis=-1, keepdims=True))
        weights = jnp.exp(s - peak)
        fade = jnp.exp(top - peak)
        total = total * fade + jnp.sum(weights, axis=-1, keepdims=True)
        out = out * fade + jnp.dot(
            weights.astype(jnp.bfloat16), kv[:, DH:], preferred_element_type=jnp.float32
        )
        top = peak
    attention = (out / total).astype(jnp.bfloat16)
    attention = jnp.concatenate(
        [attention[a * rows : (a + 1) * rows] for a in range(mine)], axis=1
    )
    half = rows // 2
    width = w_ref.shape[1]
    tile = min(width, 1024)
    for first in range(0, width, tile):
        piece = jnp.dot(
            attention, w_ref[:, first : first + tile], preferred_element_type=jnp.float32
        ).astype(jnp.bfloat16)
        keep_ref[:, first : first + tile] = piece[:half]
        send_ref[:, first : first + tile] = piece[half:]


def attend(valid, q, mask, tree, blocks, w):
    parts = len(blocks)
    rows, mine = q.shape[0], q.shape[1] // DH
    span = blocks[0].shape[0]
    full = pl.BlockSpec(memory_space=pltpu.VMEM)
    out = jax.ShapeDtypeStruct((rows // 2, w.shape[1]), jnp.bfloat16)
    reach = rows + parts * span
    return pl.pallas_call(
        functools.partial(attend_kernel, parts, mine),
        out_shape=(out, out),
        in_specs=[pl.BlockSpec(memory_space=pltpu.SMEM)] + [full] * (parts + 4),
        out_specs=(full, full),
        compiler_params=pltpu.CompilerParams(vmem_limit_bytes=VMEM_LIMIT),
        cost_estimate=pl.CostEstimate(
            flops=4 * rows * mine * DH * reach + 2 * rows * mine * DH * w.shape[1],
            bytes_accessed=2 * w.size + 4 * DH * reach + 2 * rows * w.shape[1],
            transcendentals=rows * mine * reach,
        ),
    )(valid, q, mask, tree, *blocks, w)


def rise_kernel(per_step, per_expert, started, sel_ref, rows_ref, wg_ref, wu_ref, *refs):
    if started:
        gate_in, up_in, gate_ref, up_ref, picked = refs
    else:
        gate_ref, up_ref, picked = refs
    step = pl.program_id(0)

    @pl.when(step == 0)
    def _():
        for e in range(picked.shape[0]):
            picked[e] = jnp.dot(
                sel_ref[e], rows_ref[...], preferred_element_type=jnp.float32
            ).astype(jnp.bfloat16)

    x = picked[(step * per_step) // per_expert]
    for k in range(per_step):
        w = jnp.concatenate([wg_ref[k], wu_ref[k]], axis=1)
        both = jnp.dot(x, w, preferred_element_type=jnp.float32)
        wide = wg_ref.shape[2]
        gate, up = both[:, :wide], both[:, wide:]
        if started:
            gate, up = gate + gate_in[k], up + up_in[k]
        gate_ref[k] = gate
        up_ref[k] = up


def rise(sel, rows, w_gate, w_up, chunk, before):
    held, depth, wide = w_gate.shape
    experts, seats, count = sel.shape
    per_expert = held // experts
    per_step = min(per_expert, 4)
    cut = rows.shape[1]
    weight = pl.BlockSpec((per_step, cut, wide), lambda j: (j, chunk, 0))
    total = pl.BlockSpec((per_step, seats, wide), lambda j: (j, 0, 0))
    shape = jax.ShapeDtypeStruct((held, seats, wide), jnp.float32)
    extra = [] if before is None else [total, total]
    return pl.pallas_call(
        functools.partial(rise_kernel, per_step, per_expert, before is not None),
        grid=(held // per_step,),
        out_shape=(shape, shape),
        in_specs=[
            pl.BlockSpec(sel.shape, lambda j: (0, 0, 0)),
            pl.BlockSpec(rows.shape, lambda j: (0, 0)),
            weight,
            weight,
        ]
        + extra,
        out_specs=(total, total),
        scratch_shapes=[pltpu.VMEM((experts, seats, cut), jnp.bfloat16)],
        compiler_params=pltpu.CompilerParams(vmem_limit_bytes=VMEM_LIMIT),
        cost_estimate=pl.CostEstimate(
            flops=4 * held * seats * cut * wide + 2 * experts * seats * count * cut,
            bytes_accessed=4 * held * cut * wide + 2 * count * cut,
            transcendentals=0,
        ),
    )(sel, rows, w_gate, w_up, *(() if before is None else before))


def fall_kernel(
    per_step, per_expert, gate_ref, up_ref, rate_ref, wd_ref, back_ref, keep_ref, send_ref, total
):
    step = pl.program_id(0)
    e = (step * per_step) // per_expert
    rate = rate_ref[e]
    acc = None
    for k in range(per_step):
        gate = gate_ref[k]
        hidden = (gate / (1.0 + jnp.exp(-gate)) * up_ref[k] * rate).astype(jnp.bfloat16)
        term = jnp.dot(hidden, wd_ref[k], preferred_element_type=jnp.float32)
        acc = term if acc is None else acc + term
    first = (step * per_step) % per_expert == 0

    @pl.when(first)
    def _():
        total[e] = acc

    @pl.when(jnp.logical_not(first))
    def _():
        total[e] += acc

    @pl.when(step == pl.num_programs(0) - 1)
    def _():
        experts, seats, cut = total.shape
        half = keep_ref.shape[0]
        flat = total[...].astype(jnp.bfloat16).reshape(experts * seats, cut)
        keep_ref[...] = jnp.dot(
            back_ref[:half], flat, preferred_element_type=jnp.float32
        ).astype(jnp.bfloat16)
        send_ref[...] = jnp.dot(
            back_ref[half:], flat, preferred_element_type=jnp.float32
        ).astype(jnp.bfloat16)


def fall(gate, up, rate, w_down, back, chunk, cut):
    held, wide, depth = w_down.shape
    experts, seats, _ = rate.shape
    count = back.shape[0]
    per_expert = held // experts
    per_step = min(per_expert, 4)
    shape = jax.ShapeDtypeStruct((count // 2, cut), jnp.bfloat16)
    whole = pl.BlockSpec((count // 2, cut), lambda j: (0, 0))
    total = pl.BlockSpec((per_step, seats, wide), lambda j: (j, 0, 0))
    return pl.pallas_call(
        functools.partial(fall_kernel, per_step, per_expert),
        grid=(held // per_step,),
        out_shape=(shape, shape),
        in_specs=[
            total,
            total,
            pl.BlockSpec(rate.shape, lambda j: (0, 0, 0)),
            pl.BlockSpec((per_step, wide, cut), lambda j: (j, 0, chunk)),
            pl.BlockSpec(back.shape, lambda j: (0, 0)),
        ],
        out_specs=(whole, whole),
        scratch_shapes=[pltpu.VMEM((experts, seats, cut), jnp.float32)],
        compiler_params=pltpu.CompilerParams(vmem_limit_bytes=VMEM_LIMIT),
        cost_estimate=pl.CostEstimate(
            flops=2 * held * seats * cut * wide + 2 * experts * seats * count * cut,
            bytes_accessed=2 * held * cut * wide + 4 * count * cut,
            transcendentals=held * seats * wide,
        ),
    )(gate, up, rate, w_down, back)


def body(
    queries,
    kv_cache,
    tree_kv,
    context_lengths,
    tree_parents,
    resid,
    out_weight,
    norm_gain,
    expert_ids,
    gate_weights,
    w_gate,
    w_up,
    w_down,
):
    here = lax.axis_index("seq")
    there = lax.axis_index("req")
    parts = lax.axis_size("seq")
    groups = lax.axis_size("req")
    bits = parts.bit_length() - 1
    order = block_order(parts)
    near = order[: parts // 2]
    own = queries.shape[1]
    rows = own * parts
    depth = resid.shape[2]

    table = jnp.concatenate(
        [expert_ids[0].astype(jnp.bfloat16), gate_weights[0]], axis=1
    )
    tables = [table] + [turn(table, d) for d in range(1, groups)]

    span = kv_cache.shape[1]
    share = parts // KVH
    lane = kv_cache[0]
    heads = [
        lane[:, :, h * DH : (h + 1) * DH].reshape(span, 2 * DH) for h in range(KVH)
    ]

    def head_of(device):
        pick = heads[0]
        for h in range(1, KVH):
            pick = jnp.where(device // share == h, heads[h], pick)
        return pick

    half = [head_of(here ^ mask) if mask == 0 else None for mask in near]
    same = half[0]
    other = head_of(here ^ (parts // 2))
    half = [same] + [hop(other if mask & (parts // 2) else same, mask) for mask in near[1:]]
    blocks = half + [hop(piece, 1) for piece in half]
    valid = context_lengths[0] - jnp.stack([(here ^ mask) * span for mask in order])

    q = queries[0]
    tree_heads = [
        tree_kv[0][:, :, h * DH : (h + 1) * DH].reshape(own, 2 * DH) for h in range(KVH)
    ]
    top_bit = (here >> (bits - 1)) & 1
    tree = jnp.where(top_bit == 1, tree_heads[1], tree_heads[0])
    tree_send = jnp.where(top_bit == 1, tree_heads[0], tree_heads[1])
    for bit in range(bits - 1, -1, -1):
        wide = q.shape[1] // 2
        upper = ((here >> bit) & 1) == 1
        low, high = q[:, :wide], q[:, wide:]
        kept = jnp.where(upper, high, low)
        packed = jnp.concatenate([jnp.where(upper, low, high), tree_send], axis=1)
        got = hop(packed, 1 << bit)
        q = jnp.concatenate([kept, got[:, :wide]], axis=0)
        tree = jnp.concatenate([tree, got[:, wide:]], axis=0)
        tree_send = tree

    wanted = jnp.stack([here ^ mask for mask in order])
    swap = wanted[:, None] == jnp.arange(parts, dtype=jnp.int32)[None, :]

    def placed(values):
        cut = values.reshape((parts, own) + values.shape[1:])
        tail = (1,) * (cut.ndim - 1)
        moved = jnp.sum(
            jnp.where(swap.reshape((parts, parts) + tail), cut[None].astype(jnp.float32), 0.0), axis=1
        )
        return moved.reshape((parts, own) + values.shape[1:])

    reach = ancestry(tree_parents[0])
    across = placed(reach).reshape(rows, rows).T
    linked = placed(across).reshape(rows, rows).T.astype(jnp.bfloat16)

    keep, send = attend(valid.astype(jnp.int32), q, linked, tree, blocks, out_weight)

    got = hop(send, 1)
    pair = [
        keep[i * own : (i + 1) * own].astype(jnp.float32)
        + got[i * own : (i + 1) * own].astype(jnp.float32)
        for i in range(len(near))
    ]
    terms = [pair[0]] + [
        hop(pair[i].astype(jnp.bfloat16), near[i]).astype(jnp.float32)
        for i in range(1, len(near))
    ]
    attended = sum(terms[1:], terms[0]).astype(jnp.bfloat16)
    mid = (resid[0].astype(jnp.float32) + attended.astype(jnp.float32)).astype(jnp.bfloat16)
    midf = lax.optimization_barrier(mid).astype(jnp.float32)
    factor = lax.rsqrt(jnp.mean(midf * midf, axis=-1, keepdims=True) + EPS)
    normed = (midf * factor * norm_gain.astype(jnp.float32)).astype(jnp.bfloat16)

    held = w_gate.shape[0]
    experts = max(1, held // SPLIT)
    first = ((there * parts + here) * held) // SPLIT
    count = groups * rows
    seats = groups * CAP
    listing = jnp.stack([placed(t) for t in tables], axis=1).reshape(count, -1)
    topk = listing.shape[1] // 2
    mine = (first + jnp.arange(experts, dtype=jnp.int32)).astype(jnp.float32)
    hits = listing[None, :, :topk] == mine[:, None, None]
    chosen = jnp.sum(hits.astype(jnp.float32), axis=2)
    weight = jnp.sum(jnp.where(hits, listing[None, :, topk:], 0.0), axis=2)
    index = jnp.arange(count, dtype=jnp.int32)
    before = (index[:, None] < index[None, :]).astype(jnp.bfloat16)
    seat = jnp.dot(chosen.astype(jnp.bfloat16), before, preferred_element_type=jnp.float32)
    seat = jnp.where(chosen > 0.5, seat.astype(jnp.int32), -1)
    select = seat[:, None, :] == jnp.arange(seats, dtype=jnp.int32)[None, :, None]
    sel = select.astype(jnp.bfloat16)
    rate = jnp.sum(jnp.where(select, weight[:, None, :], 0.0), axis=2)[..., None]
    back = sel.reshape(experts * seats, count).T

    cut = depth // CHUNKS
    sums = None
    for chunk in range(CHUNKS):
        piece = normed[:, chunk * cut : (chunk + 1) * cut]
        stack = jnp.concatenate([piece] + [turn(piece, d) for d in range(1, groups)], axis=0)
        plane = [stack] + [hop(stack, mask) for mask in near[1:]]
        full = jnp.concatenate(plane + [hop(p, 1) for p in plane], axis=0)
        sums = rise(sel, full, w_gate, w_up, chunk, sums)

    pieces = []
    for chunk in range(CHUNKS):
        keep, send = fall(sums[0], sums[1], rate, w_down, back, chunk, cut)
        got = hop(send, 1)
        size = groups * own
        pair = [
            keep[i * size : (i + 1) * size].astype(jnp.float32)
            + got[i * size : (i + 1) * size].astype(jnp.float32)
            for i in range(len(near))
        ]
        terms = [pair[0]] + [
            hop(pair[i].astype(jnp.bfloat16), near[i]).astype(jnp.float32)
            for i in range(1, len(near))
        ]
        flat = sum(terms[1:], terms[0])
        result = flat[:own]
        for d in range(1, groups):
            result = result + turn(
                flat[d * own : (d + 1) * own].astype(jnp.bfloat16), -d
            ).astype(jnp.float32)
        pieces.append(result.astype(jnp.bfloat16))
    return (attended[None], jnp.concatenate(pieces, axis=1)[None])


def solution(mesh):
    placed = (
        P("req", "seq", None),
        P("req", "seq", None, None),
        P("req", "seq", None, None),
        P("req"),
        P("req", None),
        P("req", "seq", None),
        P("seq", None),
        P(),
        P("req", None, None),
        P("req", None, None),
        P(("req", "seq"), None, None),
        P(("req", "seq"), None, None),
        P(("req", "seq"), None, None),
    )
    return jax.shard_map(
        body,
        mesh=mesh,
        in_specs=placed,
        out_specs=(P("req", "seq", None), P("req", "seq", None)),
        check_vma=False,
    )
```

time: 988 us -> 161 us (0.16)
  blocking collectives: 434 us -> 0 us
  waiting for transfers between devices: 435 us -> 43.4 us
  matrix products: 63.7 us -> 2.03 us
  Pallas kernels: 0 us -> 36.8 us
  starting transfers between devices: 22.4 us -> 57.3 us
  between operations: 14.7 us -> 1.93 us
    all_to_all x5 -> x0, waiting for transfers between devices: 390 us -> none  [the longest x1 362 us: body(): lax.all_to_all(send_rows, 'req', split_axis=0, concat_axis=0, tiled=True)]
    all_to_all x1 -> x0, blocking collectives: 368 us -> none  [body(): back = lax.all_to_all(part, 'req', split_axis=0, concat_axis=0, tiled=True)]
    dot_general x13 -> x1, matrix products: 61.8 us -> 0.18 us  [body(): jnp.dot(chosen.astype(jnp.bfloat16), before, preferred_element_type=jnp.f...]
    ppermute x0 -> x51, starting transfers between devices: none -> 57.3 us  [the longest x36 31.4 us: hop(): return lax.ppermute(value, 'seq', [(i, i ^ mask) for i in range(count)])]
    psum x1 -> x0, blocking collectives: 55.6 us -> none  [body(): summed = lax.psum(projected, 'seq')]
    ppermute x0 -> x51, waiting for transfers between devices: none -> 43.4 us  [the longest x36 35.7 us: hop(): return lax.ppermute(value, 'seq', [(i, i ^ mask) for i in range(count)])]
    pallas_call x0 -> x5, Pallas kernels: none -> 36.8 us  [the longest x2 16.8 us: rise(): pl.pallas_call(functools.partial(rise_kernel, per_step, per_expert, befor...]
    reduce_scatter x1 -> x0, waiting for transfers between devices: 34.4 us -> none  [body(): lax.psum_scatter(mixed.astype(jnp.bfloat16), 'seq', scatter_dimension=0,...]
  transfers between devices with their start and end apart: 8 -> 51, of which waited for: 5 -> 22; matrix products, arithmetic and copies ran while one was open for 4% -> 10% of each run, Pallas kernels for 0% -> 9%
where the time goes in v1:
time: 161 us
  starting transfers between devices  57.3 us (36%)
  waiting for transfers between devices  43.4 us (27%)
  Pallas kernels  36.8 us (23%)
  local copies, waits for them, and re-layouts  10.4 us (6%)
  other arithmetic  9.04 us (6%)
  matrix products  2.03 us (1%)
  between operations  1.93 us (1%)
    ppermute x36, waiting for transfers between devices, hop(): return lax.ppermute(value, 'seq', [(i, i ^ mask) for i in range(count)])  35.7 us
    ppermute x36, starting transfers between devices, hop(): return lax.ppermute(value, 'seq', [(i, i ^ mask) for i in range(count)])  31.4 us
    ppermute x15, starting transfers between devices, turn(): lax.ppermute(value, 'req', [(i, (i + step) % count) for i in range(count)])  25.9 us
    pallas_call x2, Pallas kernels, rise(): pl.pallas_call(functools.partial(rise_kernel, per_step, per_expert, befor...  16.8 us
    pallas_call x2, Pallas kernels, fall(): pl.pallas_call(functools.partial(fall_kernel, per_step, per_expert), grid...  13.2 us
    ppermute x15, waiting for transfers between devices, turn(): lax.ppermute(value, 'req', [(i, (i + step) % count) for i in range(count)])  7.71 us
    pallas_call x1, Pallas kernels, attend(): pl.pallas_call(functools.partial(attend_kernel, parts, mine), out_shape=(...  6.85 us
    unnamed x26, local copies, waits for them, and re-layouts  6.46 us
  transfers between devices with their start and end apart: 51, of which 22 were waited for; matrix products, arithmetic and copies ran while one was open for 10% of the time, Pallas kernels for 9%

profile of v1, /device:TPU:0, one launch (start us, length us, event | category | flops | bytes accessed | tf_op | source)
XLA Modules:
  0.0 160.9 jit_solution(1419272654138642710)
XLA Ops:
  2.2 3.0 %collective-permute-start.3 = (bf16[512,256]{1,0:T(8,128)(2,1)S(1)}, bf16[512,256]{1,0:T(8,128)(2,1)S(1)}, u32[]{:S(2)}, u32[]{:S(2)}) collective-permute-start(bf16[512,256]{1,0:T(8,128)(2,1)S(1)} %bitcast.89), channel_id=1, source_target_pairs={{0,4},{1,5},{2,6},{3,7},{4,0},{5,1},{6,2},{7,3},{8,12},{9,13},{10,... | collective-permute-start | bytes 786440 | tf_op jit(solution)/shard_map/ppermute | solution.py:26
  8.0 1.6 collective-permute-start.14
  9.6 2.6 %collective-permute-start.15 = (bf16[128,16]{0,1:T(8,128)(2,1)S(1)}, bf16[128,16]{0,1:T(8,128)(2,1)S(1)}, u32[]{:S(2)}, u32[]{:S(2)}) collective-permute-start(bf16[128,16]{0,1:T(8,128)(2,1)S(1)} %pad_maximum_fusion.8), channel_id=1, source_target_pairs={{0,16},{8,24},{16,0},{24,8},{1,17},{9,25},{17,1},{25,9},{2,18},{10... | collective-permute-start | bytes 12296 | tf_op jit(solution)/shard_map/ppermute | solution.py:31
  21.2 1.6 collective-permute-start
  23.2 2.7 %collective-permute-done = bf16[16,2304]{1,0:T(8,128)(2,1)S(1)} collective-permute-done((bf16[16,2304]{1,0:T(8,128)(2,1)S(1)}, bf16[16,2304]{1,0:T(8,128)(2,1)S(1)}, u32[]{:S(2)}, u32[]{:S(2)}) %collective-permute-start) | collective-permute-done | bytes 73760 | tf_op jit(solution)/shard_map/ppermute | solution.py:26
  26.0 1.6 collective-permute-start.1
  28.1 2.4 %collective-permute-done.1 = bf16[32,1280]{1,0:T(8,128)(2,1)S(1)} collective-permute-done((bf16[32,1280]{1,0:T(8,128)(2,1)S(1)}, bf16[32,1280]{1,0:T(8,128)(2,1)S(1)}, u32[]{:S(2)}, u32[]{:S(2)}) %collective-permute-start.1) | collective-permute-done | bytes 81952 | tf_op jit(solution)/shard_map/ppermute | solution.py:26
  33.1 6.8 %shard_map.140 = (bf16[64,4096]{1,0:T(8,128)(2,1)S(1)}, bf16[64,4096]{1,0:T(8,128)(2,1)S(1)}) custom-call(s32[8]{0:T(128)S(1)} %broadcast_subtract_fusion.valid_ref, bf16[128,512]{1,0:T(8,128)(2,1)S(1)} %pad_maximum_fusion.3.q_ref, bf16[128,128]{1,0:T(8,128)(2,1)S(1)} %bitcast.84, bf16[128,256]{1,0:T(8,128)(2,1)S(1)} %pad_maximum_fusion.7.tree_ref, ...), custom_call_target="tpu_custom_call" | custom-call | flops 1644167168 | bytes 7405568 | tf_op jit(solution)/shard_map/pallas_call | solution.py:108
  42.0 1.6 collective-permute-start.11
  45.6 2.2 %collective-permute-done.11 = bf16[16,4096]{1,0:T(8,128)(2,1)S(1)} collective-permute-done((bf16[16,4096]{1,0:T(8,128)(2,1)S(1)}, bf16[16,4096]{1,0:T(8,128)(2,1)S(1)}, u32[]{:S(2)}, u32[]{:S(2)}) %collective-permute-start.11) | collective-permute-done | bytes 131104 | tf_op jit(solution)/shard_map/ppermute | solution.py:26
  47.8 2.1 %collective-permute-done.12 = bf16[16,4096]{1,0:T(8,128)(2,1)S(1)} collective-permute-done((bf16[16,4096]{1,0:T(8,128)(2,1)S(1)}, bf16[16,4096]{1,0:T(8,128)(2,1)S(1)}, u32[]{:S(2)}, u32[]{:S(2)}) %collective-permute-start.12) | collective-permute-done | bytes 131104 | tf_op jit(solution)/shard_map/ppermute | solution.py:26
  49.9 1.9 %collective-permute-done.13 = bf16[16,4096]{1,0:T(8,128)(2,1)S(1)} collective-permute-done((bf16[16,4096]{1,0:T(8,128)(2,1)S(1)}, bf16[16,4096]{1,0:T(8,128)(2,1)S(1)}, u32[]{:S(2)}, u32[]{:S(2)}) %collective-permute-start.13) | collective-permute-done | bytes 131104 | tf_op jit(solution)/shard_map/ppermute | solution.py:26
  54.5 2.8 %collective-permute-start.29 = (bf16[16,2048]{1,0:T(8,128)(2,1)S(1)}, bf16[16,2048]{1,0:T(8,128)(2,1)S(1)}, u32[]{:S(2)}, u32[]{:S(2)}) collective-permute-start(bf16[16,2048]{1,0:T(8,128)(2,1)S(1)} %get-tuple-element.51), channel_id=1, source_target_pairs={{0,24},{8,0},{16,8},{24,16},{1,25},{9,1},{17,9},{25,17},{2,26},{10... | collective-permute-start | bytes 196616 | tf_op jit(solution)/shard_map/ppermute | solution.py:31
  58.2 1.5 collective-permute-start.18
  60.2 2.4 %collective-permute-start.19 = (bf16[16,2048]{1,0:T(8,128)(2,1)S(1)}, bf16[16,2048]{1,0:T(8,128)(2,1)S(1)}, u32[]{:S(2)}, u32[]{:S(2)}) collective-permute-start(bf16[16,2048]{1,0:T(8,128)(2,1)S(1)} %get-tuple-element.54), channel_id=1, source_target_pairs={{0,24},{8,0},{16,8},{24,16},{1,25},{9,1},{17,9},{25,17},{2,26},{10... | collective-permute-start | bytes 196616 | tf_op jit(solution)/shard_map/ppermute | solution.py:31
  70.6 5.4 %collective-permute-done.30 = bf16[64,2048]{1,0:T(8,128)(2,1)S(1)} collective-permute-done((bf16[64,2048]{1,0:T(8,128)(2,1)S(1)}, bf16[64,2048]{1,0:T(8,128)(2,1)S(1)}, u32[]{:S(2)}, u32[]{:S(2)}) %collective-permute-start.30) | collective-permute-done | bytes 262176 | tf_op jit(solution)/shard_map/ppermute | solution.py:26
  76.9 1.6 collective-permute-start.22
  79.2 4.5 %collective-permute-done.20 = bf16[64,2048]{1,0:T(8,128)(2,1)S(1)} collective-permute-done((bf16[64,2048]{1,0:T(8,128)(2,1)S(1)}, bf16[64,2048]{1,0:T(8,128)(2,1)S(1)}, u32[]{:S(2)}, u32[]{:S(2)}) %collective-permute-start.20) | collective-permute-done | bytes 262176 | tf_op jit(solution)/shard_map/ppermute | solution.py:26
  90.4 8.1 %shard_map.141 = (f32[16,128,128]{2,1,0:T(8,128)S(1)}, f32[16,128,128]{2,1,0:T(8,128)S(1)}) custom-call(bf16[2,128,512]{2,1,0:T(8,128)(2,1)S(1)} %fusion.8.sel_ref, bf16[512,2048]{1,0:T(8,128)(2,1)S(1)} %constant_dynamic-update-slice_fusion.11.rows_ref, bf16[16,4096,128]{2,1,0:T(8,128)(2,1)} %wg_ref.3, bf16[16,4096,128]{2,1,0:T(8,128)(2,1)} %wu_ref.3), custom_call_target="tpu_custom_call" | custom-call | flops 2684354560 | bytes 18874368 | tf_op jit(solution)/shard_map/pallas_call | solution.py:158
  99.2 8.7 %shard_map.142 = (f32[16,128,128]{2,1,0:T(8,128)S(1)}, f32[16,128,128]{2,1,0:T(8,128)S(1)}) custom-call(bf16[2,128,512]{2,1,0:T(8,128)(2,1)S(1)} %fusion.8.sel_ref, bf16[512,2048]{1,0:T(8,128)(2,1)} %constant_dynamic-update-slice_fusion.rows_ref, bf16[16,4096,128]{2,1,0:T(8,128)(2,1)} %wg_ref.3, bf16[16,4096,128]{2,1,0:T(8,128)(2,1)} %wu_ref.3, ...), custom_call_target="tpu_custom_call" | custom-call | flops 2684354560 | bytes 18874368 | tf_op jit(solution)/shard_map/pallas_call | solution.py:158
  107.9 6.6 %shard_map.143 = (bf16[256,2048]{1,0:T(8,128)(2,1)S(1)}, bf16[256,2048]{1,0:T(8,128)(2,1)S(1)}) custom-call(f32[16,128,128]{2,1,0:T(8,128)S(1)} %get-tuple-element.16.gate_ref, f32[16,128,128]{2,1,0:T(8,128)S(1)} %get-tuple-element.17.up_ref, f32[2,128,1]{2,1,0:T(8,128)S(1)} %copy.50.rate_ref, bf16[16,128,4096]{2,1,0:T(8,128)(2,1)} %wd_ref.3, ...), custom_call_target="tpu_custom_call" | custom-call | flops 1610612736 | bytes 12582912 | tf_op jit(solution)/shard_map/pallas_call | solution.py:224
  115.1 6.6 %shard_map.144 = (bf16[256,2048]{1,0:T(8,128)(2,1)S(1)}, bf16[256,2048]{1,0:T(8,128)(2,1)S(1)}) custom-call(f32[16,128,128]{2,1,0:T(8,128)S(1)} %get-tuple-element.16.gate_ref, f32[16,128,128]{2,1,0:T(8,128)S(1)} %get-tuple-element.17.up_ref, f32[2,128,1]{2,1,0:T(8,128)S(1)} %copy.50.rate_ref, bf16[16,128,4096]{2,1,0:T(8,128)(2,1)} %wd_ref.3, ...), custom_call_target="tpu_custom_call" | custom-call | flops 1610612736 | bytes 12582912 | tf_op jit(solution)/shard_map/pallas_call | solution.py:224
  128.7 2.6 %collective-permute-done.38 = bf16[64,2048]{1,0:T(8,128)(2,1)S(1)} collective-permute-done((bf16[64,2048]{1,0:T(8,128)(2,1)S(1)}, bf16[64,2048]{1,0:T(8,128)(2,1)S(1)}, u32[]{:S(2)}, u32[]{:S(2)}) %collective-permute-start.38) | collective-permute-done | bytes 262176 | tf_op jit(solution)/shard_map/ppermute | solution.py:26
  131.2 2.1 %collective-permute-start.47 = (bf16[64,2048]{1,0:T(8,128)(2,1)S(1)}, bf16[64,2048]{1,0:T(8,128)(2,1)S(1)}, u32[]{:S(2)}, u32[]{:S(2)}) collective-permute-start(bf16[64,2048]{1,0:T(8,128)(2,1)S(1)} %get-tuple-element.38), channel_id=1, source_target_pairs={{0,6},{1,7},{2,4},{3,5},{4,2},{5,3},{6,0},{7,1},{8,14},{9,15},{10,... | collective-permute-start | bytes 786440 | tf_op jit(solution)/shard_map/ppermute | solution.py:26
  133.4 5.0 %collective-permute-done.40 = bf16[64,2048]{1,0:T(8,128)(2,1)S(1)} collective-permute-done((bf16[64,2048]{1,0:T(8,128)(2,1)S(1)}, bf16[64,2048]{1,0:T(8,128)(2,1)S(1)}, u32[]{:S(2)}, u32[]{:S(2)}) %collective-permute-start.40) | collective-permute-done | bytes 262176 | tf_op jit(solution)/shard_map/ppermute | solution.py:26
  138.6 2.1 %collective-permute-start.41 = (bf16[16,2048]{1,0:T(8,128)(2,1)S(1)}, bf16[16,2048]{1,0:T(8,128)(2,1)S(1)}, u32[]{:S(2)}, u32[]{:S(2)}) collective-permute-start(bf16[16,2048]{1,0:T(8,128)(2,1)S(1)} %get-tuple-element.45), channel_id=1, source_target_pairs={{0,24},{8,0},{16,8},{24,16},{1,25},{9,1},{17,9},{25,17},{2,26},{10... | collective-permute-start | bytes 196616 | tf_op jit(solution)/shard_map/ppermute | solution.py:31
  140.8 2.9 %collective-permute-start.42 = (bf16[16,2048]{1,0:T(8,128)(2,1)S(1)}, bf16[16,2048]{1,0:T(8,128)(2,1)S(1)}, u32[]{:S(2)}, u32[]{:S(2)}) collective-permute-start(bf16[16,2048]{1,0:T(8,128)(2,1)S(1)} %get-tuple-element.47), channel_id=1, source_target_pairs={{0,16},{8,24},{16,0},{24,8},{1,17},{9,25},{17,1},{25,9},{2,18},{10... | collective-permute-start | bytes 196616 | tf_op jit(solution)/shard_map/ppermute | solution.py:31
  143.7 1.9 %collective-permute-start.43 = (bf16[16,2048]{1,0:T(8,128)(2,1)S(1)}, bf16[16,2048]{1,0:T(8,128)(2,1)S(1)}, u32[]{:S(2)}, u32[]{:S(2)}) collective-permute-start(bf16[16,2048]{1,0:T(8,128)(2,1)S(1)} %get-tuple-element.46), channel_id=1, source_target_pairs={{0,8},{8,16},{16,24},{24,0},{1,9},{9,17},{17,25},{25,1},{2,10},{10... | collective-permute-start | bytes 196616 | tf_op jit(solution)/shard_map/ppermute | solution.py:31
  145.6 3.3 %collective-permute-done.47 = bf16[64,2048]{1,0:T(8,128)(2,1)S(1)} collective-permute-done((bf16[64,2048]{1,0:T(8,128)(2,1)S(1)}, bf16[64,2048]{1,0:T(8,128)(2,1)S(1)}, u32[]{:S(2)}, u32[]{:S(2)}) %collective-permute-start.47) | collective-permute-done | bytes 262176 | tf_op jit(solution)/shard_map/ppermute | solution.py:26
  149.1 2.1 %collective-permute-start.48 = (bf16[16,2048]{1,0:T(8,128)(2,1)S(1)}, bf16[16,2048]{1,0:T(8,128)(2,1)S(1)}, u32[]{:S(2)}, u32[]{:S(2)}) collective-permute-start(bf16[16,2048]{1,0:T(8,128)(2,1)S(1)} %get-tuple-element.48), channel_id=1, source_target_pairs={{0,24},{8,0},{16,8},{24,16},{1,25},{9,1},{17,9},{25,17},{2,26},{10... | collective-permute-start | bytes 196616 | tf_op jit(solution)/shard_map/ppermute | solution.py:31
  151.3 2.9 %collective-permute-start.49 = (bf16[16,2048]{1,0:T(8,128)(2,1)S(1)}, bf16[16,2048]{1,0:T(8,128)(2,1)S(1)}, u32[]{:S(2)}, u32[]{:S(2)}) collective-permute-start(bf16[16,2048]{1,0:T(8,128)(2,1)S(1)} %get-tuple-element.50), channel_id=1, source_target_pairs={{0,16},{8,24},{16,0},{24,8},{1,17},{9,25},{17,1},{25,9},{2,18},{10... | collective-permute-start | bytes 196616 | tf_op jit(solution)/shard_map/ppermute | solution.py:31
  155.3 3.7 %collective-permute-done.49 = bf16[16,2048]{1,0:T(8,128)(2,1)S(1)} collective-permute-done((bf16[16,2048]{1,0:T(8,128)(2,1)S(1)}, bf16[16,2048]{1,0:T(8,128)(2,1)S(1)}, u32[]{:S(2)}, u32[]{:S(2)}) %collective-permute-start.49) | collective-permute-done | bytes 65568 | tf_op jit(solution)/shard_map/ppermute | solution.py:31
  (174 shorter events, 51.9 us)
Async XLA Ops:
  2.2 28.4 %collective-permute-start.3 = (bf16[512,256]{1,0:T(8,128)(2,1)S(1)}, bf16[512,256]{1,0:T(8,128)(2,1)S(1)}, u32[]{:S(2)}, u32[]{:S(2)}) collective-permute-start(bf16[512,256]{1,0:T(8,128)(2,1)S(1)} %bitcast.89), channel_id=1, source_target_pairs={{0,4},{1,5},{2,6},{3,7},{4,0},{5,1},{6,2},{7,3},{8,12},{9,13},{10,... | collective-permute-start | bytes 786440 | tf_op jit(solution)/shard_map/ppermute | solution.py:26
  5.2 26.0 %collective-permute-start.5 = (bf16[512,256]{1,0:T(8,128)(2,1)S(1)}, bf16[512,256]{1,0:T(8,128)(2,1)S(1)}, u32[]{:S(2)}, u32[]{:S(2)}) collective-permute-start(bf16[512,256]{1,0:T(8,128)(2,1)S(1)} %bitcast.90), channel_id=1, source_target_pairs={{0,6},{1,7},{2,4},{3,5},{4,2},{5,3},{6,0},{7,1},{8,14},{9,15},{10,... | collective-permute-start | bytes 786440 | tf_op jit(solution)/shard_map/ppermute | solution.py:26
  8.0 12.2 %collective-permute-start.14 = (bf16[128,16]{0,1:T(8,128)(2,1)S(1)}, bf16[128,16]{0,1:T(8,128)(2,1)S(1)}, u32[]{:S(2)}, u32[]{:S(2)}) collective-permute-start(bf16[128,16]{0,1:T(8,128)(2,1)S(1)} %pad_maximum_fusion.8), channel_id=1, source_target_pairs={{0,8},{8,16},{16,24},{24,0},{1,9},{9,17},{17,25},{25,1},{2,10},{10... | collective-permute-start | bytes 12296 | tf_op jit(solution)/shard_map/ppermute | solution.py:31
  9.6 11.4 %collective-permute-start.15 = (bf16[128,16]{0,1:T(8,128)(2,1)S(1)}, bf16[128,16]{0,1:T(8,128)(2,1)S(1)}, u32[]{:S(2)}, u32[]{:S(2)}) collective-permute-start(bf16[128,16]{0,1:T(8,128)(2,1)S(1)} %pad_maximum_fusion.8), channel_id=1, source_target_pairs={{0,16},{8,24},{16,0},{24,8},{1,17},{9,25},{17,1},{25,9},{2,18},{10... | collective-permute-start | bytes 12296 | tf_op jit(solution)/shard_map/ppermute | solution.py:31
  12.2 9.0 %collective-permute-start.16 = (bf16[128,16]{0,1:T(8,128)(2,1)S(1)}, bf16[128,16]{0,1:T(8,128)(2,1)S(1)}, u32[]{:S(2)}, u32[]{:S(2)}) collective-permute-start(bf16[128,16]{0,1:T(8,128)(2,1)S(1)} %pad_maximum_fusion.8), channel_id=1, source_target_pairs={{0,24},{8,0},{16,8},{24,16},{1,25},{9,1},{17,9},{25,17},{2,26},{10... | collective-permute-start | bytes 12296 | tf_op jit(solution)/shard_map/ppermute | solution.py:31
  20.3 10.9 %collective-permute-start.4 = (bf16[512,256]{1,0:T(8,128)(2,1)S(1)}, bf16[512,256]{1,0:T(8,128)(2,1)S(1)}, u32[]{:S(2)}, u32[]{:S(2)}) collective-permute-start(bf16[512,256]{1,0:T(8,128)(2,1)S(1)} %bitcast.81), channel_id=1, source_target_pairs={{0,2},{1,3},{2,0},{3,1},{4,6},{5,7},{6,4},{7,5},{8,10},{9,11},{10,... | collective-permute-start | bytes 786440 | tf_op jit(solution)/shard_map/ppermute | solution.py:26
  21.0 11.0 %collective-permute-start.6 = (bf16[512,256]{1,0:T(8,128)(2,1)S(1)}, bf16[512,256]{1,0:T(8,128)(2,1)S(1)}, u32[]{:S(2)}, u32[]{:S(2)}) collective-permute-start(bf16[512,256]{1,0:T(8,128)(2,1)S(1)} %bitcast.82), channel_id=1, source_target_pairs={{0,1},{1,0},{2,3},{3,2},{4,5},{5,4},{6,7},{7,6},{8,9},{9,8},{10,11... | collective-permute-start | bytes 786440 | tf_op jit(solution)/shard_map/ppermute | solution.py:26
  54.2 9.1 %collective-permute-start.28 = (bf16[16,2048]{1,0:T(8,128)(2,1)S(1)}, bf16[16,2048]{1,0:T(8,128)(2,1)S(1)}, u32[]{:S(2)}, u32[]{:S(2)}) collective-permute-start(bf16[16,2048]{1,0:T(8,128)(2,1)S(1)} %get-tuple-element.51), channel_id=1, source_target_pairs={{0,16},{8,24},{16,0},{24,8},{1,17},{9,25},{17,1},{25,9},{2,18},{10... | collective-permute-start | bytes 196616 | tf_op jit(solution)/shard_map/ppermute | solution.py:31
  54.5 8.7 %collective-permute-start.29 = (bf16[16,2048]{1,0:T(8,128)(2,1)S(1)}, bf16[16,2048]{1,0:T(8,128)(2,1)S(1)}, u32[]{:S(2)}, u32[]{:S(2)}) collective-permute-start(bf16[16,2048]{1,0:T(8,128)(2,1)S(1)} %get-tuple-element.51), channel_id=1, source_target_pairs={{0,24},{8,0},{16,8},{24,16},{1,25},{9,1},{17,9},{25,17},{2,26},{10... | collective-permute-start | bytes 196616 | tf_op jit(solution)/shard_map/ppermute | solution.py:31
  57.6 8.4 %collective-permute-start.17 = (bf16[16,2048]{1,0:T(8,128)(2,1)S(1)}, bf16[16,2048]{1,0:T(8,128)(2,1)S(1)}, u32[]{:S(2)}, u32[]{:S(2)}) collective-permute-start(bf16[16,2048]{1,0:T(8,128)(2,1)S(1)} %get-tuple-element.54), channel_id=1, source_target_pairs={{0,8},{8,16},{16,24},{24,0},{1,9},{9,17},{17,25},{25,1},{2,10},{10... | collective-permute-start | bytes 196616 | tf_op jit(solution)/shard_map/ppermute | solution.py:31
  58.2 9.2 %collective-permute-start.18 = (bf16[16,2048]{1,0:T(8,128)(2,1)S(1)}, bf16[16,2048]{1,0:T(8,128)(2,1)S(1)}, u32[]{:S(2)}, u32[]{:S(2)}) collective-permute-start(bf16[16,2048]{1,0:T(8,128)(2,1)S(1)} %get-tuple-element.54), channel_id=1, source_target_pairs={{0,16},{8,24},{16,0},{24,8},{1,17},{9,25},{17,1},{25,9},{2,18},{10... | collective-permute-start | bytes 196616 | tf_op jit(solution)/shard_map/ppermute | solution.py:31
  63.3 12.8 %collective-permute-start.30 = (bf16[64,2048]{1,0:T(8,128)(2,1)S(1)}, bf16[64,2048]{1,0:T(8,128)(2,1)S(1)}, u32[]{:S(2)}, u32[]{:S(2)}) collective-permute-start(bf16[64,2048]{1,0:T(8,128)(2,1)S(1)} %pad_maximum_fusion.2), channel_id=1, source_target_pairs={{0,4},{1,5},{2,6},{3,7},{4,0},{5,1},{6,2},{7,3},{8,12},{9,13},{10,... | collective-permute-start | bytes 786440 | tf_op jit(solution)/shard_map/ppermute | solution.py:26
  64.5 12.4 %collective-permute-start.31 = (bf16[64,2048]{1,0:T(8,128)(2,1)S(1)}, bf16[64,2048]{1,0:T(8,128)(2,1)S(1)}, u32[]{:S(2)}, u32[]{:S(2)}) collective-permute-start(bf16[64,2048]{1,0:T(8,128)(2,1)S(1)} %pad_maximum_fusion.2), channel_id=1, source_target_pairs={{0,2},{1,3},{2,0},{3,1},{4,6},{5,7},{6,4},{7,5},{8,10},{9,11},{10,... | collective-permute-start | bytes 786440 | tf_op jit(solution)/shard_map/ppermute | solution.py:26
  66.0 12.5 %collective-permute-start.32 = (bf16[64,2048]{1,0:T(8,128)(2,1)S(1)}, bf16[64,2048]{1,0:T(8,128)(2,1)S(1)}, u32[]{:S(2)}, u32[]{:S(2)}) collective-permute-start(bf16[64,2048]{1,0:T(8,128)(2,1)S(1)} %pad_maximum_fusion.2), channel_id=1, source_target_pairs={{0,6},{1,7},{2,4},{3,5},{4,2},{5,3},{6,0},{7,1},{8,14},{9,15},{10,... | collective-permute-start | bytes 786440 | tf_op jit(solution)/shard_map/ppermute | solution.py:26
  67.4 11.2 %collective-permute-start.33 = (bf16[64,2048]{1,0:T(8,128)(2,1)S(1)}, bf16[64,2048]{1,0:T(8,128)(2,1)S(1)}, u32[]{:S(2)}, u32[]{:S(2)}) collective-permute-start(bf16[64,2048]{1,0:T(8,128)(2,1)S(1)} %pad_maximum_fusion.2), channel_id=1, source_target_pairs={{0,1},{1,0},{2,3},{3,2},{4,5},{5,4},{6,7},{7,6},{8,9},{9,8},{10,11... | collective-permute-start | bytes 786440 | tf_op jit(solution)/shard_map/ppermute | solution.py:26
  67.4 16.3 %collective-permute-start.20 = (bf16[64,2048]{1,0:T(8,128)(2,1)S(1)}, bf16[64,2048]{1,0:T(8,128)(2,1)S(1)}, u32[]{:S(2)}, u32[]{:S(2)}) collective-permute-start(bf16[64,2048]{1,0:T(8,128)(2,1)S(1)} %pad_maximum_fusion.1), channel_id=1, source_target_pairs={{0,4},{1,5},{2,6},{3,7},{4,0},{5,1},{6,2},{7,3},{8,12},{9,13},{10,... | collective-permute-start | bytes 786440 | tf_op jit(solution)/shard_map/ppermute | solution.py:26
  76.0 8.5 %collective-permute-start.21 = (bf16[64,2048]{1,0:T(8,128)(2,1)S(1)}, bf16[64,2048]{1,0:T(8,128)(2,1)S(1)}, u32[]{:S(2)}, u32[]{:S(2)}) collective-permute-start(bf16[64,2048]{1,0:T(8,128)(2,1)S(1)} %pad_maximum_fusion.1), channel_id=1, source_target_pairs={{0,2},{1,3},{2,0},{3,1},{4,6},{5,7},{6,4},{7,5},{8,10},{9,11},{10,... | collective-permute-start | bytes 786440 | tf_op jit(solution)/shard_map/ppermute | solution.py:26
  76.9 10.0 %collective-permute-start.22 = (bf16[64,2048]{1,0:T(8,128)(2,1)S(1)}, bf16[64,2048]{1,0:T(8,128)(2,1)S(1)}, u32[]{:S(2)}, u32[]{:S(2)}) collective-permute-start(bf16[64,2048]{1,0:T(8,128)(2,1)S(1)} %pad_maximum_fusion.1), channel_id=1, source_target_pairs={{0,6},{1,7},{2,4},{3,5},{4,2},{5,3},{6,0},{7,1},{8,14},{9,15},{10,... | collective-permute-start | bytes 786440 | tf_op jit(solution)/shard_map/ppermute | solution.py:26
  78.5 9.1 %collective-permute-start.23 = (bf16[64,2048]{1,0:T(8,128)(2,1)S(1)}, bf16[64,2048]{1,0:T(8,128)(2,1)S(1)}, u32[]{:S(2)}, u32[]{:S(2)}) collective-permute-start(bf16[64,2048]{1,0:T(8,128)(2,1)S(1)} %pad_maximum_fusion.1), channel_id=1, source_target_pairs={{0,1},{1,0},{2,3},{3,2},{4,5},{5,4},{6,7},{7,6},{8,9},{9,8},{10,11... | collective-permute-start | bytes 786440 | tf_op jit(solution)/shard_map/ppermute | solution.py:26
  78.6 10.2 %collective-permute-start.34 = (bf16[64,2048]{1,0:T(8,128)(2,1)S(1)}, bf16[64,2048]{1,0:T(8,128)(2,1)S(1)}, u32[]{:S(2)}, u32[]{:S(2)}) collective-permute-start(bf16[64,2048]{1,0:T(8,128)(2,1)S(1)} %collective-permute-done.30), channel_id=1, source_target_pairs={{0,1},{1,0},{2,3},{3,2},{4,5},{5,4},{6,7},{7,6},{8,9},{9,8},{10,11... | collective-permute-start | bytes 786440 | tf_op jit(solution)/shard_map/ppermute | solution.py:26
  88.8 9.6 %collective-permute-start.26 = (bf16[64,2048]{1,0:T(8,128)(2,1)S(1)}, bf16[64,2048]{1,0:T(8,128)(2,1)S(1)}, u32[]{:S(2)}, u32[]{:S(2)}) collective-permute-start(bf16[64,2048]{1,0:T(8,128)(2,1)S(1)} %collective-permute-done.22), channel_id=1, source_target_pairs={{0,1},{1,0},{2,3},{3,2},{4,5},{5,4},{6,7},{7,6},{8,9},{9,8},{10,11... | collective-permute-start | bytes 786440 | tf_op jit(solution)/shard_map/ppermute | solution.py:26
  114.5 7.3 %collective-permute-start.37 = (bf16[256,2048]{1,0:T(8,128)(2,1)S(1)}, bf16[256,2048]{1,0:T(8,128)(2,1)S(1)}, u32[]{:S(2)}, u32[]{:S(2)}) collective-permute-start(bf16[256,2048]{1,0:T(8,128)(2,1)S(1)} %get-tuple-element.19), channel_id=1, source_target_pairs={{0,1},{1,0},{2,3},{3,2},{4,5},{5,4},{6,7},{7,6},{8,9},{9,8},{10,11... | collective-permute-start | bytes 3145736 | tf_op jit(solution)/shard_map/ppermute | solution.py:26
  122.1 9.2 %collective-permute-start.38 = (bf16[64,2048]{1,0:T(8,128)(2,1)S(1)}, bf16[64,2048]{1,0:T(8,128)(2,1)S(1)}, u32[]{:S(2)}, u32[]{:S(2)}) collective-permute-start(bf16[64,2048]{1,0:T(8,128)(2,1)S(1)} %get-tuple-element.34), channel_id=1, source_target_pairs={{0,4},{1,5},{2,6},{3,7},{4,0},{5,1},{6,2},{7,3},{8,12},{9,13},{10,... | collective-permute-start | bytes 786440 | tf_op jit(solution)/shard_map/ppermute | solution.py:26
  123.4 10.0 %collective-permute-start.39 = (bf16[64,2048]{1,0:T(8,128)(2,1)S(1)}, bf16[64,2048]{1,0:T(8,128)(2,1)S(1)}, u32[]{:S(2)}, u32[]{:S(2)}) collective-permute-start(bf16[64,2048]{1,0:T(8,128)(2,1)S(1)} %get-tuple-element.36), channel_id=1, source_target_pairs={{0,2},{1,3},{2,0},{3,1},{4,6},{5,7},{6,4},{7,5},{8,10},{9,11},{10,... | collective-permute-start | bytes 786440 | tf_op jit(solution)/shard_map/ppermute | solution.py:26
  124.8 13.6 %collective-permute-start.40 = (bf16[64,2048]{1,0:T(8,128)(2,1)S(1)}, bf16[64,2048]{1,0:T(8,128)(2,1)S(1)}, u32[]{:S(2)}, u32[]{:S(2)}) collective-permute-start(bf16[64,2048]{1,0:T(8,128)(2,1)S(1)} %get-tuple-element.35), channel_id=1, source_target_pairs={{0,6},{1,7},{2,4},{3,5},{4,2},{5,3},{6,0},{7,1},{8,14},{9,15},{10,... | collective-permute-start | bytes 786440 | tf_op jit(solution)/shard_map/ppermute | solution.py:26
  125.9 17.8 %collective-permute-start.45 = (bf16[64,2048]{1,0:T(8,128)(2,1)S(1)}, bf16[64,2048]{1,0:T(8,128)(2,1)S(1)}, u32[]{:S(2)}, u32[]{:S(2)}) collective-permute-start(bf16[64,2048]{1,0:T(8,128)(2,1)S(1)} %get-tuple-element.37), channel_id=1, source_target_pairs={{0,4},{1,5},{2,6},{3,7},{4,0},{5,1},{6,2},{7,3},{8,12},{9,13},{10,... | collective-permute-start | bytes 786440 | tf_op jit(solution)/shard_map/ppermute | solution.py:26
  127.2 18.4 %collective-permute-start.46 = (bf16[64,2048]{1,0:T(8,128)(2,1)S(1)}, bf16[64,2048]{1,0:T(8,128)(2,1)S(1)}, u32[]{:S(2)}, u32[]{:S(2)}) collective-permute-start(bf16[64,2048]{1,0:T(8,128)(2,1)S(1)} %get-tuple-element.39), channel_id=1, source_target_pairs={{0,2},{1,3},{2,0},{3,1},{4,6},{5,7},{6,4},{7,5},{8,10},{9,11},{10,... | collective-permute-start | bytes 786440 | tf_op jit(solution)/shard_map/ppermute | solution.py:26
  131.2 17.7 %collective-permute-start.47 = (bf16[64,2048]{1,0:T(8,128)(2,1)S(1)}, bf16[64,2048]{1,0:T(8,128)(2,1)S(1)}, u32[]{:S(2)}, u32[]{:S(2)}) collective-permute-start(bf16[64,2048]{1,0:T(8,128)(2,1)S(1)} %get-tuple-element.38), channel_id=1, source_target_pairs={{0,6},{1,7},{2,4},{3,5},{4,2},{5,3},{6,0},{7,1},{8,14},{9,15},{10,... | collective-permute-start | bytes 786440 | tf_op jit(solution)/shard_map/ppermute | solution.py:26
  138.6 15.6 %collective-permute-start.41 = (bf16[16,2048]{1,0:T(8,128)(2,1)S(1)}, bf16[16,2048]{1,0:T(8,128)(2,1)S(1)}, u32[]{:S(2)}, u32[]{:S(2)}) collective-permute-start(bf16[16,2048]{1,0:T(8,128)(2,1)S(1)} %get-tuple-element.45), channel_id=1, source_target_pairs={{0,24},{8,0},{16,8},{24,16},{1,25},{9,1},{17,9},{25,17},{2,26},{10... | collective-permute-start | bytes 196616 | tf_op jit(solution)/shard_map/ppermute | solution.py:31
  140.8 13.4 %collective-permute-start.42 = (bf16[16,2048]{1,0:T(8,128)(2,1)S(1)}, bf16[16,2048]{1,0:T(8,128)(2,1)S(1)}, u32[]{:S(2)}, u32[]{:S(2)}) collective-permute-start(bf16[16,2048]{1,0:T(8,128)(2,1)S(1)} %get-tuple-element.47), channel_id=1, source_target_pairs={{0,16},{8,24},{16,0},{24,8},{1,17},{9,25},{17,1},{25,9},{2,18},{10... | collective-permute-start | bytes 196616 | tf_op jit(solution)/shard_map/ppermute | solution.py:31
  143.7 10.5 %collective-permute-start.43 = (bf16[16,2048]{1,0:T(8,128)(2,1)S(1)}, bf16[16,2048]{1,0:T(8,128)(2,1)S(1)}, u32[]{:S(2)}, u32[]{:S(2)}) collective-permute-start(bf16[16,2048]{1,0:T(8,128)(2,1)S(1)} %get-tuple-element.46), channel_id=1, source_target_pairs={{0,8},{8,16},{16,24},{24,0},{1,9},{9,17},{17,25},{25,1},{2,10},{10... | collective-permute-start | bytes 196616 | tf_op jit(solution)/shard_map/ppermute | solution.py:31
  151.3 7.8 %collective-permute-start.49 = (bf16[16,2048]{1,0:T(8,128)(2,1)S(1)}, bf16[16,2048]{1,0:T(8,128)(2,1)S(1)}, u32[]{:S(2)}, u32[]{:S(2)}) collective-permute-start(bf16[16,2048]{1,0:T(8,128)(2,1)S(1)} %get-tuple-element.50), channel_id=1, source_target_pairs={{0,16},{8,24},{16,0},{24,8},{1,17},{9,25},{17,1},{25,9},{2,18},{10... | collective-permute-start | bytes 196616 | tf_op jit(solution)/shard_map/ppermute | solution.py:31
  (21 other events, 111.8 us)

commit v2 on v1

v2 whole, which is shorter than its diff:
```python
import functools

import jax
import jax.numpy as jnp
from jax import lax
from jax.experimental import pallas as pl
from jax.experimental.pallas import tpu as pltpu
from jax.sharding import PartitionSpec as P

DH = 128
HQ = 32
KVH = 2
EXPERTS = 64
CAP = 32
SPLIT = 8


NEG = -1e30
EPS = 1e-06
RISE_LIMIT = 34 * 1024 * 1024
FALL_LIMIT = 37 * 1024 * 1024
ATTEND_LIMIT = 48 * 1024 * 1024
READY = 8
LOG2E = 1.4426950408889634


def hop(value, mask):
    count = lax.axis_size("seq")
    return lax.ppermute(value, "seq", [(i, i ^ mask) for i in range(count)])


def turn(value, step):
    count = lax.axis_size("req")
    return lax.ppermute(value, "req", [(i, i ^ step) for i in range(count)])


def block_order(parts):
    bits = parts.bit_length() - 1
    return [int(format(p, "b").zfill(bits)[::-1], 2) if bits else 0 for p in range(parts)]


def ancestry(parents):
    count = parents.shape[0]
    node = jnp.arange(count, dtype=jnp.int32)
    linked = (parents[:, None] == node[None, :]) | (node[:, None] == node[None, :])
    reach = linked.astype(jnp.bfloat16)
    hops = 1
    while hops < count:
        paths = jnp.dot(reach, reach, preferred_element_type=jnp.float32)
        reach = jnp.minimum(paths, 1.0).astype(jnp.bfloat16)
        hops = hops * 2
    return reach


def attend_kernel(parts, mine, valid_ref, perm_ref, packed_ref, mask_ref, *refs):
    kv_refs = refs[:parts]
    w_any, keep_ref, send_ref, w_ref, sem = refs[parts:]
    copy = pltpu.make_async_copy(w_any, w_ref, sem)
    copy.start()
    rows = packed_ref.shape[0]
    lanes = mine * DH
    scale = DH ** (-0.5) * LOG2E
    perm = perm_ref[...]
    q = jnp.dot(perm, packed_ref[:, :lanes], preferred_element_type=jnp.float32).astype(jnp.bfloat16)
    q = jnp.concatenate([q[:, a * DH : (a + 1) * DH] for a in range(mine)], axis=0)

    def scores(keys):
        return (
            lax.dot_general(q, keys, (((1,), (1,)), ((), ())), preferred_element_type=jnp.float32)
            * scale
        )

    mask = jnp.dot(perm, mask_ref[...], preferred_element_type=jnp.float32)
    linked = jnp.concatenate([mask] * mine, axis=0) > 0.5
    s = jnp.where(linked, scores(packed_ref[:, lanes : lanes + DH]), NEG)
    top = jnp.max(s, axis=-1, keepdims=True)
    weights = jnp.exp2(s - top)
    total = jnp.sum(weights, axis=-1, keepdims=True)
    out = jnp.dot(
        weights.astype(jnp.bfloat16),
        packed_ref[:, lanes + DH :],
        preferred_element_type=jnp.float32,
    )
    for part in range(parts):
        kv = kv_refs[part]
        place = lax.broadcasted_iota(jnp.int32, (1, kv.shape[0]), 1)
        bias = jnp.where(place < valid_ref[part], 0.0, NEG)
        s = scores(kv[:, :DH]) + bias
        peak = jnp.maximum(top, jnp.max(s, axis=-1, keepdims=True))
        weights = jnp.exp2(s - peak)
        fade = jnp.exp2(top - peak)
        total = total * fade + jnp.sum(weights, axis=-1, keepdims=True)
        out = out * fade + jnp.dot(
            weights.astype(jnp.bfloat16), kv[:, DH:], preferred_element_type=jnp.float32
        )
        top = peak
    attention = (out / total).astype(jnp.bfloat16)
    attention = jnp.concatenate(
        [attention[a * rows : (a + 1) * rows] for a in range(mine)], axis=1
    )
    copy.wait()
    half = rows // 2
    width = w_ref.shape[1]
    tile = min(width, 1024)
    for first in range(0, width, tile):
        piece = jnp.dot(
            attention, w_ref[:, first : first + tile], preferred_element_type=jnp.float32
        ).astype(jnp.bfloat16)
        keep_ref[:, first : first + tile] = piece[:half]
        send_ref[:, first : first + tile] = piece[half:]


def attend(valid, perm, packed, mask, blocks, w):
    parts = len(blocks)
    rows, mine = packed.shape[0], (packed.shape[1] - 2 * DH) // DH
    span = blocks[0].shape[0]
    full = pl.BlockSpec(memory_space=pltpu.VMEM)
    out = jax.ShapeDtypeStruct((rows // 2, w.shape[1]), jnp.bfloat16)
    reach = rows + parts * span
    return pl.pallas_call(
        functools.partial(attend_kernel, parts, mine),
        out_shape=(out, out),
        in_specs=[pl.BlockSpec(memory_space=pltpu.SMEM)]
        + [full] * (parts + 3)
        + [pl.BlockSpec(memory_space=pltpu.HBM)],
        out_specs=(full, full),
        scratch_shapes=[pltpu.VMEM(w.shape, w.dtype), pltpu.SemaphoreType.DMA],
        compiler_params=pltpu.CompilerParams(vmem_limit_bytes=ATTEND_LIMIT),
        cost_estimate=pl.CostEstimate(
            flops=4 * rows * mine * DH * reach + 2 * rows * mine * DH * w.shape[1],
            bytes_accessed=2 * w.size + 4 * DH * reach + 2 * rows * w.shape[1],
            transcendentals=rows * mine * reach,
        ),
    )(valid, perm, packed, mask, *blocks, w)


def seat_rows(first_ref, topk, table, back_ref, experts, seats):
    count = table.shape[0]
    block = min(count, 256)
    lane = lax.broadcasted_iota(jnp.int32, (count, DH), 1)
    hits = []
    spread = jnp.zeros((count, DH), jnp.float32)
    for e in range(experts):
        named = (first_ref[0] + e).astype(jnp.float32)
        match = jnp.where((table == named) & (lane < topk), 1.0, 0.0)
        hits.append(jnp.max(match, axis=1, keepdims=True))
        spread = spread + jnp.where(lane == e, hits[e], 0.0)
    ahead = lax.broadcasted_iota(jnp.int32, (block, block), 0) > lax.broadcasted_iota(
        jnp.int32, (block, block), 1
    )
    ahead = jnp.where(ahead, 1.0, 0.0).astype(jnp.bfloat16)
    place = lax.broadcasted_iota(jnp.int32, (block, seats), 1).astype(jnp.float32)
    carry = jnp.zeros((1, DH), jnp.float32)
    for at in range(0, count, block):
        here = spread[at : at + block]
        before = carry + jnp.dot(
            ahead, here.astype(jnp.bfloat16), preferred_element_type=jnp.float32
        )
        carry = carry + jnp.sum(here, axis=0, keepdims=True)
        for e in range(experts):
            seat = jnp.sum(jnp.where(lane[:block] == e, before, 0.0), axis=1, keepdims=True)
            taken = (hits[e][at : at + block] > 0.5) & (seat == place)
            back_ref[at : at + block, e * seats : (e + 1) * seats] = jnp.where(
                taken, 1.0, 0.0
            ).astype(jnp.bfloat16)


def pick_rows(back_ref, rows, first, width):
    return lax.dot_general(
        back_ref[...],
        rows[:, first : first + width],
        (((0,), (0,)), ((), ())),
        preferred_element_type=jnp.float32,
    )


def expert_kernel(pieces, experts, seats, topk, chunk, *refs):
    refs = list(refs)

    def take(count):
        out = refs[:count]
        del refs[:count]
        return out

    part_refs = take(pieces)
    wg_any, wu_any = take(2)
    if chunk == 0:
        first_ref, wd_any = take(2)
        gate_ref, up_ref, back_ref, rate_ref, ready_ref = take(5)
    else:
        gate_in, up_in, back_ref, rate_ref, ready_ref, wd_any = take(6)
        outs = take(4)
    rows, picked, wg, wu, part_sem, gate_sem, up_sem = take(7)
    held, cut, wide = wg.shape
    per_expert = held // experts
    size = rows.shape[0] // pieces
    moves = [
        pltpu.make_async_copy(ref, rows.at[pl.ds(i * size, size)], part_sem.at[i])
        for i, ref in enumerate(part_refs)
    ]
    for move in moves:
        move.start()
    first = chunk * cut

    def weight_moves(p):
        return (
            pltpu.make_async_copy(wg_any.at[p, pl.ds(first, cut)], wg.at[p], gate_sem.at[p]),
            pltpu.make_async_copy(wu_any.at[p, pl.ds(first, cut)], wu.at[p], up_sem.at[p]),
        )

    for p in range(held):
        for move in weight_moves(p):
            move.start()
    if chunk == 0:
        (ready_sem,) = take(1)
        early = [
            pltpu.make_async_copy(wd_any.at[p], ready_ref.at[p], ready_sem.at[p])
            for p in range(ready_ref.shape[0])
        ]
        for move in early:
            move.start()
    else:
        wd, hidden, flat, down_sem = take(4)

        ready = ready_ref.shape[0]

        def down_move(p):
            place = pl.ds((p - ready) * wide, wide)
            return pltpu.make_async_copy(wd_any.at[p], wd.at[place], down_sem.at[p - ready])

        for p in range(ready, held):
            down_move(p).start()
    for move in moves:
        move.wait()
    if chunk == 0:
        seat_rows(first_ref, topk, rows[:, cut:].astype(jnp.float32), back_ref, experts, seats)
        meta = pick_rows(back_ref, rows, cut, DH)
        lane = lax.broadcasted_iota(jnp.int32, (seats, DH), 1)
        for e in range(experts):
            named = (first_ref[0] + e).astype(jnp.float32)
            own = meta[e * seats : (e + 1) * seats]
            gates = pltpu.roll(own, DH - topk, 1)
            rate_ref[e] = jnp.sum(
                jnp.where((own == named) & (lane < topk), gates, 0.0), axis=1, keepdims=True
            )
    tile = 512 if cut % 512 == 0 else cut
    for c in range(0, cut, tile):
        picked[:, c : c + tile] = pick_rows(back_ref, rows, c, tile).astype(jnp.bfloat16)
    for e in range(experts):

        def panel(k, carry, e=e):
            p = e * per_expert + k
            for move in weight_moves(p):
                move.wait()
            w = jnp.concatenate([wg[p], wu[p]], axis=1)
            both = jnp.dot(
                picked[e * seats : (e + 1) * seats], w, preferred_element_type=jnp.float32
            )
            gate, up = both[:, :wide], both[:, wide:]
            if chunk:
                gate, up = gate + gate_in[p], up + up_in[p]
                value = gate / (1.0 + jnp.exp(-gate)) * up * rate_ref[e]
                place = pl.ds(pl.multiple_of(k * wide, wide), wide)
                hidden[e * seats : (e + 1) * seats, place] = value.astype(jnp.bfloat16)
            else:
                gate_ref[p] = gate
                up_ref[p] = up
            return carry

        lax.fori_loop(0, per_expert, panel, 0)
    if chunk == 0:
        for move in early:
            move.wait()
        return
    deep = per_expert * wide
    depth = flat.shape[1]
    for e in range(experts):
        low, high = e * per_expert, (e + 1) * per_expert
        for p in range(max(low, ready), high):
            down_move(p).wait()
        split = min(max(ready, low), high)
        for c in range(0, depth, tile):
            total = None
            if split > low:
                total = jnp.dot(
                    hidden[e * seats : (e + 1) * seats, : (split - low) * wide],
                    ready_ref[low:split, :, c : c + tile].reshape(-1, tile),
                    preferred_element_type=jnp.float32,
                )
            if split < high:
                rest = jnp.dot(
                    hidden[e * seats : (e + 1) * seats, (split - low) * wide :],
                    wd[(split - ready) * wide : (high - ready) * wide, c : c + tile],
                    preferred_element_type=jnp.float32,
                )
                total = rest if total is None else total + rest
            flat[e * seats : (e + 1) * seats, c : c + tile] = total.astype(jnp.bfloat16)
    for c in range(0, depth, tile):
        moved = jnp.dot(
            back_ref[...], flat[:, c : c + tile], preferred_element_type=jnp.float32
        ).astype(jnp.bfloat16)
        half = moved.shape[0] // 2
        keep_ref, send_ref = outs[2 * (c // cut)], outs[2 * (c // cut) + 1]
        at = c % cut
        keep_ref[:, at : at + tile] = moved[:half]
        send_ref[:, at : at + tile] = moved[half:]


def expert_call(rows, w_gate, w_up, chunk, cut, topk, experts, seats, first=None, sums=None, w_down=None):
    held, depth, wide = w_gate.shape
    count = rows[0].shape[0] * len(rows)
    full = pl.BlockSpec(memory_space=pltpu.VMEM)
    anywhere = pl.BlockSpec(memory_space=pl.ANY)
    far = pl.BlockSpec(memory_space=pltpu.HBM)
    deep = held // experts * wide
    args = [*rows, w_gate, w_up]
    in_specs = [anywhere] * len(rows) + [far, far]
    scratch = [
        pltpu.VMEM((count, rows[0].shape[1]), jnp.bfloat16),
        pltpu.VMEM((experts * seats, cut), jnp.bfloat16),
        pltpu.VMEM((held, cut, wide), jnp.bfloat16),
        pltpu.VMEM((held, cut, wide), jnp.bfloat16),
        pltpu.SemaphoreType.DMA((len(rows),)),
        pltpu.SemaphoreType.DMA((held,)),
        pltpu.SemaphoreType.DMA((held,)),
    ]
    flops = 4 * held * seats * cut * wide + 2 * experts * seats * count * cut
    moved = 4 * held * cut * wide + 2 * count * cut
    if chunk == 0:
        early = max(1, held * READY // 16)
        args += [first, w_down]
        in_specs += [pl.BlockSpec(memory_space=pltpu.SMEM), far]
        outs = [jax.ShapeDtypeStruct((held, seats, wide), jnp.float32)] * 2 + [
            jax.ShapeDtypeStruct((count, experts * seats), jnp.bfloat16),
            jax.ShapeDtypeStruct((experts, seats, 1), jnp.float32),
            jax.ShapeDtypeStruct((early, wide, depth), jnp.bfloat16),
        ]
        scratch += [pltpu.SemaphoreType.DMA((early,))]
        moved += 2 * early * wide * depth
    else:
        ready = sums[4]
        args += [*sums, w_down]
        in_specs += [full] * 5 + [far]
        outs = [jax.ShapeDtypeStruct((count // 2, cut), jnp.bfloat16)] * 4
        scratch += [
            pltpu.VMEM((max(1, held - ready.shape[0]) * wide, depth), jnp.bfloat16),
            pltpu.VMEM((experts * seats, deep), jnp.bfloat16),
            pltpu.VMEM((experts * seats, depth), jnp.bfloat16),
            pltpu.SemaphoreType.DMA((max(1, held - ready.shape[0]),)),
        ]
        flops += 2 * held * seats * depth * wide + 2 * experts * seats * count * depth
        moved += 2 * held * depth * wide
    return pl.pallas_call(
        functools.partial(expert_kernel, len(rows), experts, seats, topk, chunk),
        out_shape=tuple(outs),
        in_specs=in_specs,
        out_specs=tuple([full] * len(outs)),
        scratch_shapes=scratch,
        compiler_params=pltpu.CompilerParams(vmem_limit_bytes=RISE_LIMIT if chunk == 0 else FALL_LIMIT),
        cost_estimate=pl.CostEstimate(flops=flops, bytes_accessed=moved, transcendentals=0),
    )(*args)


def body(
    queries,
    kv_cache,
    tree_kv,
    context_lengths,
    tree_parents,
    resid,
    out_weight,
    norm_gain,
    expert_ids,
    gate_weights,
    w_gate,
    w_up,
    w_down,
):
    here = lax.axis_index("seq")
    there = lax.axis_index("req")
    parts = lax.axis_size("seq")
    groups = lax.axis_size("req")
    bits = parts.bit_length() - 1
    order = block_order(parts)
    near = order[: parts // 2]
    own = queries.shape[1]
    rows = own * parts
    depth = resid.shape[2]

    span = kv_cache.shape[1]
    share = parts // KVH
    lane = kv_cache[0]
    heads = [
        lane[:, :, h * DH : (h + 1) * DH].reshape(span, 2 * DH) for h in range(KVH)
    ]

    def head_of(device):
        pick = heads[0]
        for h in range(1, KVH):
            pick = jnp.where(device // share == h, heads[h], pick)
        return pick

    half = [head_of(here ^ mask) if mask == 0 else None for mask in near]
    same = half[0]
    other = head_of(here ^ (parts // 2))
    half = [same] + [hop(other if mask & (parts // 2) else same, mask) for mask in near[1:]]
    valid = context_lengths[0] - jnp.stack([(here ^ mask) * span for mask in order])

    mine = HQ // parts
    tree_heads = [
        tree_kv[0][:, :, h * DH : (h + 1) * DH].reshape(own, 2 * DH) for h in range(KVH)
    ]
    asked = jnp.transpose(queries[0].reshape(own, parts, mine * DH), (1, 0, 2))
    trees = jnp.stack(tree_heads)[:, None]
    trees = jnp.broadcast_to(trees, (KVH, share, own, 2 * DH)).reshape(parts, own, 2 * DH)
    packed = jnp.concatenate([asked, trees], axis=2)
    packed = lax.all_to_all(packed, "seq", split_axis=0, concat_axis=0, tiled=True)
    packed = packed.reshape(rows, -1)

    wanted = jnp.stack([here ^ mask for mask in order])
    wanted = (wanted[:, None] * own + jnp.arange(own, dtype=jnp.int32)[None, :]).reshape(rows)
    perm = (wanted[:, None] == jnp.arange(rows, dtype=jnp.int32)[None, :]).astype(jnp.bfloat16)

    linked = ancestry(tree_parents[0])
    blocks = half + [hop(piece, 1) for piece in half]
    keep, send = attend(valid.astype(jnp.int32), perm, packed, linked, blocks, out_weight)

    got = hop(send, 1)
    pair = [
        keep[i * own : (i + 1) * own].astype(jnp.float32)
        + got[i * own : (i + 1) * own].astype(jnp.float32)
        for i in range(len(near))
    ]
    terms = [pair[0]] + [
        hop(pair[i].astype(jnp.bfloat16), near[i]).astype(jnp.float32)
        for i in range(1, len(near))
    ]
    attended = sum(terms[1:], terms[0]).astype(jnp.bfloat16)
    mid = (resid[0].astype(jnp.float32) + attended.astype(jnp.float32)).astype(jnp.bfloat16)
    midf = lax.optimization_barrier(mid).astype(jnp.float32)
    factor = lax.rsqrt(jnp.mean(midf * midf, axis=-1, keepdims=True) + EPS)
    normed = (midf * factor * norm_gain.astype(jnp.float32)).astype(jnp.bfloat16)

    table = jnp.concatenate(
        [expert_ids[0].astype(jnp.bfloat16), gate_weights[0]], axis=1
    )
    table = lax.dynamic_slice_in_dim(table, here * own, own, 0)
    topk = expert_ids.shape[2]
    table = jnp.pad(table, ((0, 0), (0, DH - 2 * topk)))
    held = w_gate.shape[0]
    experts = max(1, held // SPLIT)
    first = (((there * parts + here) * held) // SPLIT).astype(jnp.int32).reshape(1)
    seats = groups * CAP

    cut = depth // 2
    planes = []
    for chunk in range(2):
        piece = normed[:, chunk * cut : (chunk + 1) * cut]
        if chunk == 0:
            piece = jnp.concatenate([piece, table], axis=1)
        stack = jnp.concatenate([piece] + [turn(piece, d) for d in range(1, groups)], axis=0)
        planes.append([stack] + [hop(stack, mask) for mask in near[1:]])
    full = planes[0] + [hop(p, 1) for p in planes[0]]
    sums = expert_call(full, w_gate, w_up, 0, cut, topk, experts, seats, first=first, w_down=w_down)
    *plane, gate = lax.optimization_barrier((*planes[1], sums[0]))
    full = plane + [hop(p, 1) for p in plane]
    keep0, send0, keep1, send1 = expert_call(
        full, w_gate, w_up, 1, cut, topk, experts, seats, sums=(gate, *sums[1:]), w_down=w_down
    )

    size = groups * own

    def home(keep, got):
        pair = [
            keep[i * size : (i + 1) * size].astype(jnp.float32)
            + got[i * size : (i + 1) * size].astype(jnp.float32)
            for i in range(len(near))
        ]
        flat = pair[0]
        for i in range(1, len(near)):
            flat = flat + hop(pair[i].astype(jnp.bfloat16), near[i]).astype(jnp.float32)
        result = flat[:own]
        for d in range(1, groups):
            result = result + turn(
                flat[d * own : (d + 1) * own].astype(jnp.bfloat16), d
            ).astype(jnp.float32)
        return result.astype(jnp.bfloat16)

    got0 = hop(send0, 1)
    send1, got0 = lax.optimization_barrier((send1, got0))
    pieces = [home(keep0, got0), home(keep1, hop(send1, 1))]
    return (attended[None], jnp.concatenate(pieces, axis=1)[None])


def solution(mesh):
    placed = (
        P("req", "seq", None),
        P("req", "seq", None, None),
        P("req", "seq", None, None),
        P("req"),
        P("req", None),
        P("req", "seq", None),
        P("seq", None),
        P(),
        P("req", None, None),
        P("req", None, None),
        P(("req", "seq"), None, None),
        P(("req", "seq"), None, None),
        P(("req", "seq"), None, None),
    )
    return jax.shard_map(
        body,
        mesh=mesh,
        in_specs=placed,
        out_specs=(P("req", "seq", None), P("req", "seq", None)),
        check_vma=False,
    )
```

time: 161 us -> 142 us (0.88)
  starting transfers between devices: 57.3 us -> 43.3 us
  waiting for transfers between devices: 43.4 us -> 56.2 us
  Pallas kernels: 36.8 us -> 28.5 us
  local copies, waits for them, and re-layouts: 10.4 us -> 2.21 us
    ppermute x15 -> x12, starting transfers between devices: 25.9 us -> 14 us  [turn(): return lax.ppermute(value, 'req', [(i, i ^ step) for i in range(count)])]
    pallas_call x4 -> x2, Pallas kernels: 30 us -> 21.5 us  [expert_call(): pl.pallas_call(functools.partial(expert_kernel, len(rows), experts, seats...]
    ppermute x15 -> x12, waiting for transfers between devices: 7.71 us -> 15.8 us  [turn(): return lax.ppermute(value, 'req', [(i, i ^ step) for i in range(count)])]
    ppermute x36 -> x33, starting transfers between devices: 31.4 us -> 25.2 us  [hop(): return lax.ppermute(value, 'seq', [(i, i ^ mask) for i in range(count)])]
    unnamed x26 -> x4, local copies, waits for them, and re-layouts: 6.46 us -> 1.11 us
    ppermute x36 -> x33, waiting for transfers between devices: 35.7 us -> 40.4 us  [hop(): return lax.ppermute(value, 'seq', [(i, i ^ mask) for i in range(count)])]
    all_to_all x0 -> x1, starting transfers between devices: none -> 4.12 us  [body(): lax.all_to_all(packed, 'seq', split_axis=0, concat_axis=0, tiled=True)]
    select_n x4 -> x0, other arithmetic: 1.68 us -> none  [the longest x3 0.94 us: body(): kept = jnp.where(upper, high, low)]
  transfers between devices with their start and end apart: 51 -> 46, of which waited for: 22 -> 25; matrix products, arithmetic and copies ran while one was open for 10% -> 5% of each run, Pallas kernels for 9% -> 6%
where the time goes in v2:
time: 142 us
  waiting for transfers between devices  56.2 us (40%)
  starting transfers between devices  43.3 us (30%)
  Pallas kernels  28.5 us (20%)
  other arithmetic  8.14 us (6%)
  local copies, waits for them, and re-layouts  2.21 us (2%)
  matrix products  1.85 us (1%)
  between operations  1.63 us (1%)
    ppermute x33, waiting for transfers between devices, hop(): return lax.ppermute(value, 'seq', [(i, i ^ mask) for i in range(count)])  40.4 us
    ppermute x33, starting transfers between devices, hop(): return lax.ppermute(value, 'seq', [(i, i ^ mask) for i in range(count)])  25.2 us
    pallas_call x2, Pallas kernels, expert_call(): pl.pallas_call(functools.partial(expert_kernel, len(rows), experts, seats...  21.5 us
    ppermute x12, waiting for transfers between devices, turn(): return lax.ppermute(value, 'req', [(i, i ^ step) for i in range(count)])  15.8 us
    ppermute x12, starting transfers between devices, turn(): return lax.ppermute(value, 'req', [(i, i ^ step) for i in range(count)])  14 us
    pallas_call x1, Pallas kernels, attend(): pl.pallas_call(functools.partial(attend_kernel, parts, mine), out_shape=(...  7.02 us
    all_to_all x1, starting transfers between devices, body(): lax.all_to_all(packed, 'seq', split_axis=0, concat_axis=0, tiled=True)  4.12 us
  transfers between devices with their start and end apart: 46, of which 25 were waited for; matrix products, arithmetic and copies ran while one was open for 5% of the time, Pallas kernels for 6%

profile of v2, /device:TPU:0, one launch (start us, length us, event | category | flops | bytes accessed | tf_op | source)
XLA Modules:
  0.0 141.9 jit_solution(14778550369803778059)
XLA Ops:
  0.7 1.5 %broadcast_select_fusion = (bf16[512,2,128]{2,1,0:T(2,128)(2,1)S(1)}, bf16[512,2,128]{2,1,0:T(2,128)(2,1)S(1)}) fusion(pred[]{:T(512)S(6)} %eq.58, bf16[512,2,256]{2,1,0:T(2,128)(2,1)} %bitcast.59, pred[]{:T(512)S(6)} %eq.57), kind=kLoop, calls=%fused_computation.22 | loop fusion | flops 262144 | bytes 1048578 | tf_op jit(solution)/shard_map/jit(_where)/select_n | solution.py:400
  2.7 2.6 %collective-permute-start.1 = (bf16[512,256]{1,0:T(8,128)(2,1)S(1)}, bf16[512,256]{1,0:T(8,128)(2,1)S(1)}, u32[]{:S(2)}, u32[]{:S(2)}) collective-permute-start(bf16[512,256]{1,0:T(8,128)(2,1)S(1)} %bitcast.54), channel_id=1, source_target_pairs={{0,2},{1,3},{2,0},{3,1},{4,6},{5,7},{6,4},{7,5},{8,10},{9,11},{10,... | collective-permute-start | bytes 786440 | tf_op jit(solution)/shard_map/ppermute | solution.py:29
  5.3 1.6 %collective-permute-start.2 = (bf16[512,256]{1,0:T(8,128)(2,1)S(1)}, bf16[512,256]{1,0:T(8,128)(2,1)S(1)}, u32[]{:S(2)}, u32[]{:S(2)}) collective-permute-start(bf16[512,256]{1,0:T(8,128)(2,1)S(1)} %bitcast.62), channel_id=1, source_target_pairs={{0,6},{1,7},{2,4},{3,5},{4,2},{5,3},{6,0},{7,1},{8,14},{9,15},{10,... | collective-permute-start | bytes 786440 | tf_op jit(solution)/shard_map/ppermute | solution.py:29
  9.5 4.1 %all-to-all-start = ((bf16[8,16,768]{2,1,0:T(8,128)(2,1)}), bf16[8,16,768]{2,1,0:T(8,128)(2,1)S(1)}, u32[]{:S(2)}, u32[]{:S(2)}) async-start(bf16[8,16,768]{2,1,0:T(8,128)(2,1)} %pad_maximum_fusion.2), calls=%async_computation | async-start | bytes 393216 | tf_op jit(solution)/shard_map/all_to_all | solution.py:417
  16.3 3.3 %collective-permute-done.2.refs_3_ = bf16[512,256]{1,0:T(8,128)(2,1)S(1)} collective-permute-done((bf16[512,256]{1,0:T(8,128)(2,1)S(1)}, bf16[512,256]{1,0:T(8,128)(2,1)S(1)}, u32[]{:S(2)}, u32[]{:S(2)}) %collective-permute-start.2) | collective-permute-done | bytes 262176 | tf_op jit(solution)/shard_map/ppermute | solution.py:29
  19.6 2.6 %collective-permute-done.refs_1_ = bf16[512,256]{1,0:T(8,128)(2,1)S(1)} collective-permute-done((bf16[512,256]{1,0:T(8,128)(2,1)S(1)}, bf16[512,256]{1,0:T(8,128)(2,1)S(1)}, u32[]{:S(2)}, u32[]{:S(2)}) %collective-permute-start) | collective-permute-done | bytes 262176 | tf_op jit(solution)/shard_map/ppermute | solution.py:29
  23.7 7.0 %shard_map.140 = (bf16[64,4096]{1,0:T(8,128)(2,1)S(1)}, bf16[64,4096]{1,0:T(8,128)(2,1)S(1)}) custom-call(s32[8]{0:T(128)S(1)} %broadcast_subtract_fusion.valid_ref, bf16[128,128]{1,0:T(8,128)(2,1)S(1)} %fusion.17.perm_ref, bf16[128,768]{1,0:T(8,128)(2,1)S(1)} %bitcast.56, bf16[128,128]{1,0:T(8,128)(2,1)S(1)} %fusion.6.mask_ref, ...), custom_call_target="tpu_custom_call" | custom-call | flops 1644167168 | bytes 7405568 | tf_op jit(solution)/shard_map/pallas_call | solution.py:120
  30.9 1.8 %collective-permute-done.7 = bf16[64,4096]{1,0:T(8,128)(2,1)S(1)} collective-permute-done((bf16[64,4096]{1,0:T(8,128)(2,1)S(1)}, bf16[64,4096]{1,0:T(8,128)(2,1)S(1)}, u32[]{:S(2)}, u32[]{:S(2)}) %collective-permute-start.7) | collective-permute-done | bytes 524320 | tf_op jit(solution)/shard_map/ppermute | solution.py:29
  33.3 2.6 %collective-permute-start.10 = (bf16[16,4096]{1,0:T(8,128)(2,1)S(1)}, bf16[16,4096]{1,0:T(8,128)(2,1)S(1)}, u32[]{:S(2)}, u32[]{:S(2)}) collective-permute-start(bf16[16,4096]{1,0:T(8,128)(2,1)S(1)} %get-tuple-element.51), channel_id=1, source_target_pairs={{0,6},{1,7},{2,4},{3,5},{4,2},{5,3},{6,0},{7,1},{8,14},{9,15},{10,... | collective-permute-start | bytes 393224 | tf_op jit(solution)/shard_map/ppermute | solution.py:29
  38.6 2.6 %collective-permute-done.8 = bf16[16,4096]{1,0:T(8,128)(2,1)S(1)} collective-permute-done((bf16[16,4096]{1,0:T(8,128)(2,1)S(1)}, bf16[16,4096]{1,0:T(8,128)(2,1)S(1)}, u32[]{:S(2)}, u32[]{:S(2)}) %collective-permute-start.8) | collective-permute-done | bytes 131104 | tf_op jit(solution)/shard_map/ppermute | solution.py:29
  42.5 1.7 %fusion.10 = (bf16[16,4096]{1,0:T(8,128)(2,1)S(1)}, bf16[16,4096]{1,0:T(8,128)(2,1)}) fusion(bf16[1,16,4096]{2,1,0:T(8,128)(2,1)} %param.18, bf16[16,4096]{1,0:T(8,128)(2,1)S(1)} %collective-permute-done.10, bf16[16,4096]{1,0:T(8,128)(2,1)S(1)} %collective-permute-done.9, bf16[16,4096]{1,0:T(8,128)(2,1)S(1)} %collective-permute-done.8, ...), kind=kLoop, calls=%fused_computation.34 | loop fusion | flops 917504 | bytes 1048576 | tf_op jit(solution)/shard_map/convert_element_type | solution.py:439
  44.4 3.7 %collective-permute-start.19 = (bf16[16,2176]{1,0:T(8,128)(2,1)S(1)}, bf16[16,2176]{1,0:T(8,128)(2,1)S(1)}, u32[]{:S(2)}, u32[]{:S(2)}) collective-permute-start(bf16[16,2176]{1,0:T(8,128)(2,1)S(1)} %pad_maximum_fusion.3), channel_id=1, source_target_pairs={{0,24},{8,16},{16,8},{24,0},{1,25},{9,17},{17,9},{25,1},{2,26},{10... | collective-permute-start | bytes 208904 | tf_op jit(solution)/shard_map/ppermute | solution.py:34
  48.9 2.1 %collective-permute-done.19 = bf16[16,2176]{1,0:T(8,128)(2,1)S(1)} collective-permute-done((bf16[16,2176]{1,0:T(8,128)(2,1)S(1)}, bf16[16,2176]{1,0:T(8,128)(2,1)S(1)}, u32[]{:S(2)}, u32[]{:S(2)}) %collective-permute-start.19) | collective-permute-done | bytes 69664 | tf_op jit(solution)/shard_map/ppermute | solution.py:34
  50.9 2.6 %collective-permute-done.18 = bf16[16,2176]{1,0:T(8,128)(2,1)S(1)} collective-permute-done((bf16[16,2176]{1,0:T(8,128)(2,1)S(1)}, bf16[16,2176]{1,0:T(8,128)(2,1)S(1)}, u32[]{:S(2)}, u32[]{:S(2)}) %collective-permute-start.18) | collective-permute-done | bytes 69664 | tf_op jit(solution)/shard_map/ppermute | solution.py:34
  53.6 1.5 %collective-permute-start.22 = (bf16[64,2176]{1,0:T(8,128)(2,1)S(1)}, bf16[64,2176]{1,0:T(8,128)(2,1)S(1)}, u32[]{:S(2)}, u32[]{:S(2)}) collective-permute-start(bf16[64,2176]{1,0:T(8,128)(2,1)S(1)} %pad_maximum_fusion.refs_0_), channel_id=1, source_target_pairs={{0,6},{1,7},{2,4},{3,5},{4,2},{5,3},{6,0},{7,1},{8,14},{9,15},{10,... | collective-permute-start | bytes 835592 | tf_op jit(solution)/shard_map/ppermute | solution.py:29
  55.6 1.5 %collective-permute-start.20 = (bf16[64,2176]{1,0:T(8,128)(2,1)S(1)}, bf16[64,2176]{1,0:T(8,128)(2,1)S(1)}, u32[]{:S(2)}, u32[]{:S(2)}) collective-permute-start(bf16[64,2176]{1,0:T(8,128)(2,1)S(1)} %pad_maximum_fusion.refs_0_), channel_id=1, source_target_pairs={{0,4},{1,5},{2,6},{3,7},{4,0},{5,1},{6,2},{7,3},{8,12},{9,13},{10,... | collective-permute-start | bytes 835592 | tf_op jit(solution)/shard_map/ppermute | solution.py:29
  57.2 2.4 %collective-permute-start.13 = (bf16[16,2048]{1,0:T(8,128)(2,1)S(1)}, bf16[16,2048]{1,0:T(8,128)(2,1)S(1)}, u32[]{:S(2)}, u32[]{:S(2)}) collective-permute-start(bf16[16,2048]{1,0:T(8,128)(2,1)S(1)} %get-tuple-element.62), channel_id=1, source_target_pairs={{0,24},{8,16},{16,8},{24,0},{1,25},{9,17},{17,9},{25,1},{2,26},{10... | collective-permute-start | bytes 196616 | tf_op jit(solution)/shard_map/ppermute | solution.py:34
  59.6 4.0 %collective-permute-done.13 = bf16[16,2048]{1,0:T(8,128)(2,1)S(1)} collective-permute-done((bf16[16,2048]{1,0:T(8,128)(2,1)S(1)}, bf16[16,2048]{1,0:T(8,128)(2,1)S(1)}, u32[]{:S(2)}, u32[]{:S(2)}) %collective-permute-start.13) | collective-permute-done | bytes 65568 | tf_op jit(solution)/shard_map/ppermute | solution.py:34
  63.5 1.7 %collective-permute-done.12 = bf16[16,2048]{1,0:T(8,128)(2,1)S(1)} collective-permute-done((bf16[16,2048]{1,0:T(8,128)(2,1)S(1)}, bf16[16,2048]{1,0:T(8,128)(2,1)S(1)}, u32[]{:S(2)}, u32[]{:S(2)}) %collective-permute-start.12) | collective-permute-done | bytes 65568 | tf_op jit(solution)/shard_map/ppermute | solution.py:34
  68.0 2.1 %collective-permute-start.16 = (bf16[64,2048]{1,0:T(8,128)(2,1)S(1)}, bf16[64,2048]{1,0:T(8,128)(2,1)S(1)}, u32[]{:S(2)}, u32[]{:S(2)}) collective-permute-start(bf16[64,2048]{1,0:T(8,128)(2,1)S(1)} %pad_maximum_fusion.1.refs_0_), channel_id=1, source_target_pairs={{0,6},{1,7},{2,4},{3,5},{4,2},{5,3},{6,0},{7,1},{8,14},{9,15},{10,... | collective-permute-start | bytes 786440 | tf_op jit(solution)/shard_map/ppermute | solution.py:29
  71.5 8.9 %shard_map.141 = (f32[16,128,128]{2,1,0:T(8,128)S(1)}, f32[16,128,128]{2,1,0:T(8,128)S(1)}, bf16[512,256]{1,0:T(8,128)(2,1)S(1)}, f32[2,128,1]{2,1,0:T(8,128)S(1)}, bf16[8,128,4096]{2,1,0:T(8,128)(2,1)S(1)}) custom-call(bf16[64,2176]{1,0:T(8,128)(2,1)S(1)} %pad_maximum_fusion.refs_0_, bf16[64,2176]{1,0:T(8,128)(2,1)S(1)} %collective-permute-done.20.refs_1_, ...), custom_call_target="tpu_custom_call" | custom-call | flops 2684354560 | bytes 27262976 | tf_op jit(solution)/shard_map/pallas_call | solution.py:353
  80.5 2.0 %collective-permute-done.15.refs_2_ = bf16[64,2048]{1,0:T(8,128)(2,1)S(1)} collective-permute-done((bf16[64,2048]{1,0:T(8,128)(2,1)S(1)}, bf16[64,2048]{1,0:T(8,128)(2,1)S(1)}, u32[]{:S(2)}, u32[]{:S(2)}) %collective-permute-start.15) | collective-permute-done | bytes 262176 | tf_op jit(solution)/shard_map/ppermute | solution.py:29
  85.9 12.6 %shard_map.142 = (bf16[256,2048]{1,0:T(8,128)(2,1)S(1)}, bf16[256,2048]{1,0:T(8,128)(2,1)S(1)}, bf16[256,2048]{1,0:T(8,128)(2,1)S(1)}, bf16[256,2048]{1,0:T(8,128)(2,1)S(1)}) custom-call(bf16[64,2048]{1,0:T(8,128)(2,1)S(1)} %pad_maximum_fusion.1.refs_0_, bf16[64,2048]{1,0:T(8,128)(2,1)S(1)} %collective-permute-done.14.refs_1_, ...), custom_call_target="tpu_custom_call" | custom-call | flops 5905580032 | bytes 35651584 | tf_op jit(solution)/shard_map/pallas_call | solution.py:353
  98.7 2.5 %collective-permute-done.31 = bf16[256,2048]{1,0:T(8,128)(2,1)S(1)} collective-permute-done((bf16[256,2048]{1,0:T(8,128)(2,1)S(1)}, bf16[256,2048]{1,0:T(8,128)(2,1)S(1)}, u32[]{:S(2)}, u32[]{:S(2)}) %collective-permute-start.31) | collective-permute-done | bytes 1048608 | tf_op jit(solution)/shard_map/ppermute | solution.py:29
  102.3 2.3 %collective-permute-start.34 = (bf16[64,2048]{1,0:T(8,128)(2,1)S(1)}, bf16[64,2048]{1,0:T(8,128)(2,1)S(1)}, u32[]{:S(2)}, u32[]{:S(2)}) collective-permute-start(bf16[64,2048]{1,0:T(8,128)(2,1)S(1)} %get-tuple-element.45), channel_id=1, source_target_pairs={{0,6},{1,7},{2,4},{3,5},{4,2},{5,3},{6,0},{7,1},{8,14},{9,15},{10,... | collective-permute-start | bytes 786440 | tf_op jit(solution)/shard_map/ppermute | solution.py:29
  105.2 10.7 %collective-permute-done.32 = bf16[64,2048]{1,0:T(8,128)(2,1)S(1)} collective-permute-done((bf16[64,2048]{1,0:T(8,128)(2,1)S(1)}, bf16[64,2048]{1,0:T(8,128)(2,1)S(1)}, u32[]{:S(2)}, u32[]{:S(2)}) %collective-permute-start.32) | collective-permute-done | bytes 262176 | tf_op jit(solution)/shard_map/ppermute | solution.py:29
  118.2 2.3 %collective-permute-start.41 = (bf16[64,2048]{1,0:T(8,128)(2,1)S(1)}, bf16[64,2048]{1,0:T(8,128)(2,1)S(1)}, u32[]{:S(2)}, u32[]{:S(2)}) collective-permute-start(bf16[64,2048]{1,0:T(8,128)(2,1)S(1)} %get-tuple-element.48), channel_id=1, source_target_pairs={{0,6},{1,7},{2,4},{3,5},{4,2},{5,3},{6,0},{7,1},{8,14},{9,15},{10,... | collective-permute-start | bytes 786440 | tf_op jit(solution)/shard_map/ppermute | solution.py:29
  121.2 2.5 %collective-permute-start.37 = (bf16[16,2048]{1,0:T(8,128)(2,1)S(1)}, bf16[16,2048]{1,0:T(8,128)(2,1)S(1)}, u32[]{:S(2)}, u32[]{:S(2)}) collective-permute-start(bf16[16,2048]{1,0:T(8,128)(2,1)S(1)} %get-tuple-element.56), channel_id=1, source_target_pairs={{0,24},{8,16},{16,8},{24,0},{1,25},{9,17},{17,9},{25,1},{2,26},{10... | collective-permute-start | bytes 196616 | tf_op jit(solution)/shard_map/ppermute | solution.py:34
  123.7 7.0 %collective-permute-done.39 = bf16[64,2048]{1,0:T(8,128)(2,1)S(1)} collective-permute-done((bf16[64,2048]{1,0:T(8,128)(2,1)S(1)}, bf16[64,2048]{1,0:T(8,128)(2,1)S(1)}, u32[]{:S(2)}, u32[]{:S(2)}) %collective-permute-start.39) | collective-permute-done | bytes 262176 | tf_op jit(solution)/shard_map/ppermute | solution.py:29
  132.2 3.2 %collective-permute-start.44 = (bf16[16,2048]{1,0:T(8,128)(2,1)S(1)}, bf16[16,2048]{1,0:T(8,128)(2,1)S(1)}, u32[]{:S(2)}, u32[]{:S(2)}) collective-permute-start(bf16[16,2048]{1,0:T(8,128)(2,1)S(1)} %get-tuple-element.59), channel_id=1, source_target_pairs={{0,24},{8,16},{16,8},{24,0},{1,25},{9,17},{17,9},{25,1},{2,26},{10... | collective-permute-start | bytes 196616 | tf_op jit(solution)/shard_map/ppermute | solution.py:34
  135.7 3.9 %collective-permute-done.36 = bf16[16,2048]{1,0:T(8,128)(2,1)S(1)} collective-permute-done((bf16[16,2048]{1,0:T(8,128)(2,1)S(1)}, bf16[16,2048]{1,0:T(8,128)(2,1)S(1)}, u32[]{:S(2)}, u32[]{:S(2)}) %collective-permute-start.36) | collective-permute-done | bytes 65568 | tf_op jit(solution)/shard_map/ppermute | solution.py:34
  139.6 1.6 %collective-permute-done.43 = bf16[16,2048]{1,0:T(8,128)(2,1)S(1)} collective-permute-done((bf16[16,2048]{1,0:T(8,128)(2,1)S(1)}, bf16[16,2048]{1,0:T(8,128)(2,1)S(1)}, u32[]{:S(2)}, u32[]{:S(2)}) %collective-permute-start.43) | collective-permute-done | bytes 65568 | tf_op jit(solution)/shard_map/ppermute | solution.py:34
  (108 shorter events, 28.1 us)
Async XLA Ops:
  2.2 20.8 %collective-permute-start.3 = (bf16[512,256]{1,0:T(8,128)(2,1)S(1)}, bf16[512,256]{1,0:T(8,128)(2,1)S(1)}, u32[]{:S(2)}, u32[]{:S(2)}) collective-permute-start(bf16[512,256]{1,0:T(8,128)(2,1)S(1)} %bitcast.53), channel_id=1, source_target_pairs={{0,1},{1,0},{2,3},{3,2},{4,5},{5,4},{6,7},{7,6},{8,9},{9,8},{10,11... | collective-permute-start | bytes 786440 | tf_op jit(solution)/shard_map/ppermute | solution.py:29
  2.7 13.0 %collective-permute-start.1 = (bf16[512,256]{1,0:T(8,128)(2,1)S(1)}, bf16[512,256]{1,0:T(8,128)(2,1)S(1)}, u32[]{:S(2)}, u32[]{:S(2)}) collective-permute-start(bf16[512,256]{1,0:T(8,128)(2,1)S(1)} %bitcast.54), channel_id=1, source_target_pairs={{0,2},{1,3},{2,0},{3,1},{4,6},{5,7},{6,4},{7,5},{8,10},{9,11},{10,... | collective-permute-start | bytes 786440 | tf_op jit(solution)/shard_map/ppermute | solution.py:29
  5.3 14.2 %collective-permute-start.2 = (bf16[512,256]{1,0:T(8,128)(2,1)S(1)}, bf16[512,256]{1,0:T(8,128)(2,1)S(1)}, u32[]{:S(2)}, u32[]{:S(2)}) collective-permute-start(bf16[512,256]{1,0:T(8,128)(2,1)S(1)} %bitcast.62), channel_id=1, source_target_pairs={{0,6},{1,7},{2,4},{3,5},{4,2},{5,3},{6,0},{7,1},{8,14},{9,15},{10,... | collective-permute-start | bytes 786440 | tf_op jit(solution)/shard_map/ppermute | solution.py:29
  6.9 15.3 %collective-permute-start = (bf16[512,256]{1,0:T(8,128)(2,1)S(1)}, bf16[512,256]{1,0:T(8,128)(2,1)S(1)}, u32[]{:S(2)}, u32[]{:S(2)}) collective-permute-start(bf16[512,256]{1,0:T(8,128)(2,1)S(1)} %bitcast.63), channel_id=1, source_target_pairs={{0,4},{1,5},{2,6},{3,7},{4,0},{5,1},{6,2},{7,3},{8,12},{9,13},{10,... | collective-permute-start | bytes 786440 | tf_op jit(solution)/shard_map/ppermute | solution.py:29
  9.5 13.5 %all-to-all-start = ((bf16[8,16,768]{2,1,0:T(8,128)(2,1)}), bf16[8,16,768]{2,1,0:T(8,128)(2,1)S(1)}, u32[]{:S(2)}, u32[]{:S(2)}) async-start(bf16[8,16,768]{2,1,0:T(8,128)(2,1)} %pad_maximum_fusion.2), calls=%async_computation | async-start | bytes 393216 | tf_op jit(solution)/shard_map/all_to_all | solution.py:417
  15.7 7.3 %collective-permute-start.5 = (bf16[512,256]{1,0:T(8,128)(2,1)S(1)}, bf16[512,256]{1,0:T(8,128)(2,1)S(1)}, u32[]{:S(2)}, u32[]{:S(2)}) collective-permute-start(bf16[512,256]{1,0:T(8,128)(2,1)S(1)} %collective-permute-done.1.refs_2_), channel_id=1, source_target_pairs={{0,1},{1,0},{2,3},{3,2},{4,5},{5,4},{6,7},{7,6},{8,9},{9,8},{10,11... | collective-permute-start | bytes 786440 | tf_op jit(solution)/shard_map/ppermute | solution.py:29
  32.8 8.4 %collective-permute-start.8 = (bf16[16,4096]{1,0:T(8,128)(2,1)S(1)}, bf16[16,4096]{1,0:T(8,128)(2,1)S(1)}, u32[]{:S(2)}, u32[]{:S(2)}) collective-permute-start(bf16[16,4096]{1,0:T(8,128)(2,1)S(1)} %get-tuple-element.50), channel_id=1, source_target_pairs={{0,4},{1,5},{2,6},{3,7},{4,0},{5,1},{6,2},{7,3},{8,12},{9,13},{10,... | collective-permute-start | bytes 393224 | tf_op jit(solution)/shard_map/ppermute | solution.py:29
  33.3 8.0 %collective-permute-start.10 = (bf16[16,4096]{1,0:T(8,128)(2,1)S(1)}, bf16[16,4096]{1,0:T(8,128)(2,1)S(1)}, u32[]{:S(2)}, u32[]{:S(2)}) collective-permute-start(bf16[16,4096]{1,0:T(8,128)(2,1)S(1)} %get-tuple-element.51), channel_id=1, source_target_pairs={{0,6},{1,7},{2,4},{3,5},{4,2},{5,3},{6,0},{7,1},{8,14},{9,15},{10,... | collective-permute-start | bytes 393224 | tf_op jit(solution)/shard_map/ppermute | solution.py:29
  35.8 6.6 %collective-permute-start.9 = (bf16[16,4096]{1,0:T(8,128)(2,1)S(1)}, bf16[16,4096]{1,0:T(8,128)(2,1)S(1)}, u32[]{:S(2)}, u32[]{:S(2)}) collective-permute-start(bf16[16,4096]{1,0:T(8,128)(2,1)S(1)} %get-tuple-element.52), channel_id=1, source_target_pairs={{0,2},{1,3},{2,0},{3,1},{4,6},{5,7},{6,4},{7,5},{8,10},{9,11},{10,... | collective-permute-start | bytes 393224 | tf_op jit(solution)/shard_map/ppermute | solution.py:29
  44.4 6.5 %collective-permute-start.19 = (bf16[16,2176]{1,0:T(8,128)(2,1)S(1)}, bf16[16,2176]{1,0:T(8,128)(2,1)S(1)}, u32[]{:S(2)}, u32[]{:S(2)}) collective-permute-start(bf16[16,2176]{1,0:T(8,128)(2,1)S(1)} %pad_maximum_fusion.3), channel_id=1, source_target_pairs={{0,24},{8,16},{16,8},{24,0},{1,25},{9,17},{17,9},{25,1},{2,26},{10... | collective-permute-start | bytes 208904 | tf_op jit(solution)/shard_map/ppermute | solution.py:34
  48.1 5.5 %collective-permute-start.18 = (bf16[16,2176]{1,0:T(8,128)(2,1)S(1)}, bf16[16,2176]{1,0:T(8,128)(2,1)S(1)}, u32[]{:S(2)}, u32[]{:S(2)}) collective-permute-start(bf16[16,2176]{1,0:T(8,128)(2,1)S(1)} %pad_maximum_fusion.3), channel_id=1, source_target_pairs={{0,16},{8,24},{16,0},{24,8},{1,17},{9,25},{17,1},{25,9},{2,18},{10... | collective-permute-start | bytes 208904 | tf_op jit(solution)/shard_map/ppermute | solution.py:34
  53.6 11.6 %collective-permute-start.22 = (bf16[64,2176]{1,0:T(8,128)(2,1)S(1)}, bf16[64,2176]{1,0:T(8,128)(2,1)S(1)}, u32[]{:S(2)}, u32[]{:S(2)}) collective-permute-start(bf16[64,2176]{1,0:T(8,128)(2,1)S(1)} %pad_maximum_fusion.refs_0_), channel_id=1, source_target_pairs={{0,6},{1,7},{2,4},{3,5},{4,2},{5,3},{6,0},{7,1},{8,14},{9,15},{10,... | collective-permute-start | bytes 835592 | tf_op jit(solution)/shard_map/ppermute | solution.py:29
  55.1 11.9 %collective-permute-start.21 = (bf16[64,2176]{1,0:T(8,128)(2,1)S(1)}, bf16[64,2176]{1,0:T(8,128)(2,1)S(1)}, u32[]{:S(2)}, u32[]{:S(2)}) collective-permute-start(bf16[64,2176]{1,0:T(8,128)(2,1)S(1)} %pad_maximum_fusion.refs_0_), channel_id=1, source_target_pairs={{0,2},{1,3},{2,0},{3,1},{4,6},{5,7},{6,4},{7,5},{8,10},{9,11},{10,... | collective-permute-start | bytes 835592 | tf_op jit(solution)/shard_map/ppermute | solution.py:29
  55.6 12.3 %collective-permute-start.20 = (bf16[64,2176]{1,0:T(8,128)(2,1)S(1)}, bf16[64,2176]{1,0:T(8,128)(2,1)S(1)}, u32[]{:S(2)}, u32[]{:S(2)}) collective-permute-start(bf16[64,2176]{1,0:T(8,128)(2,1)S(1)} %pad_maximum_fusion.refs_0_), channel_id=1, source_target_pairs={{0,4},{1,5},{2,6},{3,7},{4,0},{5,1},{6,2},{7,3},{8,12},{9,13},{10,... | collective-permute-start | bytes 835592 | tf_op jit(solution)/shard_map/ppermute | solution.py:29
  57.2 6.4 %collective-permute-start.13 = (bf16[16,2048]{1,0:T(8,128)(2,1)S(1)}, bf16[16,2048]{1,0:T(8,128)(2,1)S(1)}, u32[]{:S(2)}, u32[]{:S(2)}) collective-permute-start(bf16[16,2048]{1,0:T(8,128)(2,1)S(1)} %get-tuple-element.62), channel_id=1, source_target_pairs={{0,24},{8,16},{16,8},{24,0},{1,25},{9,17},{17,9},{25,1},{2,26},{10... | collective-permute-start | bytes 196616 | tf_op jit(solution)/shard_map/ppermute | solution.py:34
  59.6 5.6 %collective-permute-start.12 = (bf16[16,2048]{1,0:T(8,128)(2,1)S(1)}, bf16[16,2048]{1,0:T(8,128)(2,1)S(1)}, u32[]{:S(2)}, u32[]{:S(2)}) collective-permute-start(bf16[16,2048]{1,0:T(8,128)(2,1)S(1)} %get-tuple-element.62), channel_id=1, source_target_pairs={{0,16},{8,24},{16,0},{24,8},{1,17},{9,25},{17,1},{25,9},{2,18},{10... | collective-permute-start | bytes 196616 | tf_op jit(solution)/shard_map/ppermute | solution.py:34
  68.0 12.5 %collective-permute-start.16 = (bf16[64,2048]{1,0:T(8,128)(2,1)S(1)}, bf16[64,2048]{1,0:T(8,128)(2,1)S(1)}, u32[]{:S(2)}, u32[]{:S(2)}) collective-permute-start(bf16[64,2048]{1,0:T(8,128)(2,1)S(1)} %pad_maximum_fusion.1.refs_0_), channel_id=1, source_target_pairs={{0,6},{1,7},{2,4},{3,5},{4,2},{5,3},{6,0},{7,1},{8,14},{9,15},{10,... | collective-permute-start | bytes 786440 | tf_op jit(solution)/shard_map/ppermute | solution.py:29
  70.0 12.4 %collective-permute-start.15 = (bf16[64,2048]{1,0:T(8,128)(2,1)S(1)}, bf16[64,2048]{1,0:T(8,128)(2,1)S(1)}, u32[]{:S(2)}, u32[]{:S(2)}) collective-permute-start(bf16[64,2048]{1,0:T(8,128)(2,1)S(1)} %pad_maximum_fusion.1.refs_0_), channel_id=1, source_target_pairs={{0,2},{1,3},{2,0},{3,1},{4,6},{5,7},{6,4},{7,5},{8,10},{9,11},{10,... | collective-permute-start | bytes 786440 | tf_op jit(solution)/shard_map/ppermute | solution.py:29
  70.6 12.6 %collective-permute-start.14 = (bf16[64,2048]{1,0:T(8,128)(2,1)S(1)}, bf16[64,2048]{1,0:T(8,128)(2,1)S(1)}, u32[]{:S(2)}, u32[]{:S(2)}) collective-permute-start(bf16[64,2048]{1,0:T(8,128)(2,1)S(1)} %pad_maximum_fusion.1.refs_0_), channel_id=1, source_target_pairs={{0,4},{1,5},{2,6},{3,7},{4,0},{5,1},{6,2},{7,3},{8,12},{9,13},{10,... | collective-permute-start | bytes 786440 | tf_op jit(solution)/shard_map/ppermute | solution.py:29
  101.2 16.1 %collective-permute-start.38 = (bf16[256,2048]{1,0:T(8,128)(2,1)S(1)}, bf16[256,2048]{1,0:T(8,128)(2,1)S(1)}, u32[]{:S(2)}, u32[]{:S(2)}) collective-permute-start(bf16[256,2048]{1,0:T(8,128)(2,1)S(1)} %get-tuple-element.37), channel_id=1, source_target_pairs={{0,1},{1,0},{2,3},{3,2},{4,5},{5,4},{6,7},{7,6},{8,9},{9,8},{10,11... | collective-permute-start | bytes 3145736 | tf_op jit(solution)/shard_map/ppermute | solution.py:29
  101.6 14.3 %collective-permute-start.32 = (bf16[64,2048]{1,0:T(8,128)(2,1)S(1)}, bf16[64,2048]{1,0:T(8,128)(2,1)S(1)}, u32[]{:S(2)}, u32[]{:S(2)}) collective-permute-start(bf16[64,2048]{1,0:T(8,128)(2,1)S(1)} %get-tuple-element.44), channel_id=1, source_target_pairs={{0,4},{1,5},{2,6},{3,7},{4,0},{5,1},{6,2},{7,3},{8,12},{9,13},{10,... | collective-permute-start | bytes 786440 | tf_op jit(solution)/shard_map/ppermute | solution.py:29
  102.3 13.6 %collective-permute-start.34 = (bf16[64,2048]{1,0:T(8,128)(2,1)S(1)}, bf16[64,2048]{1,0:T(8,128)(2,1)S(1)}, u32[]{:S(2)}, u32[]{:S(2)}) collective-permute-start(bf16[64,2048]{1,0:T(8,128)(2,1)S(1)} %get-tuple-element.45), channel_id=1, source_target_pairs={{0,6},{1,7},{2,4},{3,5},{4,2},{5,3},{6,0},{7,1},{8,14},{9,15},{10,... | collective-permute-start | bytes 786440 | tf_op jit(solution)/shard_map/ppermute | solution.py:29
  104.6 12.5 %collective-permute-start.33 = (bf16[64,2048]{1,0:T(8,128)(2,1)S(1)}, bf16[64,2048]{1,0:T(8,128)(2,1)S(1)}, u32[]{:S(2)}, u32[]{:S(2)}) collective-permute-start(bf16[64,2048]{1,0:T(8,128)(2,1)S(1)} %get-tuple-element.46), channel_id=1, source_target_pairs={{0,2},{1,3},{2,0},{3,1},{4,6},{5,7},{6,4},{7,5},{8,10},{9,11},{10,... | collective-permute-start | bytes 786440 | tf_op jit(solution)/shard_map/ppermute | solution.py:29
  117.5 13.1 %collective-permute-start.39 = (bf16[64,2048]{1,0:T(8,128)(2,1)S(1)}, bf16[64,2048]{1,0:T(8,128)(2,1)S(1)}, u32[]{:S(2)}, u32[]{:S(2)}) collective-permute-start(bf16[64,2048]{1,0:T(8,128)(2,1)S(1)} %get-tuple-element.47), channel_id=1, source_target_pairs={{0,4},{1,5},{2,6},{3,7},{4,0},{5,1},{6,2},{7,3},{8,12},{9,13},{10,... | collective-permute-start | bytes 786440 | tf_op jit(solution)/shard_map/ppermute | solution.py:29
  118.2 13.5 %collective-permute-start.41 = (bf16[64,2048]{1,0:T(8,128)(2,1)S(1)}, bf16[64,2048]{1,0:T(8,128)(2,1)S(1)}, u32[]{:S(2)}, u32[]{:S(2)}) collective-permute-start(bf16[64,2048]{1,0:T(8,128)(2,1)S(1)} %get-tuple-element.48), channel_id=1, source_target_pairs={{0,6},{1,7},{2,4},{3,5},{4,2},{5,3},{6,0},{7,1},{8,14},{9,15},{10,... | collective-permute-start | bytes 786440 | tf_op jit(solution)/shard_map/ppermute | solution.py:29
  120.5 11.4 %collective-permute-start.40 = (bf16[64,2048]{1,0:T(8,128)(2,1)S(1)}, bf16[64,2048]{1,0:T(8,128)(2,1)S(1)}, u32[]{:S(2)}, u32[]{:S(2)}) collective-permute-start(bf16[64,2048]{1,0:T(8,128)(2,1)S(1)} %get-tuple-element.49), channel_id=1, source_target_pairs={{0,2},{1,3},{2,0},{3,1},{4,6},{5,7},{6,4},{7,5},{8,10},{9,11},{10,... | collective-permute-start | bytes 786440 | tf_op jit(solution)/shard_map/ppermute | solution.py:29
  121.1 14.2 %collective-permute-start.35 = (bf16[16,2048]{1,0:T(8,128)(2,1)S(1)}, bf16[16,2048]{1,0:T(8,128)(2,1)S(1)}, u32[]{:S(2)}, u32[]{:S(2)}) collective-permute-start(bf16[16,2048]{1,0:T(8,128)(2,1)S(1)} %get-tuple-element.55), channel_id=1, source_target_pairs={{0,8},{8,0},{16,24},{24,16},{1,9},{9,1},{17,25},{25,17},{2,10},{10... | collective-permute-start | bytes 196616 | tf_op jit(solution)/shard_map/ppermute | solution.py:34
  121.2 14.5 %collective-permute-start.37 = (bf16[16,2048]{1,0:T(8,128)(2,1)S(1)}, bf16[16,2048]{1,0:T(8,128)(2,1)S(1)}, u32[]{:S(2)}, u32[]{:S(2)}) collective-permute-start(bf16[16,2048]{1,0:T(8,128)(2,1)S(1)} %get-tuple-element.56), channel_id=1, source_target_pairs={{0,24},{8,16},{16,8},{24,0},{1,25},{9,17},{17,9},{25,1},{2,26},{10... | collective-permute-start | bytes 196616 | tf_op jit(solution)/shard_map/ppermute | solution.py:34
  130.7 8.9 %collective-permute-start.36 = (bf16[16,2048]{1,0:T(8,128)(2,1)S(1)}, bf16[16,2048]{1,0:T(8,128)(2,1)S(1)}, u32[]{:S(2)}, u32[]{:S(2)}) collective-permute-start(bf16[16,2048]{1,0:T(8,128)(2,1)S(1)} %get-tuple-element.57), channel_id=1, source_target_pairs={{0,16},{8,24},{16,0},{24,8},{1,17},{9,25},{17,1},{25,9},{2,18},{10... | collective-permute-start | bytes 196616 | tf_op jit(solution)/shard_map/ppermute | solution.py:34
  132.1 7.5 %collective-permute-start.42 = (bf16[16,2048]{1,0:T(8,128)(2,1)S(1)}, bf16[16,2048]{1,0:T(8,128)(2,1)S(1)}, u32[]{:S(2)}, u32[]{:S(2)}) collective-permute-start(bf16[16,2048]{1,0:T(8,128)(2,1)S(1)} %get-tuple-element.58), channel_id=1, source_target_pairs={{0,8},{8,0},{16,24},{24,16},{1,9},{9,1},{17,25},{25,17},{2,10},{10... | collective-permute-start | bytes 196616 | tf_op jit(solution)/shard_map/ppermute | solution.py:34
  132.2 7.4 %collective-permute-start.44 = (bf16[16,2048]{1,0:T(8,128)(2,1)S(1)}, bf16[16,2048]{1,0:T(8,128)(2,1)S(1)}, u32[]{:S(2)}, u32[]{:S(2)}) collective-permute-start(bf16[16,2048]{1,0:T(8,128)(2,1)S(1)} %get-tuple-element.59), channel_id=1, source_target_pairs={{0,24},{8,16},{16,8},{24,0},{1,25},{9,17},{17,9},{25,1},{2,26},{10... | collective-permute-start | bytes 196616 | tf_op jit(solution)/shard_map/ppermute | solution.py:34
  135.3 5.9 %collective-permute-start.43 = (bf16[16,2048]{1,0:T(8,128)(2,1)S(1)}, bf16[16,2048]{1,0:T(8,128)(2,1)S(1)}, u32[]{:S(2)}, u32[]{:S(2)}) collective-permute-start(bf16[16,2048]{1,0:T(8,128)(2,1)S(1)} %get-tuple-element.60), channel_id=1, source_target_pairs={{0,16},{8,24},{16,0},{24,8},{1,17},{9,25},{17,1},{25,9},{2,18},{10... | collective-permute-start | bytes 196616 | tf_op jit(solution)/shard_map/ppermute | solution.py:34
  (14 other events, 45.3 us)

commit v3 on v2

--- a/solution.py
+++ b/solution.py
@@ -18,7 +18,8 @@
 NEG = -1e30
 EPS = 1e-06
 RISE_LIMIT = 34 * 1024 * 1024
-FALL_LIMIT = 37 * 1024 * 1024
+FALL_LIMIT = 33 * 1024 * 1024
+LAST_LIMIT = 30 * 1024 * 1024
 ATTEND_LIMIT = 48 * 1024 * 1024
 READY = 8
 LOG2E = 1.4426950408889634
@@ -52,6 +53,11 @@
     return reach
 
 
+def weigh(weights, values):
+    values = jnp.concatenate([values, jnp.ones_like(values)], axis=1)
+    return jnp.dot(weights.astype(jnp.bfloat16), values, preferred_element_type=jnp.float32)
+
+
 def attend_kernel(parts, mine, valid_ref, perm_ref, packed_ref, mask_ref, *refs):
     kv_refs = refs[:parts]
     w_any, keep_ref, send_ref, w_ref, sem = refs[parts:]
@@ -74,27 +80,16 @@
     linked = jnp.concatenate([mask] * mine, axis=0) > 0.5
     s = jnp.where(linked, scores(packed_ref[:, lanes : lanes + DH]), NEG)
     top = jnp.max(s, axis=-1, keepdims=True)
-    weights = jnp.exp2(s - top)
-    total = jnp.sum(weights, axis=-1, keepdims=True)
-    out = jnp.dot(
-        weights.astype(jnp.bfloat16),
-        packed_ref[:, lanes + DH :],
-        preferred_element_type=jnp.float32,
-    )
+    out = weigh(jnp.exp2(s - top), packed_ref[:, lanes + DH :])
     for part in range(parts):
         kv = kv_refs[part]
         place = lax.broadcasted_iota(jnp.int32, (1, kv.shape[0]), 1)
         bias = jnp.where(place < valid_ref[part], 0.0, NEG)
         s = scores(kv[:, :DH]) + bias
         peak = jnp.maximum(top, jnp.max(s, axis=-1, keepdims=True))
-        weights = jnp.exp2(s - peak)
-        fade = jnp.exp2(top - peak)
-        total = total * fade + jnp.sum(weights, axis=-1, keepdims=True)
-        out = out * fade + jnp.dot(
-            weights.astype(jnp.bfloat16), kv[:, DH:], preferred_element_type=jnp.float32
-        )
+        out = out * jnp.exp2(top - peak) + weigh(jnp.exp2(s - peak), kv[:, DH:])
         top = peak
-    attention = (out / total).astype(jnp.bfloat16)
+    attention = (out[:, :DH] / out[:, DH:]).astype(jnp.bfloat16)
     attention = jnp.concatenate(
         [attention[a * rows : (a + 1) * rows] for a in range(mine)], axis=1
     )
@@ -189,7 +184,8 @@
         gate_ref, up_ref, back_ref, rate_ref, ready_ref = take(5)
     else:
         gate_in, up_in, back_ref, rate_ref, ready_ref, wd_any = take(6)
-        outs = take(4)
+        outs = take(3)
+        hidden = outs[2]
     rows, picked, wg, wu, part_sem, gate_sem, up_sem = take(7)
     held, cut, wide = wg.shape
     per_expert = held // experts
@@ -220,13 +216,15 @@
         for move in early:
             move.start()
     else:
-        wd, hidden, flat, down_sem = take(4)
+        wd, flat, down_sem = take(3)
 
         ready = ready_ref.shape[0]
 
         def down_move(p):
             place = pl.ds((p - ready) * wide, wide)
-            return pltpu.make_async_copy(wd_any.at[p], wd.at[place], down_sem.at[p - ready])
+            return pltpu.make_async_copy(
+                wd_any.at[p, :, pl.ds(0, cut)], wd.at[place], down_sem.at[p - ready]
+            )
 
         for p in range(ready, held):
             down_move(p).start()
@@ -272,19 +270,29 @@
         for move in early:
             move.wait()
         return
-    deep = per_expert * wide
-    depth = flat.shape[1]
+    for p in range(ready, held):
+        down_move(p).wait()
+    drop_columns(hidden, ready_ref, wd, back_ref, flat, *outs[:2])
+
+
+def drop_columns(hidden, ready_ref, wd, back_ref, flat, keep_ref, send_ref, first=0):
+    cut = flat.shape[1]
+    lines = hidden.shape[0]
+    ready, wide, _ = ready_ref.shape
+    per_expert = hidden.shape[1] // wide
+    rest = 0 if wd is None else wd.shape[0] // wide
+    experts = (ready + rest) // per_expert
+    seats = lines // experts
+    tile = 512 if cut % 512 == 0 else cut
     for e in range(experts):
         low, high = e * per_expert, (e + 1) * per_expert
-        for p in range(max(low, ready), high):
-            down_move(p).wait()
         split = min(max(ready, low), high)
-        for c in range(0, depth, tile):
+        for c in range(0, cut, tile):
             total = None
             if split > low:
                 total = jnp.dot(
                     hidden[e * seats : (e + 1) * seats, : (split - low) * wide],
-                    ready_ref[low:split, :, c : c + tile].reshape(-1, tile),
+                    ready_ref[low:split, :, first + c : first + c + tile].reshape(-1, tile),
                     preferred_element_type=jnp.float32,
                 )
             if split < high:
@@ -295,15 +303,56 @@
                 )
                 total = rest if total is None else total + rest
             flat[e * seats : (e + 1) * seats, c : c + tile] = total.astype(jnp.bfloat16)
-    for c in range(0, depth, tile):
+    half = keep_ref.shape[0]
+    for c in range(0, cut, tile):
         moved = jnp.dot(
             back_ref[...], flat[:, c : c + tile], preferred_element_type=jnp.float32
         ).astype(jnp.bfloat16)
-        half = moved.shape[0] // 2
-        keep_ref, send_ref = outs[2 * (c // cut)], outs[2 * (c // cut) + 1]
-        at = c % cut
-        keep_ref[:, at : at + tile] = moved[:half]
-        send_ref[:, at : at + tile] = moved[half:]
+        keep_ref[:, c : c + tile] = moved[:half]
+        send_ref[:, c : c + tile] = moved[half:]
+
+
+def fall_kernel(hidden_ref, ready_ref, back_ref, wd_any, keep_ref, send_ref, flat, *refs):
+    ready, wide, depth = ready_ref.shape
+    cut = flat.shape[1]
+    wd = None
+    if refs:
+        wd, sem = refs
+        moves = [
+            pltpu.make_async_copy(
+                wd_any.at[p, :, pl.ds(cut, cut)], wd.at[pl.ds((p - ready) * wide, wide)], sem.at[p - ready]
+            )
+            for p in range(ready, wd_any.shape[0])
+        ]
+        for move in moves:
+            move.start()
+        for move in moves:
+            move.wait()
+    drop_columns(hidden_ref, ready_ref, wd, back_ref, flat, keep_ref, send_ref, first=cut)
+
+
+def fall_call(hidden, ready, back, w_down):
+    held, wide, depth = w_down.shape
+    rest = held - ready.shape[0]
+    cut = depth // 2
+    full = pl.BlockSpec(memory_space=pltpu.VMEM)
+    shape = jax.ShapeDtypeStruct((back.shape[0] // 2, cut), jnp.bfloat16)
+    scratch = [pltpu.VMEM((hidden.shape[0], cut), jnp.bfloat16)]
+    if rest:
+        scratch += [pltpu.VMEM((rest * wide, cut), jnp.bfloat16), pltpu.SemaphoreType.DMA((rest,))]
+    return pl.pallas_call(
+        fall_kernel,
+        out_shape=(shape, shape),
+        in_specs=[full, full, full, pl.BlockSpec(memory_space=pltpu.HBM)],
+        out_specs=(full, full),
+        scratch_shapes=scratch,
+        compiler_params=pltpu.CompilerParams(vmem_limit_bytes=LAST_LIMIT),
+        cost_estimate=pl.CostEstimate(
+            flops=2 * held * hidden.shape[0] * cut * wide + 2 * hidden.shape[0] * back.shape[0] * cut,
+            bytes_accessed=2 * rest * cut * wide,
+            transcendentals=0,
+        ),
+    )(hidden, ready, back, w_down)
 
 
 def expert_call(rows, w_gate, w_up, chunk, cut, topk, experts, seats, first=None, sums=None, w_down=None):
@@ -341,15 +390,15 @@
         ready = sums[4]
         args += [*sums, w_down]
         in_specs += [full] * 5 + [far]
-        outs = [jax.ShapeDtypeStruct((count // 2, cut), jnp.bfloat16)] * 4
+        outs = [jax.ShapeDtypeStruct((count // 2, cut), jnp.bfloat16)] * 2
+        outs += [jax.ShapeDtypeStruct((experts * seats, deep), jnp.bfloat16)]
         scratch += [
-            pltpu.VMEM((max(1, held - ready.shape[0]) * wide, depth), jnp.bfloat16),
-            pltpu.VMEM((experts * seats, deep), jnp.bfloat16),
-            pltpu.VMEM((experts * seats, depth), jnp.bfloat16),
+            pltpu.VMEM(((held - ready.shape[0]) * wide or 8, cut), jnp.bfloat16),
+            pltpu.VMEM((experts * seats, cut), jnp.bfloat16),
             pltpu.SemaphoreType.DMA((max(1, held - ready.shape[0]),)),
         ]
-        flops += 2 * held * seats * depth * wide + 2 * experts * seats * count * depth
-        moved += 2 * held * depth * wide
+        flops += 2 * held * seats * cut * wide + 2 * experts * seats * count * cut
+        moved += held * depth * wide
     return pl.pallas_call(
         functools.partial(expert_kernel, len(rows), experts, seats, topk, chunk),
         out_shape=tuple(outs),
@@ -357,7 +406,9 @@
         out_specs=tuple([full] * len(outs)),
         scratch_shapes=scratch,
         compiler_params=pltpu.CompilerParams(vmem_limit_bytes=RISE_LIMIT if chunk == 0 else FALL_LIMIT),
-        cost_estimate=pl.CostEstimate(flops=flops, bytes_accessed=moved, transcendentals=0),
+        cost_estimate=pl.CostEstimate(
+            flops=flops, bytes_accessed=moved, transcendentals=0
+        ),
     )(*args)
 
 
@@ -400,11 +451,11 @@
             pick = jnp.where(device // share == h, heads[h], pick)
         return pick
 
-    half = [head_of(here ^ mask) if mask == 0 else None for mask in near]
-    same = half[0]
-    other = head_of(here ^ (parts // 2))
-    half = [same] + [hop(other if mask & (parts // 2) else same, mask) for mask in near[1:]]
-    valid = context_lengths[0] - jnp.stack([(here ^ mask) * span for mask in order])
+    same, other = head_of(here), head_of(here ^ (parts // 2))
+    turns = [near[0]] + ([near[i] for i in (2, 3, 1)] if len(near) == 4 else near[1:])
+    order_kv = turns + [mask ^ 1 for mask in turns]
+    half = [same] + [hop(other if mask & (parts // 2) else same, mask) for mask in turns[1:]]
+    valid = context_lengths[0] - jnp.stack([(here ^ mask) * span for mask in order_kv])
 
     mine = HQ // parts
     tree_heads = [
@@ -453,32 +504,35 @@
     seats = groups * CAP
 
     cut = depth // 2
+    ring = [near[0]] + ([near[i] for i in (3, 1, 2)] if len(near) == 4 else near[1:])
     planes = []
     for chunk in range(2):
         piece = normed[:, chunk * cut : (chunk + 1) * cut]
         if chunk == 0:
             piece = jnp.concatenate([piece, table], axis=1)
         stack = jnp.concatenate([piece] + [turn(piece, d) for d in range(1, groups)], axis=0)
-        planes.append([stack] + [hop(stack, mask) for mask in near[1:]])
+        planes.append([stack] + [hop(stack, mask) for mask in ring[1:]])
     full = planes[0] + [hop(p, 1) for p in planes[0]]
     sums = expert_call(full, w_gate, w_up, 0, cut, topk, experts, seats, first=first, w_down=w_down)
     *plane, gate = lax.optimization_barrier((*planes[1], sums[0]))
     full = plane + [hop(p, 1) for p in plane]
-    keep0, send0, keep1, send1 = expert_call(
+    keep0, send0, hidden = expert_call(
         full, w_gate, w_up, 1, cut, topk, experts, seats, sums=(gate, *sums[1:]), w_down=w_down
     )
 
     size = groups * own
 
-    def home(keep, got):
-        pair = [
-            keep[i * size : (i + 1) * size].astype(jnp.float32)
+    def paired(keep, got):
+        return {
+            mask: keep[i * size : (i + 1) * size].astype(jnp.float32)
             + got[i * size : (i + 1) * size].astype(jnp.float32)
-            for i in range(len(near))
-        ]
-        flat = pair[0]
-        for i in range(1, len(near)):
-            flat = flat + hop(pair[i].astype(jnp.bfloat16), near[i]).astype(jnp.float32)
+            for i, mask in enumerate(ring)
+        }
+
+    def send(value, mask):
+        return hop(value.astype(jnp.bfloat16), mask).astype(jnp.float32)
+
+    def home(flat):
         result = flat[:own]
         for d in range(1, groups):
             result = result + turn(
@@ -487,8 +541,26 @@
         return result.astype(jnp.bfloat16)
 
     got0 = hop(send0, 1)
+    keep1, send1 = fall_call(hidden, sums[4], sums[2], w_down)
     send1, got0 = lax.optimization_barrier((send1, got0))
-    pieces = [home(keep0, got0), home(keep1, hop(send1, 1))]
+    got1 = hop(send1, 1)
+    low, high = paired(keep0, got0), paired(keep1, got1)
+    if len(near) == 4:
+        near_x, near_y = 2, 4
+        far = near_x ^ near_y
+        got_low, got_high = send(low[far], near_x), send(high[far], near_y)
+        go_x, go_y = low[near_x].astype(jnp.bfloat16), (low[near_y] + got_low).astype(jnp.bfloat16)
+        go_x, go_y, got_high = lax.optimization_barrier((go_x, go_y, got_high))
+        got_x, got_y = send(go_x, near_x), send(go_y, near_y)
+        flat_low = low[0] + got_x + got_y
+        go_x, go_y = (high[near_x] + got_high).astype(jnp.bfloat16), high[near_y].astype(jnp.bfloat16)
+        go_x, go_y, flat_low = lax.optimization_barrier((go_x, go_y, flat_low))
+        flat_high = high[0] + send(go_x, near_x) + send(go_y, near_y)
+    else:
+        flat_low, flat_high = (
+            sum([send(blocks[mask], mask) for mask in near[1:]], blocks[0]) for blocks in (low, high)
+        )
+    pieces = [home(flat_low), home(flat_high)]
     return (attended[None], jnp.concatenate(pieces, axis=1)[None])
 
 

time: 142 us -> 136 us (0.958)
  waiting for transfers between devices: 56.2 us -> 48.8 us
    ppermute x33, waiting for transfers between devices: 40.4 us -> 33.5 us  [hop(): return lax.ppermute(value, 'seq', [(i, i ^ mask) for i in range(count)])]
    pallas_call x0 -> x1, Pallas kernels: none -> 4.03 us  [fall_call(): pl.pallas_call(fall_kernel, out_shape=(shape, shape), in_specs=[full, ful...]
    pallas_call x2, Pallas kernels: 21.5 us -> 18.6 us  [expert_call(): pl.pallas_call(functools.partial(expert_kernel, len(rows), experts, seats...]
  transfers between devices with their start and end apart: 46 -> 46, of which waited for: 25 -> 30; matrix products, arithmetic and copies ran while one was open for 5% -> 6% of each run, Pallas kernels for 6% -> 10%
where the time goes in v3:
time: 136 us; the launch traced here: 135 us
  waiting for transfers between devices  48.8 us (36%)
  starting transfers between devices  43.9 us (32%)
  Pallas kernels  29.1 us (21%)
  other arithmetic  8.05 us (6%)
  local copies, waits for them, and re-layouts  2.21 us (2%)
  matrix products  1.85 us (1%)
  between operations  1.61 us (1%)
    ppermute x33, waiting for transfers between devices, hop(): return lax.ppermute(value, 'seq', [(i, i ^ mask) for i in range(count)])  33.5 us
    ppermute x33, starting transfers between devices, hop(): return lax.ppermute(value, 'seq', [(i, i ^ mask) for i in range(count)])  25.6 us
    pallas_call x2, Pallas kernels, expert_call(): pl.pallas_call(functools.partial(expert_kernel, len(rows), experts, seats...  18.6 us
    ppermute x12, waiting for transfers between devices, turn(): return lax.ppermute(value, 'req', [(i, i ^ step) for i in range(count)])  15.1 us
    ppermute x12, starting transfers between devices, turn(): return lax.ppermute(value, 'req', [(i, i ^ step) for i in range(count)])  14.1 us
    pallas_call x1, Pallas kernels, attend(): pl.pallas_call(functools.partial(attend_kernel, parts, mine), out_shape=(...  6.44 us
    all_to_all x1, starting transfers between devices, body(): lax.all_to_all(packed, 'seq', split_axis=0, concat_axis=0, tiled=True)  4.15 us
    pallas_call x1, Pallas kernels, fall_call(): pl.pallas_call(fall_kernel, out_shape=(shape, shape), in_specs=[full, ful...  4.03 us
  transfers between devices with their start and end apart: 46, of which 30 were waited for; matrix products, arithmetic and copies ran while one was open for 6% of the time, Pallas kernels for 10%

profile of v3, /device:TPU:0, one launch (start us, length us, event | category | flops | bytes accessed | tf_op | source)
XLA Modules:
  0.0 135.5 jit_solution(15581565963929167700)
XLA Ops:
  0.7 1.5 %broadcast_select_fusion = (bf16[512,2,128]{2,1,0:T(2,128)(2,1)S(1)}, bf16[512,2,128]{2,1,0:T(2,128)(2,1)S(1)}) fusion(pred[]{:T(512)S(6)} %eq.58, bf16[512,2,256]{2,1,0:T(2,128)(2,1)} %bitcast.59, pred[]{:T(512)S(6)} %eq.57), kind=kLoop, calls=%fused_computation.22 | loop fusion | flops 262144 | bytes 1048578 | tf_op jit(solution)/shard_map/jit(_where)/select_n | solution.py:451
  2.7 2.6 %collective-permute-start = (bf16[512,256]{1,0:T(8,128)(2,1)S(1)}, bf16[512,256]{1,0:T(8,128)(2,1)S(1)}, u32[]{:S(2)}, u32[]{:S(2)}) collective-permute-start(bf16[512,256]{1,0:T(8,128)(2,1)S(1)} %bitcast.54), channel_id=1, source_target_pairs={{0,2},{1,3},{2,0},{3,1},{4,6},{5,7},{6,4},{7,5},{8,10},{9,11},{10,... | collective-permute-start | bytes 786440 | tf_op jit(solution)/shard_map/ppermute | solution.py:30
  5.3 1.6 %collective-permute-start.2 = (bf16[512,256]{1,0:T(8,128)(2,1)S(1)}, bf16[512,256]{1,0:T(8,128)(2,1)S(1)}, u32[]{:S(2)}, u32[]{:S(2)}) collective-permute-start(bf16[512,256]{1,0:T(8,128)(2,1)S(1)} %bitcast.62), channel_id=1, source_target_pairs={{0,4},{1,5},{2,6},{3,7},{4,0},{5,1},{6,2},{7,3},{8,12},{9,13},{10,... | collective-permute-start | bytes 786440 | tf_op jit(solution)/shard_map/ppermute | solution.py:30
  9.4 4.2 %all-to-all-start = ((bf16[8,16,768]{2,1,0:T(8,128)(2,1)}), bf16[8,16,768]{2,1,0:T(8,128)(2,1)S(1)}, u32[]{:S(2)}, u32[]{:S(2)}) async-start(bf16[8,16,768]{2,1,0:T(8,128)(2,1)} %pad_maximum_fusion.2), calls=%async_computation | async-start | bytes 393216 | tf_op jit(solution)/shard_map/all_to_all | solution.py:468
  16.3 3.7 %collective-permute-done.2.refs_3_ = bf16[512,256]{1,0:T(8,128)(2,1)S(1)} collective-permute-done((bf16[512,256]{1,0:T(8,128)(2,1)S(1)}, bf16[512,256]{1,0:T(8,128)(2,1)S(1)}, u32[]{:S(2)}, u32[]{:S(2)}) %collective-permute-start.2) | collective-permute-done | bytes 262176 | tf_op jit(solution)/shard_map/ppermute | solution.py:30
  21.9 6.4 %shard_map.140 = (bf16[64,4096]{1,0:T(8,128)(2,1)S(1)}, bf16[64,4096]{1,0:T(8,128)(2,1)S(1)}) custom-call(s32[8]{0:T(128)S(1)} %broadcast_subtract_fusion.valid_ref, bf16[128,128]{1,0:T(8,128)(2,1)S(1)} %fusion.14.perm_ref, bf16[128,768]{1,0:T(8,128)(2,1)S(1)} %bitcast.56, bf16[128,128]{1,0:T(8,128)(2,1)S(1)} %fusion.6.mask_ref, ...), custom_call_target="tpu_custom_call" | custom-call | flops 1644167168 | bytes 7405568 | tf_op jit(solution)/shard_map/pallas_call | solution.py:115
  28.6 1.8 %collective-permute-done.7 = bf16[64,4096]{1,0:T(8,128)(2,1)S(1)} collective-permute-done((bf16[64,4096]{1,0:T(8,128)(2,1)S(1)}, bf16[64,4096]{1,0:T(8,128)(2,1)S(1)}, u32[]{:S(2)}, u32[]{:S(2)}) %collective-permute-start.7) | collective-permute-done | bytes 524320 | tf_op jit(solution)/shard_map/ppermute | solution.py:30
  30.4 2.5 %collective-permute-start.8 = (bf16[16,4096]{1,0:T(8,128)(2,1)S(1)}, bf16[16,4096]{1,0:T(8,128)(2,1)S(1)}, u32[]{:S(2)}, u32[]{:S(2)}) collective-permute-start(bf16[16,4096]{1,0:T(8,128)(2,1)S(1)} %get-tuple-element.60), channel_id=1, source_target_pairs={{0,4},{1,5},{2,6},{3,7},{4,0},{5,1},{6,2},{7,3},{8,12},{9,13},{10,... | collective-permute-start | bytes 393224 | tf_op jit(solution)/shard_map/ppermute | solution.py:30
  33.0 1.5 %collective-permute-start.9 = (bf16[16,4096]{1,0:T(8,128)(2,1)S(1)}, bf16[16,4096]{1,0:T(8,128)(2,1)S(1)}, u32[]{:S(2)}, u32[]{:S(2)}) collective-permute-start(bf16[16,4096]{1,0:T(8,128)(2,1)S(1)} %get-tuple-element.62), channel_id=1, source_target_pairs={{0,2},{1,3},{2,0},{3,1},{4,6},{5,7},{6,4},{7,5},{8,10},{9,11},{10,... | collective-permute-start | bytes 393224 | tf_op jit(solution)/shard_map/ppermute | solution.py:30
  36.8 2.2 %collective-permute-done.8 = bf16[16,4096]{1,0:T(8,128)(2,1)S(1)} collective-permute-done((bf16[16,4096]{1,0:T(8,128)(2,1)S(1)}, bf16[16,4096]{1,0:T(8,128)(2,1)S(1)}, u32[]{:S(2)}, u32[]{:S(2)}) %collective-permute-start.8) | collective-permute-done | bytes 131104 | tf_op jit(solution)/shard_map/ppermute | solution.py:30
  40.9 1.7 %fusion.10 = (bf16[16,4096]{1,0:T(8,128)(2,1)S(1)}, bf16[16,4096]{1,0:T(8,128)(2,1)}) fusion(bf16[1,16,4096]{2,1,0:T(8,128)(2,1)} %param.18, bf16[16,4096]{1,0:T(8,128)(2,1)S(1)} %collective-permute-done.10, bf16[16,4096]{1,0:T(8,128)(2,1)S(1)} %collective-permute-done.9, bf16[16,4096]{1,0:T(8,128)(2,1)S(1)} %collective-permute-done.8, ...), kind=kLoop, calls=%fused_computation.34 | loop fusion | flops 917504 | bytes 1048576 | tf_op jit(solution)/shard_map/convert_element_type | solution.py:490
  42.9 3.7 %collective-permute-start.19 = (bf16[16,2176]{1,0:T(8,128)(2,1)S(1)}, bf16[16,2176]{1,0:T(8,128)(2,1)S(1)}, u32[]{:S(2)}, u32[]{:S(2)}) collective-permute-start(bf16[16,2176]{1,0:T(8,128)(2,1)S(1)} %pad_maximum_fusion.3), channel_id=1, source_target_pairs={{0,24},{8,16},{16,8},{24,0},{1,25},{9,17},{17,9},{25,1},{2,26},{10... | collective-permute-start | bytes 208904 | tf_op jit(solution)/shard_map/ppermute | solution.py:35
  47.3 2.3 %collective-permute-done.19 = bf16[16,2176]{1,0:T(8,128)(2,1)S(1)} collective-permute-done((bf16[16,2176]{1,0:T(8,128)(2,1)S(1)}, bf16[16,2176]{1,0:T(8,128)(2,1)S(1)}, u32[]{:S(2)}, u32[]{:S(2)}) %collective-permute-start.19) | collective-permute-done | bytes 69664 | tf_op jit(solution)/shard_map/ppermute | solution.py:35
  49.6 2.4 %collective-permute-done.18 = bf16[16,2176]{1,0:T(8,128)(2,1)S(1)} collective-permute-done((bf16[16,2176]{1,0:T(8,128)(2,1)S(1)}, bf16[16,2176]{1,0:T(8,128)(2,1)S(1)}, u32[]{:S(2)}, u32[]{:S(2)}) %collective-permute-start.18) | collective-permute-done | bytes 69664 | tf_op jit(solution)/shard_map/ppermute | solution.py:35
  53.8 1.8 %collective-permute-start.20 = (bf16[64,2176]{1,0:T(8,128)(2,1)S(1)}, bf16[64,2176]{1,0:T(8,128)(2,1)S(1)}, u32[]{:S(2)}, u32[]{:S(2)}) collective-permute-start(bf16[64,2176]{1,0:T(8,128)(2,1)S(1)} %pad_maximum_fusion.refs_0_), channel_id=1, source_target_pairs={{0,6},{1,7},{2,4},{3,5},{4,2},{5,3},{6,0},{7,1},{8,14},{9,15},{10,... | collective-permute-start | bytes 835592 | tf_op jit(solution)/shard_map/ppermute | solution.py:30
  55.7 2.5 %collective-permute-start.13 = (bf16[16,2048]{1,0:T(8,128)(2,1)S(1)}, bf16[16,2048]{1,0:T(8,128)(2,1)S(1)}, u32[]{:S(2)}, u32[]{:S(2)}) collective-permute-start(bf16[16,2048]{1,0:T(8,128)(2,1)S(1)} %get-tuple-element.72), channel_id=1, source_target_pairs={{0,24},{8,16},{16,8},{24,0},{1,25},{9,17},{17,9},{25,1},{2,26},{10... | collective-permute-start | bytes 196616 | tf_op jit(solution)/shard_map/ppermute | solution.py:35
  58.2 4.2 %collective-permute-done.13 = bf16[16,2048]{1,0:T(8,128)(2,1)S(1)} collective-permute-done((bf16[16,2048]{1,0:T(8,128)(2,1)S(1)}, bf16[16,2048]{1,0:T(8,128)(2,1)S(1)}, u32[]{:S(2)}, u32[]{:S(2)}) %collective-permute-start.13) | collective-permute-done | bytes 65568 | tf_op jit(solution)/shard_map/ppermute | solution.py:35
  64.3 2.2 %collective-permute-done.20.refs_1_ = bf16[64,2176]{1,0:T(8,128)(2,1)S(1)} collective-permute-done((bf16[64,2176]{1,0:T(8,128)(2,1)S(1)}, bf16[64,2176]{1,0:T(8,128)(2,1)S(1)}, u32[]{:S(2)}, u32[]{:S(2)}) %collective-permute-start.20) | collective-permute-done | bytes 278560 | tf_op jit(solution)/shard_map/ppermute | solution.py:30
  66.7 1.7 %collective-permute-start.16 = (bf16[64,2048]{1,0:T(8,128)(2,1)S(1)}, bf16[64,2048]{1,0:T(8,128)(2,1)S(1)}, u32[]{:S(2)}, u32[]{:S(2)}) collective-permute-start(bf16[64,2048]{1,0:T(8,128)(2,1)S(1)} %pad_maximum_fusion.1.refs_0_), channel_id=1, source_target_pairs={{0,2},{1,3},{2,0},{3,1},{4,6},{5,7},{6,4},{7,5},{8,10},{9,11},{10,... | collective-permute-start | bytes 786440 | tf_op jit(solution)/shard_map/ppermute | solution.py:30
  70.3 8.9 %shard_map.141 = (f32[16,128,128]{2,1,0:T(8,128)S(1)}, f32[16,128,128]{2,1,0:T(8,128)S(1)}, bf16[512,256]{1,0:T(8,128)(2,1)S(1)}, f32[2,128,1]{2,1,0:T(8,128)S(1)}, bf16[8,128,4096]{2,1,0:T(8,128)(2,1)S(1)}) custom-call(bf16[64,2176]{1,0:T(8,128)(2,1)S(1)} %pad_maximum_fusion.refs_0_, bf16[64,2176]{1,0:T(8,128)(2,1)S(1)} %collective-permute-done.20.refs_1_, ...), custom_call_target="tpu_custom_call" | custom-call | flops 2684354560 | bytes 27262976 | tf_op jit(solution)/shard_map/pallas_call | solution.py:402
  79.2 2.7 %collective-permute-done.15.refs_2_ = bf16[64,2048]{1,0:T(8,128)(2,1)S(1)} collective-permute-done((bf16[64,2048]{1,0:T(8,128)(2,1)S(1)}, bf16[64,2048]{1,0:T(8,128)(2,1)S(1)}, u32[]{:S(2)}, u32[]{:S(2)}) %collective-permute-start.15) | collective-permute-done | bytes 262176 | tf_op jit(solution)/shard_map/ppermute | solution.py:30
  84.6 9.7 %shard_map.142 = (bf16[256,2048]{1,0:T(8,128)(2,1)S(1)}, bf16[256,2048]{1,0:T(8,128)(2,1)S(1)}, bf16[256,1024]{1,0:T(8,128)(2,1)S(1)}) custom-call(bf16[64,2048]{1,0:T(8,128)(2,1)S(1)} %pad_maximum_fusion.1.refs_0_, bf16[64,2048]{1,0:T(8,128)(2,1)S(1)} %collective-permute-done.14.refs_1_, bf16[64,2048]{1,0:T(8,128)(2,1)S(1)} %collective-permute-done.15.refs_2_, ...), custom_call_target="tpu_custom_call" | custom-call | flops 4294967296 | bytes 27262976 | tf_op jit(solution)/shard_map/pallas_call | solution.py:402
  94.5 4.0 %shard_map.143 = (bf16[256,2048]{1,0:T(8,128)(2,1)S(1)}, bf16[256,2048]{1,0:T(8,128)(2,1)S(1)}) custom-call(bf16[256,1024]{1,0:T(8,128)(2,1)S(1)} %get-tuple-element.39.hidden_ref, bf16[8,128,4096]{2,1,0:T(8,128)(2,1)S(1)} %get-tuple-element.38.refs_14_.ready_ref, bf16[512,256]{1,0:T(8,128)(2,1)S(1)} %get-tuple-element.36.refs_12_.back_ref, ...), custom_call_target="tpu_custom_call" | custom-call | flops 2684354560 | bytes 4194304 | tf_op jit(solution)/shard_map/pallas_call | solution.py:343
  99.9 1.4 %collective-permute-done.32 = bf16[256,2048]{1,0:T(8,128)(2,1)S(1)} collective-permute-done((bf16[256,2048]{1,0:T(8,128)(2,1)S(1)}, bf16[256,2048]{1,0:T(8,128)(2,1)S(1)}, u32[]{:S(2)}, u32[]{:S(2)}) %collective-permute-start.32) | collective-permute-done | bytes 1048608 | tf_op jit(solution)/shard_map/ppermute | solution.py:30
  102.6 4.9 %collective-permute-done.33 = bf16[64,2048]{1,0:T(8,128)(2,1)S(1)} collective-permute-done((bf16[64,2048]{1,0:T(8,128)(2,1)S(1)}, bf16[64,2048]{1,0:T(8,128)(2,1)S(1)}, u32[]{:S(2)}, u32[]{:S(2)}) %collective-permute-start.33) | collective-permute-done | bytes 262176 | tf_op jit(solution)/shard_map/ppermute | solution.py:30
  107.7 2.4 %collective-permute-done.34 = bf16[64,2048]{1,0:T(8,128)(2,1)S(1)} collective-permute-done((bf16[64,2048]{1,0:T(8,128)(2,1)S(1)}, bf16[64,2048]{1,0:T(8,128)(2,1)S(1)}, u32[]{:S(2)}, u32[]{:S(2)}) %collective-permute-start.34) | collective-permute-done | bytes 262176 | tf_op jit(solution)/shard_map/ppermute | solution.py:30
  112.0 5.9 %collective-permute-done.35 = bf16[64,2048]{1,0:T(8,128)(2,1)S(1)} collective-permute-done((bf16[64,2048]{1,0:T(8,128)(2,1)S(1)}, bf16[64,2048]{1,0:T(8,128)(2,1)S(1)}, u32[]{:S(2)}, u32[]{:S(2)}) %collective-permute-start.35) | collective-permute-done | bytes 262176 | tf_op jit(solution)/shard_map/ppermute | solution.py:30
  121.1 2.5 %collective-permute-start.39 = (bf16[16,2048]{1,0:T(8,128)(2,1)S(1)}, bf16[16,2048]{1,0:T(8,128)(2,1)S(1)}, u32[]{:S(2)}, u32[]{:S(2)}) collective-permute-start(bf16[16,2048]{1,0:T(8,128)(2,1)S(1)} %get-tuple-element.66), channel_id=1, source_target_pairs={{0,24},{8,16},{16,8},{24,0},{1,25},{9,17},{17,9},{25,1},{2,26},{10... | collective-permute-start | bytes 196616 | tf_op jit(solution)/shard_map/ppermute | solution.py:35
  126.6 2.1 %collective-permute-start.44 = (bf16[16,2048]{1,0:T(8,128)(2,1)S(1)}, bf16[16,2048]{1,0:T(8,128)(2,1)S(1)}, u32[]{:S(2)}, u32[]{:S(2)}) collective-permute-start(bf16[16,2048]{1,0:T(8,128)(2,1)S(1)} %get-tuple-element.69), channel_id=1, source_target_pairs={{0,24},{8,16},{16,8},{24,0},{1,25},{9,17},{17,9},{25,1},{2,26},{10... | collective-permute-start | bytes 196616 | tf_op jit(solution)/shard_map/ppermute | solution.py:35
  128.6 1.4 %collective-permute-start.43 = (bf16[16,2048]{1,0:T(8,128)(2,1)S(1)}, bf16[16,2048]{1,0:T(8,128)(2,1)S(1)}, u32[]{:S(2)}, u32[]{:S(2)}) collective-permute-start(bf16[16,2048]{1,0:T(8,128)(2,1)S(1)} %get-tuple-element.70), channel_id=1, source_target_pairs={{0,16},{8,24},{16,0},{24,8},{1,17},{9,25},{17,1},{25,9},{2,18},{10... | collective-permute-start | bytes 196616 | tf_op jit(solution)/shard_map/ppermute | solution.py:35
  130.0 1.5 %collective-permute-done.38 = bf16[16,2048]{1,0:T(8,128)(2,1)S(1)} collective-permute-done((bf16[16,2048]{1,0:T(8,128)(2,1)S(1)}, bf16[16,2048]{1,0:T(8,128)(2,1)S(1)}, u32[]{:S(2)}, u32[]{:S(2)}) %collective-permute-start.38) | collective-permute-done | bytes 65568 | tf_op jit(solution)/shard_map/ppermute | solution.py:35
  132.8 2.0 %collective-permute-done.43 = bf16[16,2048]{1,0:T(8,128)(2,1)S(1)} collective-permute-done((bf16[16,2048]{1,0:T(8,128)(2,1)S(1)}, bf16[16,2048]{1,0:T(8,128)(2,1)S(1)}, u32[]{:S(2)}, u32[]{:S(2)}) %collective-permute-start.43) | collective-permute-done | bytes 65568 | tf_op jit(solution)/shard_map/ppermute | solution.py:35
  (113 shorter events, 34.0 us)
Async XLA Ops:
  2.2 19.3 %collective-permute-start.3 = (bf16[512,256]{1,0:T(8,128)(2,1)S(1)}, bf16[512,256]{1,0:T(8,128)(2,1)S(1)}, u32[]{:S(2)}, u32[]{:S(2)}) collective-permute-start(bf16[512,256]{1,0:T(8,128)(2,1)S(1)} %bitcast.53), channel_id=1, source_target_pairs={{0,1},{1,0},{2,3},{3,2},{4,5},{5,4},{6,7},{7,6},{8,9},{9,8},{10,11... | collective-permute-start | bytes 786440 | tf_op jit(solution)/shard_map/ppermute | solution.py:30
  2.7 13.0 %collective-permute-start = (bf16[512,256]{1,0:T(8,128)(2,1)S(1)}, bf16[512,256]{1,0:T(8,128)(2,1)S(1)}, u32[]{:S(2)}, u32[]{:S(2)}) collective-permute-start(bf16[512,256]{1,0:T(8,128)(2,1)S(1)} %bitcast.54), channel_id=1, source_target_pairs={{0,2},{1,3},{2,0},{3,1},{4,6},{5,7},{6,4},{7,5},{8,10},{9,11},{10,... | collective-permute-start | bytes 786440 | tf_op jit(solution)/shard_map/ppermute | solution.py:30
  5.3 14.7 %collective-permute-start.2 = (bf16[512,256]{1,0:T(8,128)(2,1)S(1)}, bf16[512,256]{1,0:T(8,128)(2,1)S(1)}, u32[]{:S(2)}, u32[]{:S(2)}) collective-permute-start(bf16[512,256]{1,0:T(8,128)(2,1)S(1)} %bitcast.62), channel_id=1, source_target_pairs={{0,4},{1,5},{2,6},{3,7},{4,0},{5,1},{6,2},{7,3},{8,12},{9,13},{10,... | collective-permute-start | bytes 786440 | tf_op jit(solution)/shard_map/ppermute | solution.py:30
  6.9 13.1 %collective-permute-start.1 = (bf16[512,256]{1,0:T(8,128)(2,1)S(1)}, bf16[512,256]{1,0:T(8,128)(2,1)S(1)}, u32[]{:S(2)}, u32[]{:S(2)}) collective-permute-start(bf16[512,256]{1,0:T(8,128)(2,1)S(1)} %bitcast.63), channel_id=1, source_target_pairs={{0,6},{1,7},{2,4},{3,5},{4,2},{5,3},{6,0},{7,1},{8,14},{9,15},{10,... | collective-permute-start | bytes 786440 | tf_op jit(solution)/shard_map/ppermute | solution.py:30
  9.4 12.0 %all-to-all-start = ((bf16[8,16,768]{2,1,0:T(8,128)(2,1)}), bf16[8,16,768]{2,1,0:T(8,128)(2,1)S(1)}, u32[]{:S(2)}, u32[]{:S(2)}) async-start(bf16[8,16,768]{2,1,0:T(8,128)(2,1)} %pad_maximum_fusion.2), calls=%async_computation | async-start | bytes 393216 | tf_op jit(solution)/shard_map/all_to_all | solution.py:468
  15.7 5.8 %collective-permute-start.4 = (bf16[512,256]{1,0:T(8,128)(2,1)S(1)}, bf16[512,256]{1,0:T(8,128)(2,1)S(1)}, u32[]{:S(2)}, u32[]{:S(2)}) collective-permute-start(bf16[512,256]{1,0:T(8,128)(2,1)S(1)} %collective-permute-done.refs_1_), channel_id=1, source_target_pairs={{0,1},{1,0},{2,3},{3,2},{4,5},{5,4},{6,7},{7,6},{8,9},{9,8},{10,11... | collective-permute-start | bytes 786440 | tf_op jit(solution)/shard_map/ppermute | solution.py:30
  30.4 8.5 %collective-permute-start.8 = (bf16[16,4096]{1,0:T(8,128)(2,1)S(1)}, bf16[16,4096]{1,0:T(8,128)(2,1)S(1)}, u32[]{:S(2)}, u32[]{:S(2)}) collective-permute-start(bf16[16,4096]{1,0:T(8,128)(2,1)S(1)} %get-tuple-element.60), channel_id=1, source_target_pairs={{0,4},{1,5},{2,6},{3,7},{4,0},{5,1},{6,2},{7,3},{8,12},{9,13},{10,... | collective-permute-start | bytes 393224 | tf_op jit(solution)/shard_map/ppermute | solution.py:30
  33.0 7.3 %collective-permute-start.10 = (bf16[16,4096]{1,0:T(8,128)(2,1)S(1)}, bf16[16,4096]{1,0:T(8,128)(2,1)S(1)}, u32[]{:S(2)}, u32[]{:S(2)}) collective-permute-start(bf16[16,4096]{1,0:T(8,128)(2,1)S(1)} %get-tuple-element.61), channel_id=1, source_target_pairs={{0,6},{1,7},{2,4},{3,5},{4,2},{5,3},{6,0},{7,1},{8,14},{9,15},{10,... | collective-permute-start | bytes 393224 | tf_op jit(solution)/shard_map/ppermute | solution.py:30
  33.0 7.9 %collective-permute-start.9 = (bf16[16,4096]{1,0:T(8,128)(2,1)S(1)}, bf16[16,4096]{1,0:T(8,128)(2,1)S(1)}, u32[]{:S(2)}, u32[]{:S(2)}) collective-permute-start(bf16[16,4096]{1,0:T(8,128)(2,1)S(1)} %get-tuple-element.62), channel_id=1, source_target_pairs={{0,2},{1,3},{2,0},{3,1},{4,6},{5,7},{6,4},{7,5},{8,10},{9,11},{10,... | collective-permute-start | bytes 393224 | tf_op jit(solution)/shard_map/ppermute | solution.py:30
  42.9 6.8 %collective-permute-start.19 = (bf16[16,2176]{1,0:T(8,128)(2,1)S(1)}, bf16[16,2176]{1,0:T(8,128)(2,1)S(1)}, u32[]{:S(2)}, u32[]{:S(2)}) collective-permute-start(bf16[16,2176]{1,0:T(8,128)(2,1)S(1)} %pad_maximum_fusion.3), channel_id=1, source_target_pairs={{0,24},{8,16},{16,8},{24,0},{1,25},{9,17},{17,9},{25,1},{2,26},{10... | collective-permute-start | bytes 208904 | tf_op jit(solution)/shard_map/ppermute | solution.py:35
  46.5 5.6 %collective-permute-start.17 = (bf16[16,2176]{1,0:T(8,128)(2,1)S(1)}, bf16[16,2176]{1,0:T(8,128)(2,1)S(1)}, u32[]{:S(2)}, u32[]{:S(2)}) collective-permute-start(bf16[16,2176]{1,0:T(8,128)(2,1)S(1)} %pad_maximum_fusion.3), channel_id=1, source_target_pairs={{0,8},{8,0},{16,24},{24,16},{1,9},{9,1},{17,25},{25,17},{2,10},{10... | collective-permute-start | bytes 208904 | tf_op jit(solution)/shard_map/ppermute | solution.py:35
  52.1 11.6 %collective-permute-start.22 = (bf16[64,2176]{1,0:T(8,128)(2,1)S(1)}, bf16[64,2176]{1,0:T(8,128)(2,1)S(1)}, u32[]{:S(2)}, u32[]{:S(2)}) collective-permute-start(bf16[64,2176]{1,0:T(8,128)(2,1)S(1)} %pad_maximum_fusion.refs_0_), channel_id=1, source_target_pairs={{0,2},{1,3},{2,0},{3,1},{4,6},{5,7},{6,4},{7,5},{8,10},{9,11},{10,... | collective-permute-start | bytes 835592 | tf_op jit(solution)/shard_map/ppermute | solution.py:30
  52.7 11.6 %collective-permute-start.21 = (bf16[64,2176]{1,0:T(8,128)(2,1)S(1)}, bf16[64,2176]{1,0:T(8,128)(2,1)S(1)}, u32[]{:S(2)}, u32[]{:S(2)}) collective-permute-start(bf16[64,2176]{1,0:T(8,128)(2,1)S(1)} %pad_maximum_fusion.refs_0_), channel_id=1, source_target_pairs={{0,4},{1,5},{2,6},{3,7},{4,0},{5,1},{6,2},{7,3},{8,12},{9,13},{10,... | collective-permute-start | bytes 835592 | tf_op jit(solution)/shard_map/ppermute | solution.py:30
  53.8 12.7 %collective-permute-start.20 = (bf16[64,2176]{1,0:T(8,128)(2,1)S(1)}, bf16[64,2176]{1,0:T(8,128)(2,1)S(1)}, u32[]{:S(2)}, u32[]{:S(2)}) collective-permute-start(bf16[64,2176]{1,0:T(8,128)(2,1)S(1)} %pad_maximum_fusion.refs_0_), channel_id=1, source_target_pairs={{0,6},{1,7},{2,4},{3,5},{4,2},{5,3},{6,0},{7,1},{8,14},{9,15},{10,... | collective-permute-start | bytes 835592 | tf_op jit(solution)/shard_map/ppermute | solution.py:30
  55.7 6.8 %collective-permute-start.13 = (bf16[16,2048]{1,0:T(8,128)(2,1)S(1)}, bf16[16,2048]{1,0:T(8,128)(2,1)S(1)}, u32[]{:S(2)}, u32[]{:S(2)}) collective-permute-start(bf16[16,2048]{1,0:T(8,128)(2,1)S(1)} %get-tuple-element.72), channel_id=1, source_target_pairs={{0,24},{8,16},{16,8},{24,0},{1,25},{9,17},{17,9},{25,1},{2,26},{10... | collective-permute-start | bytes 196616 | tf_op jit(solution)/shard_map/ppermute | solution.py:35
  63.7 5.7 %collective-permute-start.26 = (bf16[64,2176]{1,0:T(8,128)(2,1)S(1)}, bf16[64,2176]{1,0:T(8,128)(2,1)S(1)}, u32[]{:S(2)}, u32[]{:S(2)}) collective-permute-start(bf16[64,2176]{1,0:T(8,128)(2,1)S(1)} %collective-permute-done.22.refs_3_), channel_id=1, source_target_pairs={{0,1},{1,0},{2,3},{3,2},{4,5},{5,4},{6,7},{7,6},{8,9},{9,8},{10,11... | collective-permute-start | bytes 835592 | tf_op jit(solution)/shard_map/ppermute | solution.py:30
  64.2 6.0 %collective-permute-start.25 = (bf16[64,2176]{1,0:T(8,128)(2,1)S(1)}, bf16[64,2176]{1,0:T(8,128)(2,1)S(1)}, u32[]{:S(2)}, u32[]{:S(2)}) collective-permute-start(bf16[64,2176]{1,0:T(8,128)(2,1)S(1)} %collective-permute-done.21.refs_2_), channel_id=1, source_target_pairs={{0,1},{1,0},{2,3},{3,2},{4,5},{5,4},{6,7},{7,6},{8,9},{9,8},{10,11... | collective-permute-start | bytes 835592 | tf_op jit(solution)/shard_map/ppermute | solution.py:30
  66.7 12.5 %collective-permute-start.16 = (bf16[64,2048]{1,0:T(8,128)(2,1)S(1)}, bf16[64,2048]{1,0:T(8,128)(2,1)S(1)}, u32[]{:S(2)}, u32[]{:S(2)}) collective-permute-start(bf16[64,2048]{1,0:T(8,128)(2,1)S(1)} %pad_maximum_fusion.1.refs_0_), channel_id=1, source_target_pairs={{0,2},{1,3},{2,0},{3,1},{4,6},{5,7},{6,4},{7,5},{8,10},{9,11},{10,... | collective-permute-start | bytes 786440 | tf_op jit(solution)/shard_map/ppermute | solution.py:30
  68.4 13.6 %collective-permute-start.15 = (bf16[64,2048]{1,0:T(8,128)(2,1)S(1)}, bf16[64,2048]{1,0:T(8,128)(2,1)S(1)}, u32[]{:S(2)}, u32[]{:S(2)}) collective-permute-start(bf16[64,2048]{1,0:T(8,128)(2,1)S(1)} %pad_maximum_fusion.1.refs_0_), channel_id=1, source_target_pairs={{0,4},{1,5},{2,6},{3,7},{4,0},{5,1},{6,2},{7,3},{8,12},{9,13},{10,... | collective-permute-start | bytes 786440 | tf_op jit(solution)/shard_map/ppermute | solution.py:30
  69.5 12.5 %collective-permute-start.14 = (bf16[64,2048]{1,0:T(8,128)(2,1)S(1)}, bf16[64,2048]{1,0:T(8,128)(2,1)S(1)}, u32[]{:S(2)}, u32[]{:S(2)}) collective-permute-start(bf16[64,2048]{1,0:T(8,128)(2,1)S(1)} %pad_maximum_fusion.1.refs_0_), channel_id=1, source_target_pairs={{0,6},{1,7},{2,4},{3,5},{4,2},{5,3},{6,0},{7,1},{8,14},{9,15},{10,... | collective-permute-start | bytes 786440 | tf_op jit(solution)/shard_map/ppermute | solution.py:30
  99.1 8.4 %collective-permute-start.33 = (bf16[64,2048]{1,0:T(8,128)(2,1)S(1)}, bf16[64,2048]{1,0:T(8,128)(2,1)S(1)}, u32[]{:S(2)}, u32[]{:S(2)}) collective-permute-start(bf16[64,2048]{1,0:T(8,128)(2,1)S(1)} %add_convert_fusion.4), channel_id=1, source_target_pairs={{0,2},{1,3},{2,0},{3,1},{4,6},{5,7},{6,4},{7,5},{8,10},{9,11},{10,... | collective-permute-start | bytes 786440 | tf_op jit(solution)/shard_map/ppermute | solution.py:30
  101.4 8.7 %collective-permute-start.34 = (bf16[64,2048]{1,0:T(8,128)(2,1)S(1)}, bf16[64,2048]{1,0:T(8,128)(2,1)S(1)}, u32[]{:S(2)}, u32[]{:S(2)}) collective-permute-start(bf16[64,2048]{1,0:T(8,128)(2,1)S(1)} %get-tuple-element.57), channel_id=1, source_target_pairs={{0,4},{1,5},{2,6},{3,7},{4,0},{5,1},{6,2},{7,3},{8,12},{9,13},{10,... | collective-permute-start | bytes 786440 | tf_op jit(solution)/shard_map/ppermute | solution.py:30
  110.1 7.8 %collective-permute-start.35 = (bf16[64,2048]{1,0:T(8,128)(2,1)S(1)}, bf16[64,2048]{1,0:T(8,128)(2,1)S(1)}, u32[]{:S(2)}, u32[]{:S(2)}) collective-permute-start(bf16[64,2048]{1,0:T(8,128)(2,1)S(1)} %get-tuple-element.47), channel_id=1, source_target_pairs={{0,2},{1,3},{2,0},{3,1},{4,6},{5,7},{6,4},{7,5},{8,10},{9,11},{10,... | collective-permute-start | bytes 786440 | tf_op jit(solution)/shard_map/ppermute | solution.py:30
  111.0 7.5 %collective-permute-start.36 = (bf16[64,2048]{1,0:T(8,128)(2,1)S(1)}, bf16[64,2048]{1,0:T(8,128)(2,1)S(1)}, u32[]{:S(2)}, u32[]{:S(2)}) collective-permute-start(bf16[64,2048]{1,0:T(8,128)(2,1)S(1)} %get-tuple-element.48), channel_id=1, source_target_pairs={{0,4},{1,5},{2,6},{3,7},{4,0},{5,1},{6,2},{7,3},{8,12},{9,13},{10,... | collective-permute-start | bytes 786440 | tf_op jit(solution)/shard_map/ppermute | solution.py:30
  118.6 6.6 %collective-permute-start.40 = (bf16[64,2048]{1,0:T(8,128)(2,1)S(1)}, bf16[64,2048]{1,0:T(8,128)(2,1)S(1)}, u32[]{:S(2)}, u32[]{:S(2)}) collective-permute-start(bf16[64,2048]{1,0:T(8,128)(2,1)S(1)} %add_convert_fusion.1), channel_id=1, source_target_pairs={{0,2},{1,3},{2,0},{3,1},{4,6},{5,7},{6,4},{7,5},{8,10},{9,11},{10,... | collective-permute-start | bytes 786440 | tf_op jit(solution)/shard_map/ppermute | solution.py:30
  119.9 6.4 %collective-permute-start.41 = (bf16[64,2048]{1,0:T(8,128)(2,1)S(1)}, bf16[64,2048]{1,0:T(8,128)(2,1)S(1)}, u32[]{:S(2)}, u32[]{:S(2)}) collective-permute-start(bf16[64,2048]{1,0:T(8,128)(2,1)S(1)} %get-tuple-element.51), channel_id=1, source_target_pairs={{0,4},{1,5},{2,6},{3,7},{4,0},{5,1},{6,2},{7,3},{8,12},{9,13},{10,... | collective-permute-start | bytes 786440 | tf_op jit(solution)/shard_map/ppermute | solution.py:30
  121.0 7.6 %collective-permute-start.37 = (bf16[16,2048]{1,0:T(8,128)(2,1)S(1)}, bf16[16,2048]{1,0:T(8,128)(2,1)S(1)}, u32[]{:S(2)}, u32[]{:S(2)}) collective-permute-start(bf16[16,2048]{1,0:T(8,128)(2,1)S(1)} %get-tuple-element.65), channel_id=1, source_target_pairs={{0,8},{8,0},{16,24},{24,16},{1,9},{9,1},{17,25},{25,17},{2,10},{10... | collective-permute-start | bytes 196616 | tf_op jit(solution)/shard_map/ppermute | solution.py:35
  121.1 8.9 %collective-permute-start.39 = (bf16[16,2048]{1,0:T(8,128)(2,1)S(1)}, bf16[16,2048]{1,0:T(8,128)(2,1)S(1)}, u32[]{:S(2)}, u32[]{:S(2)}) collective-permute-start(bf16[16,2048]{1,0:T(8,128)(2,1)S(1)} %get-tuple-element.66), channel_id=1, source_target_pairs={{0,24},{8,16},{16,8},{24,0},{1,25},{9,17},{17,9},{25,1},{2,26},{10... | collective-permute-start | bytes 196616 | tf_op jit(solution)/shard_map/ppermute | solution.py:35
  123.6 8.0 %collective-permute-start.38 = (bf16[16,2048]{1,0:T(8,128)(2,1)S(1)}, bf16[16,2048]{1,0:T(8,128)(2,1)S(1)}, u32[]{:S(2)}, u32[]{:S(2)}) collective-permute-start(bf16[16,2048]{1,0:T(8,128)(2,1)S(1)} %get-tuple-element.67), channel_id=1, source_target_pairs={{0,16},{8,24},{16,0},{24,8},{1,17},{9,25},{17,1},{25,9},{2,18},{10... | collective-permute-start | bytes 196616 | tf_op jit(solution)/shard_map/ppermute | solution.py:35
  126.5 5.6 %collective-permute-start.42 = (bf16[16,2048]{1,0:T(8,128)(2,1)S(1)}, bf16[16,2048]{1,0:T(8,128)(2,1)S(1)}, u32[]{:S(2)}, u32[]{:S(2)}) collective-permute-start(bf16[16,2048]{1,0:T(8,128)(2,1)S(1)} %get-tuple-element.68), channel_id=1, source_target_pairs={{0,8},{8,0},{16,24},{24,16},{1,9},{9,1},{17,25},{25,17},{2,10},{10... | collective-permute-start | bytes 196616 | tf_op jit(solution)/shard_map/ppermute | solution.py:35
  126.6 6.2 %collective-permute-start.44 = (bf16[16,2048]{1,0:T(8,128)(2,1)S(1)}, bf16[16,2048]{1,0:T(8,128)(2,1)S(1)}, u32[]{:S(2)}, u32[]{:S(2)}) collective-permute-start(bf16[16,2048]{1,0:T(8,128)(2,1)S(1)} %get-tuple-element.69), channel_id=1, source_target_pairs={{0,24},{8,16},{16,8},{24,0},{1,25},{9,17},{17,9},{25,1},{2,26},{10... | collective-permute-start | bytes 196616 | tf_op jit(solution)/shard_map/ppermute | solution.py:35
  128.6 6.1 %collective-permute-start.43 = (bf16[16,2048]{1,0:T(8,128)(2,1)S(1)}, bf16[16,2048]{1,0:T(8,128)(2,1)S(1)}, u32[]{:S(2)}, u32[]{:S(2)}) collective-permute-start(bf16[16,2048]{1,0:T(8,128)(2,1)S(1)} %get-tuple-element.70), channel_id=1, source_target_pairs={{0,16},{8,24},{16,0},{24,8},{1,17},{9,25},{17,1},{25,9},{2,18},{10... | collective-permute-start | bytes 196616 | tf_op jit(solution)/shard_map/ppermute | solution.py:35
  (14 other events, 43.5 us)

commit v4 on v3

--- a/solution.py
+++ b/solution.py
@@ -17,11 +17,11 @@
 
 NEG = -1e30
 EPS = 1e-06
-RISE_LIMIT = 34 * 1024 * 1024
-FALL_LIMIT = 33 * 1024 * 1024
-LAST_LIMIT = 30 * 1024 * 1024
+RISE_LIMIT = 30 * 1024 * 1024
+FALL_LIMIT = 29 * 1024 * 1024
+LAST_LIMIT = 26 * 1024 * 1024
 ATTEND_LIMIT = 48 * 1024 * 1024
-READY = 8
+READY = 12
 LOG2E = 1.4426950408889634
 
 
@@ -270,12 +270,11 @@
         for move in early:
             move.wait()
         return
-    for p in range(ready, held):
-        down_move(p).wait()
-    drop_columns(hidden, ready_ref, wd, back_ref, flat, *outs[:2])
-
-
-def drop_columns(hidden, ready_ref, wd, back_ref, flat, keep_ref, send_ref, first=0):
+    moves = [down_move(p) for p in range(ready, held)]
+    drop_columns(hidden, ready_ref, wd, back_ref, flat, *outs[:2], moves)
+
+
+def drop_columns(hidden, ready_ref, wd, back_ref, flat, keep_ref, send_ref, moves, first=0):
     cut = flat.shape[1]
     lines = hidden.shape[0]
     ready, wide, _ = ready_ref.shape
@@ -287,6 +286,8 @@
     for e in range(experts):
         low, high = e * per_expert, (e + 1) * per_expert
         split = min(max(ready, low), high)
+        for move in moves[split - ready : high - ready] if split < high else []:
+            move.wait()
         for c in range(0, cut, tile):
             total = None
             if split > low:
@@ -315,7 +316,7 @@
 def fall_kernel(hidden_ref, ready_ref, back_ref, wd_any, keep_ref, send_ref, flat, *refs):
     ready, wide, depth = ready_ref.shape
     cut = flat.shape[1]
-    wd = None
+    wd, moves = None, []
     if refs:
         wd, sem = refs
         moves = [
@@ -326,9 +327,7 @@
         ]
         for move in moves:
             move.start()
-        for move in moves:
-            move.wait()
-    drop_columns(hidden_ref, ready_ref, wd, back_ref, flat, keep_ref, send_ref, first=cut)
+    drop_columns(hidden_ref, ready_ref, wd, back_ref, flat, keep_ref, send_ref, moves, first=cut)
 
 
 def fall_call(hidden, ready, back, w_down):
@@ -514,7 +513,10 @@
         planes.append([stack] + [hop(stack, mask) for mask in ring[1:]])
     full = planes[0] + [hop(p, 1) for p in planes[0]]
     sums = expert_call(full, w_gate, w_up, 0, cut, topk, experts, seats, first=first, w_down=w_down)
-    *plane, gate = lax.optimization_barrier((*planes[1], sums[0]))
+    plane = planes[1][:1]
+    gate = sums[0]
+    for piece in planes[1][1:]:
+        plane.append(lax.optimization_barrier((piece, gate))[0])
     full = plane + [hop(p, 1) for p in plane]
     keep0, send0, hidden = expert_call(
         full, w_gate, w_up, 1, cut, topk, experts, seats, sums=(gate, *sums[1:]), w_down=w_down

time: 136 us -> 134 us (0.985)
  transfers between devices with their start and end apart: 46 -> 46, of which waited for: 30 -> 29; matrix products, arithmetic and copies ran while one was open for 6% -> 6% of each run, Pallas kernels for 10% -> 10%
where the time goes in v4:
time: 134 us; the launch traced here: 133 us
  waiting for transfers between devices  47.6 us (36%)
  starting transfers between devices  43.3 us (32%)
  Pallas kernels  28.7 us (21%)
  other arithmetic  8.09 us (6%)
  local copies, waits for them, and re-layouts  2.21 us (2%)
  matrix products  1.85 us (1%)
  between operations  1.61 us (1%)
    ppermute x33, waiting for transfers between devices, hop(): return lax.ppermute(value, 'seq', [(i, i ^ mask) for i in range(count)])  32.4 us
    ppermute x33, starting transfers between devices, hop(): return lax.ppermute(value, 'seq', [(i, i ^ mask) for i in range(count)])  25.1 us
    pallas_call x2, Pallas kernels, expert_call(): pl.pallas_call(functools.partial(expert_kernel, len(rows), experts, seats...  19.4 us
    ppermute x12, waiting for transfers between devices, turn(): return lax.ppermute(value, 'req', [(i, i ^ step) for i in range(count)])  15.1 us
    ppermute x12, starting transfers between devices, turn(): return lax.ppermute(value, 'req', [(i, i ^ step) for i in range(count)])  14.1 us
    pallas_call x1, Pallas kernels, attend(): pl.pallas_call(functools.partial(attend_kernel, parts, mine), out_shape=(...  6.44 us
    all_to_all x1, starting transfers between devices, body(): lax.all_to_all(packed, 'seq', split_axis=0, concat_axis=0, tiled=True)  4.15 us
    pallas_call x1, Pallas kernels, fall_call(): pl.pallas_call(fall_kernel, out_shape=(shape, shape), in_specs=[full, ful...  2.85 us
  transfers between devices with their start and end apart: 46, of which 29 were waited for; matrix products, arithmetic and copies ran while one was open for 6% of the time, Pallas kernels for 10%

profile of v4, /device:TPU:0, one launch (start us, length us, event | category | flops | bytes accessed | tf_op | source)
XLA Modules:
  0.0 133.5 jit_solution(13577616271749491409)
XLA Ops:
  0.7 1.5 %broadcast_select_fusion = (bf16[512,2,128]{2,1,0:T(2,128)(2,1)S(1)}, bf16[512,2,128]{2,1,0:T(2,128)(2,1)S(1)}) fusion(pred[]{:T(512)S(6)} %eq.58, bf16[512,2,256]{2,1,0:T(2,128)(2,1)} %bitcast.59, pred[]{:T(512)S(6)} %eq.57), kind=kLoop, calls=%fused_computation.22 | loop fusion | flops 262144 | bytes 1048578 | tf_op jit(solution)/shard_map/jit(_where)/select_n | solution.py:450
  2.7 2.6 %collective-permute-start = (bf16[512,256]{1,0:T(8,128)(2,1)S(1)}, bf16[512,256]{1,0:T(8,128)(2,1)S(1)}, u32[]{:S(2)}, u32[]{:S(2)}) collective-permute-start(bf16[512,256]{1,0:T(8,128)(2,1)S(1)} %bitcast.54), channel_id=1, source_target_pairs={{0,2},{1,3},{2,0},{3,1},{4,6},{5,7},{6,4},{7,5},{8,10},{9,11},{10,... | collective-permute-start | bytes 786440 | tf_op jit(solution)/shard_map/ppermute | solution.py:30
  5.3 1.6 %collective-permute-start.2 = (bf16[512,256]{1,0:T(8,128)(2,1)S(1)}, bf16[512,256]{1,0:T(8,128)(2,1)S(1)}, u32[]{:S(2)}, u32[]{:S(2)}) collective-permute-start(bf16[512,256]{1,0:T(8,128)(2,1)S(1)} %bitcast.62), channel_id=1, source_target_pairs={{0,4},{1,5},{2,6},{3,7},{4,0},{5,1},{6,2},{7,3},{8,12},{9,13},{10,... | collective-permute-start | bytes 786440 | tf_op jit(solution)/shard_map/ppermute | solution.py:30
  9.4 4.2 %all-to-all-start = ((bf16[8,16,768]{2,1,0:T(8,128)(2,1)}), bf16[8,16,768]{2,1,0:T(8,128)(2,1)S(1)}, u32[]{:S(2)}, u32[]{:S(2)}) async-start(bf16[8,16,768]{2,1,0:T(8,128)(2,1)} %pad_maximum_fusion.2), calls=%async_computation | async-start | bytes 393216 | tf_op jit(solution)/shard_map/all_to_all | solution.py:467
  16.3 3.7 %collective-permute-done.2.refs_3_ = bf16[512,256]{1,0:T(8,128)(2,1)S(1)} collective-permute-done((bf16[512,256]{1,0:T(8,128)(2,1)S(1)}, bf16[512,256]{1,0:T(8,128)(2,1)S(1)}, u32[]{:S(2)}, u32[]{:S(2)}) %collective-permute-start.2) | collective-permute-done | bytes 262176 | tf_op jit(solution)/shard_map/ppermute | solution.py:30
  21.9 6.4 %shard_map.140 = (bf16[64,4096]{1,0:T(8,128)(2,1)S(1)}, bf16[64,4096]{1,0:T(8,128)(2,1)S(1)}) custom-call(s32[8]{0:T(128)S(1)} %broadcast_subtract_fusion.valid_ref, bf16[128,128]{1,0:T(8,128)(2,1)S(1)} %fusion.14.perm_ref, bf16[128,768]{1,0:T(8,128)(2,1)S(1)} %bitcast.56, bf16[128,128]{1,0:T(8,128)(2,1)S(1)} %fusion.6.mask_ref, ...), custom_call_target="tpu_custom_call" | custom-call | flops 1644167168 | bytes 7405568 | tf_op jit(solution)/shard_map/pallas_call | solution.py:115
  28.6 1.8 %collective-permute-done.7 = bf16[64,4096]{1,0:T(8,128)(2,1)S(1)} collective-permute-done((bf16[64,4096]{1,0:T(8,128)(2,1)S(1)}, bf16[64,4096]{1,0:T(8,128)(2,1)S(1)}, u32[]{:S(2)}, u32[]{:S(2)}) %collective-permute-start.7) | collective-permute-done | bytes 524320 | tf_op jit(solution)/shard_map/ppermute | solution.py:30
  30.4 2.5 %collective-permute-start.8 = (bf16[16,4096]{1,0:T(8,128)(2,1)S(1)}, bf16[16,4096]{1,0:T(8,128)(2,1)S(1)}, u32[]{:S(2)}, u32[]{:S(2)}) collective-permute-start(bf16[16,4096]{1,0:T(8,128)(2,1)S(1)} %get-tuple-element.56), channel_id=1, source_target_pairs={{0,4},{1,5},{2,6},{3,7},{4,0},{5,1},{6,2},{7,3},{8,12},{9,13},{10,... | collective-permute-start | bytes 393224 | tf_op jit(solution)/shard_map/ppermute | solution.py:30
  33.0 1.5 %collective-permute-start.9 = (bf16[16,4096]{1,0:T(8,128)(2,1)S(1)}, bf16[16,4096]{1,0:T(8,128)(2,1)S(1)}, u32[]{:S(2)}, u32[]{:S(2)}) collective-permute-start(bf16[16,4096]{1,0:T(8,128)(2,1)S(1)} %get-tuple-element.58), channel_id=1, source_target_pairs={{0,2},{1,3},{2,0},{3,1},{4,6},{5,7},{6,4},{7,5},{8,10},{9,11},{10,... | collective-permute-start | bytes 393224 | tf_op jit(solution)/shard_map/ppermute | solution.py:30
  36.8 2.2 %collective-permute-done.8 = bf16[16,4096]{1,0:T(8,128)(2,1)S(1)} collective-permute-done((bf16[16,4096]{1,0:T(8,128)(2,1)S(1)}, bf16[16,4096]{1,0:T(8,128)(2,1)S(1)}, u32[]{:S(2)}, u32[]{:S(2)}) %collective-permute-start.8) | collective-permute-done | bytes 131104 | tf_op jit(solution)/shard_map/ppermute | solution.py:30
  40.9 1.7 %fusion.10 = (bf16[16,4096]{1,0:T(8,128)(2,1)S(1)}, bf16[16,4096]{1,0:T(8,128)(2,1)}) fusion(bf16[1,16,4096]{2,1,0:T(8,128)(2,1)} %param.18, bf16[16,4096]{1,0:T(8,128)(2,1)S(1)} %collective-permute-done.10, bf16[16,4096]{1,0:T(8,128)(2,1)S(1)} %collective-permute-done.9, bf16[16,4096]{1,0:T(8,128)(2,1)S(1)} %collective-permute-done.8, ...), kind=kLoop, calls=%fused_computation.34 | loop fusion | flops 917504 | bytes 1048576 | tf_op jit(solution)/shard_map/convert_element_type | solution.py:489
  42.9 3.7 %collective-permute-start.17 = (bf16[16,2176]{1,0:T(8,128)(2,1)S(1)}, bf16[16,2176]{1,0:T(8,128)(2,1)S(1)}, u32[]{:S(2)}, u32[]{:S(2)}) collective-permute-start(bf16[16,2176]{1,0:T(8,128)(2,1)S(1)} %pad_maximum_fusion.3), channel_id=1, source_target_pairs={{0,24},{8,16},{16,8},{24,0},{1,25},{9,17},{17,9},{25,1},{2,26},{10... | collective-permute-start | bytes 208904 | tf_op jit(solution)/shard_map/ppermute | solution.py:35
  47.3 2.3 %collective-permute-done.17 = bf16[16,2176]{1,0:T(8,128)(2,1)S(1)} collective-permute-done((bf16[16,2176]{1,0:T(8,128)(2,1)S(1)}, bf16[16,2176]{1,0:T(8,128)(2,1)S(1)}, u32[]{:S(2)}, u32[]{:S(2)}) %collective-permute-start.17) | collective-permute-done | bytes 69664 | tf_op jit(solution)/shard_map/ppermute | solution.py:35
  49.6 2.4 %collective-permute-done.16 = bf16[16,2176]{1,0:T(8,128)(2,1)S(1)} collective-permute-done((bf16[16,2176]{1,0:T(8,128)(2,1)S(1)}, bf16[16,2176]{1,0:T(8,128)(2,1)S(1)}, u32[]{:S(2)}, u32[]{:S(2)}) %collective-permute-start.16) | collective-permute-done | bytes 69664 | tf_op jit(solution)/shard_map/ppermute | solution.py:35
  53.8 1.8 %collective-permute-start.18 = (bf16[64,2176]{1,0:T(8,128)(2,1)S(1)}, bf16[64,2176]{1,0:T(8,128)(2,1)S(1)}, u32[]{:S(2)}, u32[]{:S(2)}) collective-permute-start(bf16[64,2176]{1,0:T(8,128)(2,1)S(1)} %pad_maximum_fusion.refs_0_), channel_id=1, source_target_pairs={{0,6},{1,7},{2,4},{3,5},{4,2},{5,3},{6,0},{7,1},{8,14},{9,15},{10,... | collective-permute-start | bytes 835592 | tf_op jit(solution)/shard_map/ppermute | solution.py:30
  55.7 2.5 %collective-permute-start.13 = (bf16[16,2048]{1,0:T(8,128)(2,1)S(1)}, bf16[16,2048]{1,0:T(8,128)(2,1)S(1)}, u32[]{:S(2)}, u32[]{:S(2)}) collective-permute-start(bf16[16,2048]{1,0:T(8,128)(2,1)S(1)} %get-tuple-element.68), channel_id=1, source_target_pairs={{0,24},{8,16},{16,8},{24,0},{1,25},{9,17},{17,9},{25,1},{2,26},{10... | collective-permute-start | bytes 196616 | tf_op jit(solution)/shard_map/ppermute | solution.py:35
  58.2 4.2 %collective-permute-done.13 = bf16[16,2048]{1,0:T(8,128)(2,1)S(1)} collective-permute-done((bf16[16,2048]{1,0:T(8,128)(2,1)S(1)}, bf16[16,2048]{1,0:T(8,128)(2,1)S(1)}, u32[]{:S(2)}, u32[]{:S(2)}) %collective-permute-start.13) | collective-permute-done | bytes 65568 | tf_op jit(solution)/shard_map/ppermute | solution.py:35
  64.3 2.2 %collective-permute-done.18.refs_1_ = bf16[64,2176]{1,0:T(8,128)(2,1)S(1)} collective-permute-done((bf16[64,2176]{1,0:T(8,128)(2,1)S(1)}, bf16[64,2176]{1,0:T(8,128)(2,1)S(1)}, u32[]{:S(2)}, u32[]{:S(2)}) %collective-permute-start.18) | collective-permute-done | bytes 278560 | tf_op jit(solution)/shard_map/ppermute | solution.py:30
  66.7 1.7 %collective-permute-start.26 = (bf16[64,2048]{1,0:T(8,128)(2,1)S(1)}, bf16[64,2048]{1,0:T(8,128)(2,1)S(1)}, u32[]{:S(2)}, u32[]{:S(2)}) collective-permute-start(bf16[64,2048]{1,0:T(8,128)(2,1)S(1)} %pad_maximum_fusion.1.refs_0_), channel_id=1, source_target_pairs={{0,2},{1,3},{2,0},{3,1},{4,6},{5,7},{6,4},{7,5},{8,10},{9,11},{10,... | collective-permute-start | bytes 786440 | tf_op jit(solution)/shard_map/ppermute | solution.py:30
  70.3 10.2 %shard_map.141 = (f32[16,128,128]{2,1,0:T(8,128)S(1)}, f32[16,128,128]{2,1,0:T(8,128)S(1)}, bf16[512,256]{1,0:T(8,128)(2,1)S(1)}, f32[2,128,1]{2,1,0:T(8,128)S(1)}, bf16[12,128,4096]{2,1,0:T(8,128)(2,1)S(1)}) custom-call(bf16[64,2176]{1,0:T(8,128)(2,1)S(1)} %pad_maximum_fusion.refs_0_, bf16[64,2176]{1,0:T(8,128)(2,1)S(1)} %collective-permute-done.18.refs_1_, ...), custom_call_target="tpu_custom_call" | custom-call | flops 2684354560 | bytes 31457280 | tf_op jit(solution)/shard_map/pallas_call | solution.py:401
  80.5 1.5 %collective-permute-done.25.refs_2_ = bf16[64,2048]{1,0:T(8,128)(2,1)S(1)} collective-permute-done((bf16[64,2048]{1,0:T(8,128)(2,1)S(1)}, bf16[64,2048]{1,0:T(8,128)(2,1)S(1)}, u32[]{:S(2)}, u32[]{:S(2)}) %collective-permute-start.25) | collective-permute-done | bytes 262176 | tf_op jit(solution)/shard_map/ppermute | solution.py:30
  84.2 9.3 %shard_map.142 = (bf16[256,2048]{1,0:T(8,128)(2,1)S(1)}, bf16[256,2048]{1,0:T(8,128)(2,1)S(1)}, bf16[256,1024]{1,0:T(8,128)(2,1)S(1)}) custom-call(bf16[64,2048]{1,0:T(8,128)(2,1)S(1)} %pad_maximum_fusion.1.refs_0_, bf16[64,2048]{1,0:T(8,128)(2,1)S(1)} %collective-permute-done.14.refs_1_, bf16[64,2048]{1,0:T(8,128)(2,1)S(1)} %collective-permute-done.25.refs_2_, ...), custom_call_target="tpu_custom_call" | custom-call | flops 4294967296 | bytes 27262976 | tf_op jit(solution)/shard_map/pallas_call | solution.py:401
  93.7 2.9 %shard_map.143 = (bf16[256,2048]{1,0:T(8,128)(2,1)S(1)}, bf16[256,2048]{1,0:T(8,128)(2,1)S(1)}) custom-call(bf16[256,1024]{1,0:T(8,128)(2,1)S(1)} %get-tuple-element.35.hidden_ref, bf16[12,128,4096]{2,1,0:T(8,128)(2,1)S(1)} %get-tuple-element.34.refs_14_.ready_ref, bf16[512,256]{1,0:T(8,128)(2,1)S(1)} %get-tuple-element.32.refs_12_.back_ref, ...), custom_call_target="tpu_custom_call" | custom-call | flops 2684354560 | bytes 2097152 | tf_op jit(solution)/shard_map/pallas_call | solution.py:342
  97.9 1.4 %collective-permute-done.32 = bf16[256,2048]{1,0:T(8,128)(2,1)S(1)} collective-permute-done((bf16[256,2048]{1,0:T(8,128)(2,1)S(1)}, bf16[256,2048]{1,0:T(8,128)(2,1)S(1)}, u32[]{:S(2)}, u32[]{:S(2)}) %collective-permute-start.32) | collective-permute-done | bytes 1048608 | tf_op jit(solution)/shard_map/ppermute | solution.py:30
  100.6 4.9 %collective-permute-done.33 = bf16[64,2048]{1,0:T(8,128)(2,1)S(1)} collective-permute-done((bf16[64,2048]{1,0:T(8,128)(2,1)S(1)}, bf16[64,2048]{1,0:T(8,128)(2,1)S(1)}, u32[]{:S(2)}, u32[]{:S(2)}) %collective-permute-start.33) | collective-permute-done | bytes 262176 | tf_op jit(solution)/shard_map/ppermute | solution.py:30
  105.7 2.4 %collective-permute-done.34 = bf16[64,2048]{1,0:T(8,128)(2,1)S(1)} collective-permute-done((bf16[64,2048]{1,0:T(8,128)(2,1)S(1)}, bf16[64,2048]{1,0:T(8,128)(2,1)S(1)}, u32[]{:S(2)}, u32[]{:S(2)}) %collective-permute-start.34) | collective-permute-done | bytes 262176 | tf_op jit(solution)/shard_map/ppermute | solution.py:30
  110.0 5.9 %collective-permute-done.35 = bf16[64,2048]{1,0:T(8,128)(2,1)S(1)} collective-permute-done((bf16[64,2048]{1,0:T(8,128)(2,1)S(1)}, bf16[64,2048]{1,0:T(8,128)(2,1)S(1)}, u32[]{:S(2)}, u32[]{:S(2)}) %collective-permute-start.35) | collective-permute-done | bytes 262176 | tf_op jit(solution)/shard_map/ppermute | solution.py:30
  119.1 2.5 %collective-permute-start.39 = (bf16[16,2048]{1,0:T(8,128)(2,1)S(1)}, bf16[16,2048]{1,0:T(8,128)(2,1)S(1)}, u32[]{:S(2)}, u32[]{:S(2)}) collective-permute-start(bf16[16,2048]{1,0:T(8,128)(2,1)S(1)} %get-tuple-element.62), channel_id=1, source_target_pairs={{0,24},{8,16},{16,8},{24,0},{1,25},{9,17},{17,9},{25,1},{2,26},{10... | collective-permute-start | bytes 196616 | tf_op jit(solution)/shard_map/ppermute | solution.py:35
  124.6 2.0 %collective-permute-start.44 = (bf16[16,2048]{1,0:T(8,128)(2,1)S(1)}, bf16[16,2048]{1,0:T(8,128)(2,1)S(1)}, u32[]{:S(2)}, u32[]{:S(2)}) collective-permute-start(bf16[16,2048]{1,0:T(8,128)(2,1)S(1)} %get-tuple-element.65), channel_id=1, source_target_pairs={{0,24},{8,16},{16,8},{24,0},{1,25},{9,17},{17,9},{25,1},{2,26},{10... | collective-permute-start | bytes 196616 | tf_op jit(solution)/shard_map/ppermute | solution.py:35
  126.6 1.4 %collective-permute-start.43 = (bf16[16,2048]{1,0:T(8,128)(2,1)S(1)}, bf16[16,2048]{1,0:T(8,128)(2,1)S(1)}, u32[]{:S(2)}, u32[]{:S(2)}) collective-permute-start(bf16[16,2048]{1,0:T(8,128)(2,1)S(1)} %get-tuple-element.66), channel_id=1, source_target_pairs={{0,16},{8,24},{16,0},{24,8},{1,17},{9,25},{17,1},{25,9},{2,18},{10... | collective-permute-start | bytes 196616 | tf_op jit(solution)/shard_map/ppermute | solution.py:35
  128.0 1.4 %collective-permute-done.38 = bf16[16,2048]{1,0:T(8,128)(2,1)S(1)} collective-permute-done((bf16[16,2048]{1,0:T(8,128)(2,1)S(1)}, bf16[16,2048]{1,0:T(8,128)(2,1)S(1)}, u32[]{:S(2)}, u32[]{:S(2)}) %collective-permute-start.38) | collective-permute-done | bytes 65568 | tf_op jit(solution)/shard_map/ppermute | solution.py:35
  130.8 2.0 %collective-permute-done.43 = bf16[16,2048]{1,0:T(8,128)(2,1)S(1)} collective-permute-done((bf16[16,2048]{1,0:T(8,128)(2,1)S(1)}, bf16[16,2048]{1,0:T(8,128)(2,1)S(1)}, u32[]{:S(2)}, u32[]{:S(2)}) %collective-permute-start.43) | collective-permute-done | bytes 65568 | tf_op jit(solution)/shard_map/ppermute | solution.py:35
  (113 shorter events, 33.7 us)
Async XLA Ops:
  2.2 19.3 %collective-permute-start.3 = (bf16[512,256]{1,0:T(8,128)(2,1)S(1)}, bf16[512,256]{1,0:T(8,128)(2,1)S(1)}, u32[]{:S(2)}, u32[]{:S(2)}) collective-permute-start(bf16[512,256]{1,0:T(8,128)(2,1)S(1)} %bitcast.53), channel_id=1, source_target_pairs={{0,1},{1,0},{2,3},{3,2},{4,5},{5,4},{6,7},{7,6},{8,9},{9,8},{10,11... | collective-permute-start | bytes 786440 | tf_op jit(solution)/shard_map/ppermute | solution.py:30
  2.7 13.0 %collective-permute-start = (bf16[512,256]{1,0:T(8,128)(2,1)S(1)}, bf16[512,256]{1,0:T(8,128)(2,1)S(1)}, u32[]{:S(2)}, u32[]{:S(2)}) collective-permute-start(bf16[512,256]{1,0:T(8,128)(2,1)S(1)} %bitcast.54), channel_id=1, source_target_pairs={{0,2},{1,3},{2,0},{3,1},{4,6},{5,7},{6,4},{7,5},{8,10},{9,11},{10,... | collective-permute-start | bytes 786440 | tf_op jit(solution)/shard_map/ppermute | solution.py:30
  5.3 14.7 %collective-permute-start.2 = (bf16[512,256]{1,0:T(8,128)(2,1)S(1)}, bf16[512,256]{1,0:T(8,128)(2,1)S(1)}, u32[]{:S(2)}, u32[]{:S(2)}) collective-permute-start(bf16[512,256]{1,0:T(8,128)(2,1)S(1)} %bitcast.62), channel_id=1, source_target_pairs={{0,4},{1,5},{2,6},{3,7},{4,0},{5,1},{6,2},{7,3},{8,12},{9,13},{10,... | collective-permute-start | bytes 786440 | tf_op jit(solution)/shard_map/ppermute | solution.py:30
  6.9 13.1 %collective-permute-start.1 = (bf16[512,256]{1,0:T(8,128)(2,1)S(1)}, bf16[512,256]{1,0:T(8,128)(2,1)S(1)}, u32[]{:S(2)}, u32[]{:S(2)}) collective-permute-start(bf16[512,256]{1,0:T(8,128)(2,1)S(1)} %bitcast.63), channel_id=1, source_target_pairs={{0,6},{1,7},{2,4},{3,5},{4,2},{5,3},{6,0},{7,1},{8,14},{9,15},{10,... | collective-permute-start | bytes 786440 | tf_op jit(solution)/shard_map/ppermute | solution.py:30
  9.4 12.0 %all-to-all-start = ((bf16[8,16,768]{2,1,0:T(8,128)(2,1)}), bf16[8,16,768]{2,1,0:T(8,128)(2,1)S(1)}, u32[]{:S(2)}, u32[]{:S(2)}) async-start(bf16[8,16,768]{2,1,0:T(8,128)(2,1)} %pad_maximum_fusion.2), calls=%async_computation | async-start | bytes 393216 | tf_op jit(solution)/shard_map/all_to_all | solution.py:467
  15.7 5.8 %collective-permute-start.4 = (bf16[512,256]{1,0:T(8,128)(2,1)S(1)}, bf16[512,256]{1,0:T(8,128)(2,1)S(1)}, u32[]{:S(2)}, u32[]{:S(2)}) collective-permute-start(bf16[512,256]{1,0:T(8,128)(2,1)S(1)} %collective-permute-done.refs_1_), channel_id=1, source_target_pairs={{0,1},{1,0},{2,3},{3,2},{4,5},{5,4},{6,7},{7,6},{8,9},{9,8},{10,11... | collective-permute-start | bytes 786440 | tf_op jit(solution)/shard_map/ppermute | solution.py:30
  30.4 8.5 %collective-permute-start.8 = (bf16[16,4096]{1,0:T(8,128)(2,1)S(1)}, bf16[16,4096]{1,0:T(8,128)(2,1)S(1)}, u32[]{:S(2)}, u32[]{:S(2)}) collective-permute-start(bf16[16,4096]{1,0:T(8,128)(2,1)S(1)} %get-tuple-element.56), channel_id=1, source_target_pairs={{0,4},{1,5},{2,6},{3,7},{4,0},{5,1},{6,2},{7,3},{8,12},{9,13},{10,... | collective-permute-start | bytes 393224 | tf_op jit(solution)/shard_map/ppermute | solution.py:30
  33.0 7.3 %collective-permute-start.10 = (bf16[16,4096]{1,0:T(8,128)(2,1)S(1)}, bf16[16,4096]{1,0:T(8,128)(2,1)S(1)}, u32[]{:S(2)}, u32[]{:S(2)}) collective-permute-start(bf16[16,4096]{1,0:T(8,128)(2,1)S(1)} %get-tuple-element.57), channel_id=1, source_target_pairs={{0,6},{1,7},{2,4},{3,5},{4,2},{5,3},{6,0},{7,1},{8,14},{9,15},{10,... | collective-permute-start | bytes 393224 | tf_op jit(solution)/shard_map/ppermute | solution.py:30
  33.0 7.9 %collective-permute-start.9 = (bf16[16,4096]{1,0:T(8,128)(2,1)S(1)}, bf16[16,4096]{1,0:T(8,128)(2,1)S(1)}, u32[]{:S(2)}, u32[]{:S(2)}) collective-permute-start(bf16[16,4096]{1,0:T(8,128)(2,1)S(1)} %get-tuple-element.58), channel_id=1, source_target_pairs={{0,2},{1,3},{2,0},{3,1},{4,6},{5,7},{6,4},{7,5},{8,10},{9,11},{10,... | collective-permute-start | bytes 393224 | tf_op jit(solution)/shard_map/ppermute | solution.py:30
  42.9 6.8 %collective-permute-start.17 = (bf16[16,2176]{1,0:T(8,128)(2,1)S(1)}, bf16[16,2176]{1,0:T(8,128)(2,1)S(1)}, u32[]{:S(2)}, u32[]{:S(2)}) collective-permute-start(bf16[16,2176]{1,0:T(8,128)(2,1)S(1)} %pad_maximum_fusion.3), channel_id=1, source_target_pairs={{0,24},{8,16},{16,8},{24,0},{1,25},{9,17},{17,9},{25,1},{2,26},{10... | collective-permute-start | bytes 208904 | tf_op jit(solution)/shard_map/ppermute | solution.py:35
  52.1 11.6 %collective-permute-start.20 = (bf16[64,2176]{1,0:T(8,128)(2,1)S(1)}, bf16[64,2176]{1,0:T(8,128)(2,1)S(1)}, u32[]{:S(2)}, u32[]{:S(2)}) collective-permute-start(bf16[64,2176]{1,0:T(8,128)(2,1)S(1)} %pad_maximum_fusion.refs_0_), channel_id=1, source_target_pairs={{0,2},{1,3},{2,0},{3,1},{4,6},{5,7},{6,4},{7,5},{8,10},{9,11},{10,... | collective-permute-start | bytes 835592 | tf_op jit(solution)/shard_map/ppermute | solution.py:30
  52.7 11.6 %collective-permute-start.19 = (bf16[64,2176]{1,0:T(8,128)(2,1)S(1)}, bf16[64,2176]{1,0:T(8,128)(2,1)S(1)}, u32[]{:S(2)}, u32[]{:S(2)}) collective-permute-start(bf16[64,2176]{1,0:T(8,128)(2,1)S(1)} %pad_maximum_fusion.refs_0_), channel_id=1, source_target_pairs={{0,4},{1,5},{2,6},{3,7},{4,0},{5,1},{6,2},{7,3},{8,12},{9,13},{10,... | collective-permute-start | bytes 835592 | tf_op jit(solution)/shard_map/ppermute | solution.py:30
  53.8 12.7 %collective-permute-start.18 = (bf16[64,2176]{1,0:T(8,128)(2,1)S(1)}, bf16[64,2176]{1,0:T(8,128)(2,1)S(1)}, u32[]{:S(2)}, u32[]{:S(2)}) collective-permute-start(bf16[64,2176]{1,0:T(8,128)(2,1)S(1)} %pad_maximum_fusion.refs_0_), channel_id=1, source_target_pairs={{0,6},{1,7},{2,4},{3,5},{4,2},{5,3},{6,0},{7,1},{8,14},{9,15},{10,... | collective-permute-start | bytes 835592 | tf_op jit(solution)/shard_map/ppermute | solution.py:30
  55.7 6.8 %collective-permute-start.13 = (bf16[16,2048]{1,0:T(8,128)(2,1)S(1)}, bf16[16,2048]{1,0:T(8,128)(2,1)S(1)}, u32[]{:S(2)}, u32[]{:S(2)}) collective-permute-start(bf16[16,2048]{1,0:T(8,128)(2,1)S(1)} %get-tuple-element.68), channel_id=1, source_target_pairs={{0,24},{8,16},{16,8},{24,0},{1,25},{9,17},{17,9},{25,1},{2,26},{10... | collective-permute-start | bytes 196616 | tf_op jit(solution)/shard_map/ppermute | solution.py:35
  63.7 5.7 %collective-permute-start.24 = (bf16[64,2176]{1,0:T(8,128)(2,1)S(1)}, bf16[64,2176]{1,0:T(8,128)(2,1)S(1)}, u32[]{:S(2)}, u32[]{:S(2)}) collective-permute-start(bf16[64,2176]{1,0:T(8,128)(2,1)S(1)} %collective-permute-done.20.refs_3_), channel_id=1, source_target_pairs={{0,1},{1,0},{2,3},{3,2},{4,5},{5,4},{6,7},{7,6},{8,9},{9,8},{10,11... | collective-permute-start | bytes 835592 | tf_op jit(solution)/shard_map/ppermute | solution.py:30
  64.2 6.0 %collective-permute-start.23 = (bf16[64,2176]{1,0:T(8,128)(2,1)S(1)}, bf16[64,2176]{1,0:T(8,128)(2,1)S(1)}, u32[]{:S(2)}, u32[]{:S(2)}) collective-permute-start(bf16[64,2176]{1,0:T(8,128)(2,1)S(1)} %collective-permute-done.19.refs_2_), channel_id=1, source_target_pairs={{0,1},{1,0},{2,3},{3,2},{4,5},{5,4},{6,7},{7,6},{8,9},{9,8},{10,11... | collective-permute-start | bytes 835592 | tf_op jit(solution)/shard_map/ppermute | solution.py:30
  66.7 13.8 %collective-permute-start.26 = (bf16[64,2048]{1,0:T(8,128)(2,1)S(1)}, bf16[64,2048]{1,0:T(8,128)(2,1)S(1)}, u32[]{:S(2)}, u32[]{:S(2)}) collective-permute-start(bf16[64,2048]{1,0:T(8,128)(2,1)S(1)} %pad_maximum_fusion.1.refs_0_), channel_id=1, source_target_pairs={{0,2},{1,3},{2,0},{3,1},{4,6},{5,7},{6,4},{7,5},{8,10},{9,11},{10,... | collective-permute-start | bytes 786440 | tf_op jit(solution)/shard_map/ppermute | solution.py:30
  68.4 13.6 %collective-permute-start.25 = (bf16[64,2048]{1,0:T(8,128)(2,1)S(1)}, bf16[64,2048]{1,0:T(8,128)(2,1)S(1)}, u32[]{:S(2)}, u32[]{:S(2)}) collective-permute-start(bf16[64,2048]{1,0:T(8,128)(2,1)S(1)} %pad_maximum_fusion.1.refs_0_), channel_id=1, source_target_pairs={{0,4},{1,5},{2,6},{3,7},{4,0},{5,1},{6,2},{7,3},{8,12},{9,13},{10,... | collective-permute-start | bytes 786440 | tf_op jit(solution)/shard_map/ppermute | solution.py:30
  69.5 12.5 %collective-permute-start.14 = (bf16[64,2048]{1,0:T(8,128)(2,1)S(1)}, bf16[64,2048]{1,0:T(8,128)(2,1)S(1)}, u32[]{:S(2)}, u32[]{:S(2)}) collective-permute-start(bf16[64,2048]{1,0:T(8,128)(2,1)S(1)} %pad_maximum_fusion.1.refs_0_), channel_id=1, source_target_pairs={{0,6},{1,7},{2,4},{3,5},{4,2},{5,3},{6,0},{7,1},{8,14},{9,15},{10,... | collective-permute-start | bytes 786440 | tf_op jit(solution)/shard_map/ppermute | solution.py:30
  70.3 12.2 %collective-permute-start.27 = (bf16[64,2048]{1,0:T(8,128)(2,1)S(1)}, bf16[64,2048]{1,0:T(8,128)(2,1)S(1)}, u32[]{:S(2)}, u32[]{:S(2)}) collective-permute-start(bf16[64,2048]{1,0:T(8,128)(2,1)S(1)} %pad_maximum_fusion.1.refs_0_), channel_id=1, source_target_pairs={{0,1},{1,0},{2,3},{3,2},{4,5},{5,4},{6,7},{7,6},{8,9},{9,8},{10,11... | collective-permute-start | bytes 786440 | tf_op jit(solution)/shard_map/ppermute | solution.py:30
  97.1 8.4 %collective-permute-start.33 = (bf16[64,2048]{1,0:T(8,128)(2,1)S(1)}, bf16[64,2048]{1,0:T(8,128)(2,1)S(1)}, u32[]{:S(2)}, u32[]{:S(2)}) collective-permute-start(bf16[64,2048]{1,0:T(8,128)(2,1)S(1)} %add_convert_fusion.4), channel_id=1, source_target_pairs={{0,2},{1,3},{2,0},{3,1},{4,6},{5,7},{6,4},{7,5},{8,10},{9,11},{10,... | collective-permute-start | bytes 786440 | tf_op jit(solution)/shard_map/ppermute | solution.py:30
  99.4 8.7 %collective-permute-start.34 = (bf16[64,2048]{1,0:T(8,128)(2,1)S(1)}, bf16[64,2048]{1,0:T(8,128)(2,1)S(1)}, u32[]{:S(2)}, u32[]{:S(2)}) collective-permute-start(bf16[64,2048]{1,0:T(8,128)(2,1)S(1)} %get-tuple-element.53), channel_id=1, source_target_pairs={{0,4},{1,5},{2,6},{3,7},{4,0},{5,1},{6,2},{7,3},{8,12},{9,13},{10,... | collective-permute-start | bytes 786440 | tf_op jit(solution)/shard_map/ppermute | solution.py:30
  108.1 7.8 %collective-permute-start.35 = (bf16[64,2048]{1,0:T(8,128)(2,1)S(1)}, bf16[64,2048]{1,0:T(8,128)(2,1)S(1)}, u32[]{:S(2)}, u32[]{:S(2)}) collective-permute-start(bf16[64,2048]{1,0:T(8,128)(2,1)S(1)} %get-tuple-element.43), channel_id=1, source_target_pairs={{0,2},{1,3},{2,0},{3,1},{4,6},{5,7},{6,4},{7,5},{8,10},{9,11},{10,... | collective-permute-start | bytes 786440 | tf_op jit(solution)/shard_map/ppermute | solution.py:30
  109.0 7.5 %collective-permute-start.36 = (bf16[64,2048]{1,0:T(8,128)(2,1)S(1)}, bf16[64,2048]{1,0:T(8,128)(2,1)S(1)}, u32[]{:S(2)}, u32[]{:S(2)}) collective-permute-start(bf16[64,2048]{1,0:T(8,128)(2,1)S(1)} %get-tuple-element.44), channel_id=1, source_target_pairs={{0,4},{1,5},{2,6},{3,7},{4,0},{5,1},{6,2},{7,3},{8,12},{9,13},{10,... | collective-permute-start | bytes 786440 | tf_op jit(solution)/shard_map/ppermute | solution.py:30
  116.6 6.6 %collective-permute-start.40 = (bf16[64,2048]{1,0:T(8,128)(2,1)S(1)}, bf16[64,2048]{1,0:T(8,128)(2,1)S(1)}, u32[]{:S(2)}, u32[]{:S(2)}) collective-permute-start(bf16[64,2048]{1,0:T(8,128)(2,1)S(1)} %add_convert_fusion.1), channel_id=1, source_target_pairs={{0,2},{1,3},{2,0},{3,1},{4,6},{5,7},{6,4},{7,5},{8,10},{9,11},{10,... | collective-permute-start | bytes 786440 | tf_op jit(solution)/shard_map/ppermute | solution.py:30
  117.9 6.4 %collective-permute-start.41 = (bf16[64,2048]{1,0:T(8,128)(2,1)S(1)}, bf16[64,2048]{1,0:T(8,128)(2,1)S(1)}, u32[]{:S(2)}, u32[]{:S(2)}) collective-permute-start(bf16[64,2048]{1,0:T(8,128)(2,1)S(1)} %get-tuple-element.47), channel_id=1, source_target_pairs={{0,4},{1,5},{2,6},{3,7},{4,0},{5,1},{6,2},{7,3},{8,12},{9,13},{10,... | collective-permute-start | bytes 786440 | tf_op jit(solution)/shard_map/ppermute | solution.py:30
  119.0 7.6 %collective-permute-start.37 = (bf16[16,2048]{1,0:T(8,128)(2,1)S(1)}, bf16[16,2048]{1,0:T(8,128)(2,1)S(1)}, u32[]{:S(2)}, u32[]{:S(2)}) collective-permute-start(bf16[16,2048]{1,0:T(8,128)(2,1)S(1)} %get-tuple-element.61), channel_id=1, source_target_pairs={{0,8},{8,0},{16,24},{24,16},{1,9},{9,1},{17,25},{25,17},{2,10},{10... | collective-permute-start | bytes 196616 | tf_op jit(solution)/shard_map/ppermute | solution.py:35
  119.1 8.9 %collective-permute-start.39 = (bf16[16,2048]{1,0:T(8,128)(2,1)S(1)}, bf16[16,2048]{1,0:T(8,128)(2,1)S(1)}, u32[]{:S(2)}, u32[]{:S(2)}) collective-permute-start(bf16[16,2048]{1,0:T(8,128)(2,1)S(1)} %get-tuple-element.62), channel_id=1, source_target_pairs={{0,24},{8,16},{16,8},{24,0},{1,25},{9,17},{17,9},{25,1},{2,26},{10... | collective-permute-start | bytes 196616 | tf_op jit(solution)/shard_map/ppermute | solution.py:35
  121.6 7.9 %collective-permute-start.38 = (bf16[16,2048]{1,0:T(8,128)(2,1)S(1)}, bf16[16,2048]{1,0:T(8,128)(2,1)S(1)}, u32[]{:S(2)}, u32[]{:S(2)}) collective-permute-start(bf16[16,2048]{1,0:T(8,128)(2,1)S(1)} %get-tuple-element.63), channel_id=1, source_target_pairs={{0,16},{8,24},{16,0},{24,8},{1,17},{9,25},{17,1},{25,9},{2,18},{10... | collective-permute-start | bytes 196616 | tf_op jit(solution)/shard_map/ppermute | solution.py:35
  124.5 5.6 %collective-permute-start.42 = (bf16[16,2048]{1,0:T(8,128)(2,1)S(1)}, bf16[16,2048]{1,0:T(8,128)(2,1)S(1)}, u32[]{:S(2)}, u32[]{:S(2)}) collective-permute-start(bf16[16,2048]{1,0:T(8,128)(2,1)S(1)} %get-tuple-element.64), channel_id=1, source_target_pairs={{0,8},{8,0},{16,24},{24,16},{1,9},{9,1},{17,25},{25,17},{2,10},{10... | collective-permute-start | bytes 196616 | tf_op jit(solution)/shard_map/ppermute | solution.py:35
  124.6 6.2 %collective-permute-start.44 = (bf16[16,2048]{1,0:T(8,128)(2,1)S(1)}, bf16[16,2048]{1,0:T(8,128)(2,1)S(1)}, u32[]{:S(2)}, u32[]{:S(2)}) collective-permute-start(bf16[16,2048]{1,0:T(8,128)(2,1)S(1)} %get-tuple-element.65), channel_id=1, source_target_pairs={{0,24},{8,16},{16,8},{24,0},{1,25},{9,17},{17,9},{25,1},{2,26},{10... | collective-permute-start | bytes 196616 | tf_op jit(solution)/shard_map/ppermute | solution.py:35
  126.6 6.2 %collective-permute-start.43 = (bf16[16,2048]{1,0:T(8,128)(2,1)S(1)}, bf16[16,2048]{1,0:T(8,128)(2,1)S(1)}, u32[]{:S(2)}, u32[]{:S(2)}) collective-permute-start(bf16[16,2048]{1,0:T(8,128)(2,1)S(1)} %get-tuple-element.66), channel_id=1, source_target_pairs={{0,16},{8,24},{16,0},{24,8},{1,17},{9,25},{17,1},{25,9},{2,18},{10... | collective-permute-start | bytes 196616 | tf_op jit(solution)/shard_map/ppermute | solution.py:35
  (14 other events, 45.7 us)

commit v5 on v4

--- a/solution.py
+++ b/solution.py
@@ -504,12 +504,13 @@
 
     cut = depth // 2
     ring = [near[0]] + ([near[i] for i in (3, 1, 2)] if len(near) == 4 else near[1:])
+    spin = [0] + ([1, 2, 3] if groups == 4 else list(range(1, groups)))
     planes = []
     for chunk in range(2):
         piece = normed[:, chunk * cut : (chunk + 1) * cut]
         if chunk == 0:
             piece = jnp.concatenate([piece, table], axis=1)
-        stack = jnp.concatenate([piece] + [turn(piece, d) for d in range(1, groups)], axis=0)
+        stack = jnp.concatenate([piece] + [turn(piece, d) for d in spin[1:]], axis=0)
         planes.append([stack] + [hop(stack, mask) for mask in ring[1:]])
     full = planes[0] + [hop(p, 1) for p in planes[0]]
     sums = expert_call(full, w_gate, w_up, 0, cut, topk, experts, seats, first=first, w_down=w_down)
@@ -536,9 +537,9 @@
 
     def home(flat):
         result = flat[:own]
-        for d in range(1, groups):
+        for i in range(groups - 1, 0, -1):
             result = result + turn(
-                flat[d * own : (d + 1) * own].astype(jnp.bfloat16), d
+                flat[i * own : (i + 1) * own].astype(jnp.bfloat16), spin[i]
             ).astype(jnp.float32)
         return result.astype(jnp.bfloat16)
 

time: 134 us -> 133 us (level)
  waiting for transfers between devices: 47.6 us -> 44.4 us
  starting transfers between devices: 43.3 us -> 45.2 us
    ppermute x12, waiting for transfers between devices: 15.1 us -> 12.8 us  [turn(): return lax.ppermute(value, 'req', [(i, i ^ step) for i in range(count)])]
    ppermute x12, starting transfers between devices: 14.1 us -> 15.9 us  [turn(): return lax.ppermute(value, 'req', [(i, i ^ step) for i in range(count)])]
  transfers between devices with their start and end apart: 46 -> 46, of which waited for: 29 -> 26; matrix products, arithmetic and copies ran while one was open for 6% -> 6% of each run, Pallas kernels for 10% -> 10%
where the time goes in v5:
time: 133 us; the launch traced here: 132 us
  starting transfers between devices  45.2 us (34%)
  waiting for transfers between devices  44.4 us (33%)
  Pallas kernels  28.7 us (22%)
  other arithmetic  8.09 us (6%)
  local copies, waits for them, and re-layouts  2.21 us (2%)
  matrix products  1.85 us (1%)
  between operations  1.6 us (1%)
    ppermute x33, waiting for transfers between devices, hop(): return lax.ppermute(value, 'seq', [(i, i ^ mask) for i in range(count)])  31.5 us
    ppermute x33, starting transfers between devices, hop(): return lax.ppermute(value, 'seq', [(i, i ^ mask) for i in range(count)])  25.1 us
    pallas_call x2, Pallas kernels, expert_call(): pl.pallas_call(functools.partial(expert_kernel, len(rows), experts, seats...  19.4 us
    ppermute x12, starting transfers between devices, turn(): return lax.ppermute(value, 'req', [(i, i ^ step) for i in range(count)])  15.9 us
    ppermute x12, waiting for transfers between devices, turn(): return lax.ppermute(value, 'req', [(i, i ^ step) for i in range(count)])  12.8 us
    pallas_call x1, Pallas kernels, attend(): pl.pallas_call(functools.partial(attend_kernel, parts, mine), out_shape=(...  6.44 us
    all_to_all x1, starting transfers between devices, body(): lax.all_to_all(packed, 'seq', split_axis=0, concat_axis=0, tiled=True)  4.15 us
    pallas_call x1, Pallas kernels, fall_call(): pl.pallas_call(fall_kernel, out_shape=(shape, shape), in_specs=[full, ful...  2.85 us
  transfers between devices with their start and end apart: 46, of which 26 were waited for; matrix products, arithmetic and copies ran while one was open for 6% of the time, Pallas kernels for 10%

profile of v5, /device:TPU:0, one launch (start us, length us, event | category | flops | bytes accessed | tf_op | source)
XLA Modules:
  0.0 132.1 jit_solution(15923753744077755946)
XLA Ops:
  0.7 1.5 %broadcast_select_fusion = (bf16[512,2,128]{2,1,0:T(2,128)(2,1)S(1)}, bf16[512,2,128]{2,1,0:T(2,128)(2,1)S(1)}) fusion(pred[]{:T(512)S(6)} %eq.58, bf16[512,2,256]{2,1,0:T(2,128)(2,1)} %bitcast.59, pred[]{:T(512)S(6)} %eq.57), kind=kLoop, calls=%fused_computation.22 | loop fusion | flops 262144 | bytes 1048578 | tf_op jit(solution)/shard_map/jit(_where)/select_n | solution.py:450
  2.7 2.6 %collective-permute-start = (bf16[512,256]{1,0:T(8,128)(2,1)S(1)}, bf16[512,256]{1,0:T(8,128)(2,1)S(1)}, u32[]{:S(2)}, u32[]{:S(2)}) collective-permute-start(bf16[512,256]{1,0:T(8,128)(2,1)S(1)} %bitcast.54), channel_id=1, source_target_pairs={{0,2},{1,3},{2,0},{3,1},{4,6},{5,7},{6,4},{7,5},{8,10},{9,11},{10,... | collective-permute-start | bytes 786440 | tf_op jit(solution)/shard_map/ppermute | solution.py:30
  5.3 1.6 %collective-permute-start.2 = (bf16[512,256]{1,0:T(8,128)(2,1)S(1)}, bf16[512,256]{1,0:T(8,128)(2,1)S(1)}, u32[]{:S(2)}, u32[]{:S(2)}) collective-permute-start(bf16[512,256]{1,0:T(8,128)(2,1)S(1)} %bitcast.62), channel_id=1, source_target_pairs={{0,4},{1,5},{2,6},{3,7},{4,0},{5,1},{6,2},{7,3},{8,12},{9,13},{10,... | collective-permute-start | bytes 786440 | tf_op jit(solution)/shard_map/ppermute | solution.py:30
  9.4 4.2 %all-to-all-start = ((bf16[8,16,768]{2,1,0:T(8,128)(2,1)}), bf16[8,16,768]{2,1,0:T(8,128)(2,1)S(1)}, u32[]{:S(2)}, u32[]{:S(2)}) async-start(bf16[8,16,768]{2,1,0:T(8,128)(2,1)} %pad_maximum_fusion.2), calls=%async_computation | async-start | bytes 393216 | tf_op jit(solution)/shard_map/all_to_all | solution.py:467
  16.3 3.7 %collective-permute-done.2.refs_3_ = bf16[512,256]{1,0:T(8,128)(2,1)S(1)} collective-permute-done((bf16[512,256]{1,0:T(8,128)(2,1)S(1)}, bf16[512,256]{1,0:T(8,128)(2,1)S(1)}, u32[]{:S(2)}, u32[]{:S(2)}) %collective-permute-start.2) | collective-permute-done | bytes 262176 | tf_op jit(solution)/shard_map/ppermute | solution.py:30
  21.9 6.4 %shard_map.140 = (bf16[64,4096]{1,0:T(8,128)(2,1)S(1)}, bf16[64,4096]{1,0:T(8,128)(2,1)S(1)}) custom-call(s32[8]{0:T(128)S(1)} %broadcast_subtract_fusion.valid_ref, bf16[128,128]{1,0:T(8,128)(2,1)S(1)} %fusion.14.perm_ref, bf16[128,768]{1,0:T(8,128)(2,1)S(1)} %bitcast.56, bf16[128,128]{1,0:T(8,128)(2,1)S(1)} %fusion.6.mask_ref, ...), custom_call_target="tpu_custom_call" | custom-call | flops 1644167168 | bytes 7405568 | tf_op jit(solution)/shard_map/pallas_call | solution.py:115
  28.6 1.8 %collective-permute-done.7 = bf16[64,4096]{1,0:T(8,128)(2,1)S(1)} collective-permute-done((bf16[64,4096]{1,0:T(8,128)(2,1)S(1)}, bf16[64,4096]{1,0:T(8,128)(2,1)S(1)}, u32[]{:S(2)}, u32[]{:S(2)}) %collective-permute-start.7) | collective-permute-done | bytes 524320 | tf_op jit(solution)/shard_map/ppermute | solution.py:30
  30.4 2.5 %collective-permute-start.8 = (bf16[16,4096]{1,0:T(8,128)(2,1)S(1)}, bf16[16,4096]{1,0:T(8,128)(2,1)S(1)}, u32[]{:S(2)}, u32[]{:S(2)}) collective-permute-start(bf16[16,4096]{1,0:T(8,128)(2,1)S(1)} %get-tuple-element.56), channel_id=1, source_target_pairs={{0,4},{1,5},{2,6},{3,7},{4,0},{5,1},{6,2},{7,3},{8,12},{9,13},{10,... | collective-permute-start | bytes 393224 | tf_op jit(solution)/shard_map/ppermute | solution.py:30
  33.0 1.5 %collective-permute-start.9 = (bf16[16,4096]{1,0:T(8,128)(2,1)S(1)}, bf16[16,4096]{1,0:T(8,128)(2,1)S(1)}, u32[]{:S(2)}, u32[]{:S(2)}) collective-permute-start(bf16[16,4096]{1,0:T(8,128)(2,1)S(1)} %get-tuple-element.58), channel_id=1, source_target_pairs={{0,2},{1,3},{2,0},{3,1},{4,6},{5,7},{6,4},{7,5},{8,10},{9,11},{10,... | collective-permute-start | bytes 393224 | tf_op jit(solution)/shard_map/ppermute | solution.py:30
  36.8 2.2 %collective-permute-done.8 = bf16[16,4096]{1,0:T(8,128)(2,1)S(1)} collective-permute-done((bf16[16,4096]{1,0:T(8,128)(2,1)S(1)}, bf16[16,4096]{1,0:T(8,128)(2,1)S(1)}, u32[]{:S(2)}, u32[]{:S(2)}) %collective-permute-start.8) | collective-permute-done | bytes 131104 | tf_op jit(solution)/shard_map/ppermute | solution.py:30
  38.9 1.3 %collective-permute-done.10 = bf16[16,4096]{1,0:T(8,128)(2,1)S(1)} collective-permute-done((bf16[16,4096]{1,0:T(8,128)(2,1)S(1)}, bf16[16,4096]{1,0:T(8,128)(2,1)S(1)}, u32[]{:S(2)}, u32[]{:S(2)}) %collective-permute-start.10) | collective-permute-done | bytes 131104 | tf_op jit(solution)/shard_map/ppermute | solution.py:30
  40.9 1.7 %fusion.10 = (bf16[16,4096]{1,0:T(8,128)(2,1)S(1)}, bf16[16,4096]{1,0:T(8,128)(2,1)}) fusion(bf16[1,16,4096]{2,1,0:T(8,128)(2,1)} %param.18, bf16[16,4096]{1,0:T(8,128)(2,1)S(1)} %collective-permute-done.10, bf16[16,4096]{1,0:T(8,128)(2,1)S(1)} %collective-permute-done.9, bf16[16,4096]{1,0:T(8,128)(2,1)S(1)} %collective-permute-done.8, ...), kind=kLoop, calls=%fused_computation.34 | loop fusion | flops 917504 | bytes 1048576 | tf_op jit(solution)/shard_map/convert_element_type | solution.py:489
  42.9 3.7 %collective-permute-start.17 = (bf16[16,2176]{1,0:T(8,128)(2,1)S(1)}, bf16[16,2176]{1,0:T(8,128)(2,1)S(1)}, u32[]{:S(2)}, u32[]{:S(2)}) collective-permute-start(bf16[16,2176]{1,0:T(8,128)(2,1)S(1)} %pad_maximum_fusion.3), channel_id=1, source_target_pairs={{0,24},{8,16},{16,8},{24,0},{1,25},{9,17},{17,9},{25,1},{2,26},{10... | collective-permute-start | bytes 208904 | tf_op jit(solution)/shard_map/ppermute | solution.py:35
  47.3 2.3 %collective-permute-done.17 = bf16[16,2176]{1,0:T(8,128)(2,1)S(1)} collective-permute-done((bf16[16,2176]{1,0:T(8,128)(2,1)S(1)}, bf16[16,2176]{1,0:T(8,128)(2,1)S(1)}, u32[]{:S(2)}, u32[]{:S(2)}) %collective-permute-start.17) | collective-permute-done | bytes 69664 | tf_op jit(solution)/shard_map/ppermute | solution.py:35
  49.6 2.4 %collective-permute-done.16 = bf16[16,2176]{1,0:T(8,128)(2,1)S(1)} collective-permute-done((bf16[16,2176]{1,0:T(8,128)(2,1)S(1)}, bf16[16,2176]{1,0:T(8,128)(2,1)S(1)}, u32[]{:S(2)}, u32[]{:S(2)}) %collective-permute-start.16) | collective-permute-done | bytes 69664 | tf_op jit(solution)/shard_map/ppermute | solution.py:35
  53.8 1.8 %collective-permute-start.18 = (bf16[64,2176]{1,0:T(8,128)(2,1)S(1)}, bf16[64,2176]{1,0:T(8,128)(2,1)S(1)}, u32[]{:S(2)}, u32[]{:S(2)}) collective-permute-start(bf16[64,2176]{1,0:T(8,128)(2,1)S(1)} %pad_maximum_fusion.refs_0_), channel_id=1, source_target_pairs={{0,6},{1,7},{2,4},{3,5},{4,2},{5,3},{6,0},{7,1},{8,14},{9,15},{10,... | collective-permute-start | bytes 835592 | tf_op jit(solution)/shard_map/ppermute | solution.py:30
  55.7 2.5 %collective-permute-start.13 = (bf16[16,2048]{1,0:T(8,128)(2,1)S(1)}, bf16[16,2048]{1,0:T(8,128)(2,1)S(1)}, u32[]{:S(2)}, u32[]{:S(2)}) collective-permute-start(bf16[16,2048]{1,0:T(8,128)(2,1)S(1)} %get-tuple-element.68), channel_id=1, source_target_pairs={{0,24},{8,16},{16,8},{24,0},{1,25},{9,17},{17,9},{25,1},{2,26},{10... | collective-permute-start | bytes 196616 | tf_op jit(solution)/shard_map/ppermute | solution.py:35
  58.2 4.2 %collective-permute-done.13 = bf16[16,2048]{1,0:T(8,128)(2,1)S(1)} collective-permute-done((bf16[16,2048]{1,0:T(8,128)(2,1)S(1)}, bf16[16,2048]{1,0:T(8,128)(2,1)S(1)}, u32[]{:S(2)}, u32[]{:S(2)}) %collective-permute-start.13) | collective-permute-done | bytes 65568 | tf_op jit(solution)/shard_map/ppermute | solution.py:35
  64.3 2.2 %collective-permute-done.18.refs_1_ = bf16[64,2176]{1,0:T(8,128)(2,1)S(1)} collective-permute-done((bf16[64,2176]{1,0:T(8,128)(2,1)S(1)}, bf16[64,2176]{1,0:T(8,128)(2,1)S(1)}, u32[]{:S(2)}, u32[]{:S(2)}) %collective-permute-start.18) | collective-permute-done | bytes 278560 | tf_op jit(solution)/shard_map/ppermute | solution.py:30
  66.7 1.7 %collective-permute-start.26 = (bf16[64,2048]{1,0:T(8,128)(2,1)S(1)}, bf16[64,2048]{1,0:T(8,128)(2,1)S(1)}, u32[]{:S(2)}, u32[]{:S(2)}) collective-permute-start(bf16[64,2048]{1,0:T(8,128)(2,1)S(1)} %pad_maximum_fusion.1.refs_0_), channel_id=1, source_target_pairs={{0,2},{1,3},{2,0},{3,1},{4,6},{5,7},{6,4},{7,5},{8,10},{9,11},{10,... | collective-permute-start | bytes 786440 | tf_op jit(solution)/shard_map/ppermute | solution.py:30
  70.3 10.2 %shard_map.141 = (f32[16,128,128]{2,1,0:T(8,128)S(1)}, f32[16,128,128]{2,1,0:T(8,128)S(1)}, bf16[512,256]{1,0:T(8,128)(2,1)S(1)}, f32[2,128,1]{2,1,0:T(8,128)S(1)}, bf16[12,128,4096]{2,1,0:T(8,128)(2,1)S(1)}) custom-call(bf16[64,2176]{1,0:T(8,128)(2,1)S(1)} %pad_maximum_fusion.refs_0_, bf16[64,2176]{1,0:T(8,128)(2,1)S(1)} %collective-permute-done.18.refs_1_, ...), custom_call_target="tpu_custom_call" | custom-call | flops 2684354560 | bytes 31457280 | tf_op jit(solution)/shard_map/pallas_call | solution.py:401
  80.5 1.5 %collective-permute-done.25.refs_2_ = bf16[64,2048]{1,0:T(8,128)(2,1)S(1)} collective-permute-done((bf16[64,2048]{1,0:T(8,128)(2,1)S(1)}, bf16[64,2048]{1,0:T(8,128)(2,1)S(1)}, u32[]{:S(2)}, u32[]{:S(2)}) %collective-permute-start.25) | collective-permute-done | bytes 262176 | tf_op jit(solution)/shard_map/ppermute | solution.py:30
  84.2 9.3 %shard_map.142 = (bf16[256,2048]{1,0:T(8,128)(2,1)S(1)}, bf16[256,2048]{1,0:T(8,128)(2,1)S(1)}, bf16[256,1024]{1,0:T(8,128)(2,1)S(1)}) custom-call(bf16[64,2048]{1,0:T(8,128)(2,1)S(1)} %pad_maximum_fusion.1.refs_0_, bf16[64,2048]{1,0:T(8,128)(2,1)S(1)} %collective-permute-done.14.refs_1_, bf16[64,2048]{1,0:T(8,128)(2,1)S(1)} %collective-permute-done.25.refs_2_, ...), custom_call_target="tpu_custom_call" | custom-call | flops 4294967296 | bytes 27262976 | tf_op jit(solution)/shard_map/pallas_call | solution.py:401
  93.7 2.9 %shard_map.143 = (bf16[256,2048]{1,0:T(8,128)(2,1)S(1)}, bf16[256,2048]{1,0:T(8,128)(2,1)S(1)}) custom-call(bf16[256,1024]{1,0:T(8,128)(2,1)S(1)} %get-tuple-element.35.hidden_ref, bf16[12,128,4096]{2,1,0:T(8,128)(2,1)S(1)} %get-tuple-element.34.refs_14_.ready_ref, bf16[512,256]{1,0:T(8,128)(2,1)S(1)} %get-tuple-element.32.refs_12_.back_ref, ...), custom_call_target="tpu_custom_call" | custom-call | flops 2684354560 | bytes 2097152 | tf_op jit(solution)/shard_map/pallas_call | solution.py:342
  97.9 1.4 %collective-permute-done.32 = bf16[256,2048]{1,0:T(8,128)(2,1)S(1)} collective-permute-done((bf16[256,2048]{1,0:T(8,128)(2,1)S(1)}, bf16[256,2048]{1,0:T(8,128)(2,1)S(1)}, u32[]{:S(2)}, u32[]{:S(2)}) %collective-permute-start.32) | collective-permute-done | bytes 1048608 | tf_op jit(solution)/shard_map/ppermute | solution.py:30
  100.6 4.9 %collective-permute-done.33 = bf16[64,2048]{1,0:T(8,128)(2,1)S(1)} collective-permute-done((bf16[64,2048]{1,0:T(8,128)(2,1)S(1)}, bf16[64,2048]{1,0:T(8,128)(2,1)S(1)}, u32[]{:S(2)}, u32[]{:S(2)}) %collective-permute-start.33) | collective-permute-done | bytes 262176 | tf_op jit(solution)/shard_map/ppermute | solution.py:30
  105.7 2.4 %collective-permute-done.34 = bf16[64,2048]{1,0:T(8,128)(2,1)S(1)} collective-permute-done((bf16[64,2048]{1,0:T(8,128)(2,1)S(1)}, bf16[64,2048]{1,0:T(8,128)(2,1)S(1)}, u32[]{:S(2)}, u32[]{:S(2)}) %collective-permute-start.34) | collective-permute-done | bytes 262176 | tf_op jit(solution)/shard_map/ppermute | solution.py:30
  110.0 5.9 %collective-permute-done.35 = bf16[64,2048]{1,0:T(8,128)(2,1)S(1)} collective-permute-done((bf16[64,2048]{1,0:T(8,128)(2,1)S(1)}, bf16[64,2048]{1,0:T(8,128)(2,1)S(1)}, u32[]{:S(2)}, u32[]{:S(2)}) %collective-permute-start.35) | collective-permute-done | bytes 262176 | tf_op jit(solution)/shard_map/ppermute | solution.py:30
  119.0 1.4 %collective-permute-start.37 = (bf16[16,2048]{1,0:T(8,128)(2,1)S(1)}, bf16[16,2048]{1,0:T(8,128)(2,1)S(1)}, u32[]{:S(2)}, u32[]{:S(2)}) collective-permute-start(bf16[16,2048]{1,0:T(8,128)(2,1)S(1)} %get-tuple-element.61), channel_id=1, source_target_pairs={{0,24},{8,16},{16,8},{24,0},{1,25},{9,17},{17,9},{25,1},{2,26},{10... | collective-permute-start | bytes 196616 | tf_op jit(solution)/shard_map/ppermute | solution.py:35
  120.7 2.8 %collective-permute-start.38 = (bf16[16,2048]{1,0:T(8,128)(2,1)S(1)}, bf16[16,2048]{1,0:T(8,128)(2,1)S(1)}, u32[]{:S(2)}, u32[]{:S(2)}) collective-permute-start(bf16[16,2048]{1,0:T(8,128)(2,1)S(1)} %get-tuple-element.63), channel_id=1, source_target_pairs={{0,16},{8,24},{16,0},{24,8},{1,17},{9,25},{17,1},{25,9},{2,18},{10... | collective-permute-start | bytes 196616 | tf_op jit(solution)/shard_map/ppermute | solution.py:35
  125.7 3.2 %collective-permute-start.43 = (bf16[16,2048]{1,0:T(8,128)(2,1)S(1)}, bf16[16,2048]{1,0:T(8,128)(2,1)S(1)}, u32[]{:S(2)}, u32[]{:S(2)}) collective-permute-start(bf16[16,2048]{1,0:T(8,128)(2,1)S(1)} %get-tuple-element.66), channel_id=1, source_target_pairs={{0,16},{8,24},{16,0},{24,8},{1,17},{9,25},{17,1},{25,9},{2,18},{10... | collective-permute-start | bytes 196616 | tf_op jit(solution)/shard_map/ppermute | solution.py:35
  129.0 1.7 %collective-permute-done.42 = bf16[16,2048]{1,0:T(8,128)(2,1)S(1)} collective-permute-done((bf16[16,2048]{1,0:T(8,128)(2,1)S(1)}, bf16[16,2048]{1,0:T(8,128)(2,1)S(1)}, u32[]{:S(2)}, u32[]{:S(2)}) %collective-permute-start.42) | collective-permute-done | bytes 65568 | tf_op jit(solution)/shard_map/ppermute | solution.py:35
  (113 shorter events, 31.2 us)
Async XLA Ops:
  2.2 19.3 %collective-permute-start.3 = (bf16[512,256]{1,0:T(8,128)(2,1)S(1)}, bf16[512,256]{1,0:T(8,128)(2,1)S(1)}, u32[]{:S(2)}, u32[]{:S(2)}) collective-permute-start(bf16[512,256]{1,0:T(8,128)(2,1)S(1)} %bitcast.53), channel_id=1, source_target_pairs={{0,1},{1,0},{2,3},{3,2},{4,5},{5,4},{6,7},{7,6},{8,9},{9,8},{10,11... | collective-permute-start | bytes 786440 | tf_op jit(solution)/shard_map/ppermute | solution.py:30
  2.7 13.0 %collective-permute-start = (bf16[512,256]{1,0:T(8,128)(2,1)S(1)}, bf16[512,256]{1,0:T(8,128)(2,1)S(1)}, u32[]{:S(2)}, u32[]{:S(2)}) collective-permute-start(bf16[512,256]{1,0:T(8,128)(2,1)S(1)} %bitcast.54), channel_id=1, source_target_pairs={{0,2},{1,3},{2,0},{3,1},{4,6},{5,7},{6,4},{7,5},{8,10},{9,11},{10,... | collective-permute-start | bytes 786440 | tf_op jit(solution)/shard_map/ppermute | solution.py:30
  5.3 14.7 %collective-permute-start.2 = (bf16[512,256]{1,0:T(8,128)(2,1)S(1)}, bf16[512,256]{1,0:T(8,128)(2,1)S(1)}, u32[]{:S(2)}, u32[]{:S(2)}) collective-permute-start(bf16[512,256]{1,0:T(8,128)(2,1)S(1)} %bitcast.62), channel_id=1, source_target_pairs={{0,4},{1,5},{2,6},{3,7},{4,0},{5,1},{6,2},{7,3},{8,12},{9,13},{10,... | collective-permute-start | bytes 786440 | tf_op jit(solution)/shard_map/ppermute | solution.py:30
  6.9 13.1 %collective-permute-start.1 = (bf16[512,256]{1,0:T(8,128)(2,1)S(1)}, bf16[512,256]{1,0:T(8,128)(2,1)S(1)}, u32[]{:S(2)}, u32[]{:S(2)}) collective-permute-start(bf16[512,256]{1,0:T(8,128)(2,1)S(1)} %bitcast.63), channel_id=1, source_target_pairs={{0,6},{1,7},{2,4},{3,5},{4,2},{5,3},{6,0},{7,1},{8,14},{9,15},{10,... | collective-permute-start | bytes 786440 | tf_op jit(solution)/shard_map/ppermute | solution.py:30
  9.4 12.0 %all-to-all-start = ((bf16[8,16,768]{2,1,0:T(8,128)(2,1)}), bf16[8,16,768]{2,1,0:T(8,128)(2,1)S(1)}, u32[]{:S(2)}, u32[]{:S(2)}) async-start(bf16[8,16,768]{2,1,0:T(8,128)(2,1)} %pad_maximum_fusion.2), calls=%async_computation | async-start | bytes 393216 | tf_op jit(solution)/shard_map/all_to_all | solution.py:467
  15.7 5.8 %collective-permute-start.4 = (bf16[512,256]{1,0:T(8,128)(2,1)S(1)}, bf16[512,256]{1,0:T(8,128)(2,1)S(1)}, u32[]{:S(2)}, u32[]{:S(2)}) collective-permute-start(bf16[512,256]{1,0:T(8,128)(2,1)S(1)} %collective-permute-done.refs_1_), channel_id=1, source_target_pairs={{0,1},{1,0},{2,3},{3,2},{4,5},{5,4},{6,7},{7,6},{8,9},{9,8},{10,11... | collective-permute-start | bytes 786440 | tf_op jit(solution)/shard_map/ppermute | solution.py:30
  30.4 8.5 %collective-permute-start.8 = (bf16[16,4096]{1,0:T(8,128)(2,1)S(1)}, bf16[16,4096]{1,0:T(8,128)(2,1)S(1)}, u32[]{:S(2)}, u32[]{:S(2)}) collective-permute-start(bf16[16,4096]{1,0:T(8,128)(2,1)S(1)} %get-tuple-element.56), channel_id=1, source_target_pairs={{0,4},{1,5},{2,6},{3,7},{4,0},{5,1},{6,2},{7,3},{8,12},{9,13},{10,... | collective-permute-start | bytes 393224 | tf_op jit(solution)/shard_map/ppermute | solution.py:30
  33.0 7.3 %collective-permute-start.10 = (bf16[16,4096]{1,0:T(8,128)(2,1)S(1)}, bf16[16,4096]{1,0:T(8,128)(2,1)S(1)}, u32[]{:S(2)}, u32[]{:S(2)}) collective-permute-start(bf16[16,4096]{1,0:T(8,128)(2,1)S(1)} %get-tuple-element.57), channel_id=1, source_target_pairs={{0,6},{1,7},{2,4},{3,5},{4,2},{5,3},{6,0},{7,1},{8,14},{9,15},{10,... | collective-permute-start | bytes 393224 | tf_op jit(solution)/shard_map/ppermute | solution.py:30
  33.0 7.9 %collective-permute-start.9 = (bf16[16,4096]{1,0:T(8,128)(2,1)S(1)}, bf16[16,4096]{1,0:T(8,128)(2,1)S(1)}, u32[]{:S(2)}, u32[]{:S(2)}) collective-permute-start(bf16[16,4096]{1,0:T(8,128)(2,1)S(1)} %get-tuple-element.58), channel_id=1, source_target_pairs={{0,2},{1,3},{2,0},{3,1},{4,6},{5,7},{6,4},{7,5},{8,10},{9,11},{10,... | collective-permute-start | bytes 393224 | tf_op jit(solution)/shard_map/ppermute | solution.py:30
  42.9 6.8 %collective-permute-start.17 = (bf16[16,2176]{1,0:T(8,128)(2,1)S(1)}, bf16[16,2176]{1,0:T(8,128)(2,1)S(1)}, u32[]{:S(2)}, u32[]{:S(2)}) collective-permute-start(bf16[16,2176]{1,0:T(8,128)(2,1)S(1)} %pad_maximum_fusion.3), channel_id=1, source_target_pairs={{0,24},{8,16},{16,8},{24,0},{1,25},{9,17},{17,9},{25,1},{2,26},{10... | collective-permute-start | bytes 208904 | tf_op jit(solution)/shard_map/ppermute | solution.py:35
  46.5 5.6 %collective-permute-start.15 = (bf16[16,2176]{1,0:T(8,128)(2,1)S(1)}, bf16[16,2176]{1,0:T(8,128)(2,1)S(1)}, u32[]{:S(2)}, u32[]{:S(2)}) collective-permute-start(bf16[16,2176]{1,0:T(8,128)(2,1)S(1)} %pad_maximum_fusion.3), channel_id=1, source_target_pairs={{0,8},{8,0},{16,24},{24,16},{1,9},{9,1},{17,25},{25,17},{2,10},{10... | collective-permute-start | bytes 208904 | tf_op jit(solution)/shard_map/ppermute | solution.py:35
  52.1 11.6 %collective-permute-start.20 = (bf16[64,2176]{1,0:T(8,128)(2,1)S(1)}, bf16[64,2176]{1,0:T(8,128)(2,1)S(1)}, u32[]{:S(2)}, u32[]{:S(2)}) collective-permute-start(bf16[64,2176]{1,0:T(8,128)(2,1)S(1)} %pad_maximum_fusion.refs_0_), channel_id=1, source_target_pairs={{0,2},{1,3},{2,0},{3,1},{4,6},{5,7},{6,4},{7,5},{8,10},{9,11},{10,... | collective-permute-start | bytes 835592 | tf_op jit(solution)/shard_map/ppermute | solution.py:30
  52.7 11.6 %collective-permute-start.19 = (bf16[64,2176]{1,0:T(8,128)(2,1)S(1)}, bf16[64,2176]{1,0:T(8,128)(2,1)S(1)}, u32[]{:S(2)}, u32[]{:S(2)}) collective-permute-start(bf16[64,2176]{1,0:T(8,128)(2,1)S(1)} %pad_maximum_fusion.refs_0_), channel_id=1, source_target_pairs={{0,4},{1,5},{2,6},{3,7},{4,0},{5,1},{6,2},{7,3},{8,12},{9,13},{10,... | collective-permute-start | bytes 835592 | tf_op jit(solution)/shard_map/ppermute | solution.py:30
  53.8 12.7 %collective-permute-start.18 = (bf16[64,2176]{1,0:T(8,128)(2,1)S(1)}, bf16[64,2176]{1,0:T(8,128)(2,1)S(1)}, u32[]{:S(2)}, u32[]{:S(2)}) collective-permute-start(bf16[64,2176]{1,0:T(8,128)(2,1)S(1)} %pad_maximum_fusion.refs_0_), channel_id=1, source_target_pairs={{0,6},{1,7},{2,4},{3,5},{4,2},{5,3},{6,0},{7,1},{8,14},{9,15},{10,... | collective-permute-start | bytes 835592 | tf_op jit(solution)/shard_map/ppermute | solution.py:30
  55.7 6.8 %collective-permute-start.13 = (bf16[16,2048]{1,0:T(8,128)(2,1)S(1)}, bf16[16,2048]{1,0:T(8,128)(2,1)S(1)}, u32[]{:S(2)}, u32[]{:S(2)}) collective-permute-start(bf16[16,2048]{1,0:T(8,128)(2,1)S(1)} %get-tuple-element.68), channel_id=1, source_target_pairs={{0,24},{8,16},{16,8},{24,0},{1,25},{9,17},{17,9},{25,1},{2,26},{10... | collective-permute-start | bytes 196616 | tf_op jit(solution)/shard_map/ppermute | solution.py:35
  63.7 5.7 %collective-permute-start.24 = (bf16[64,2176]{1,0:T(8,128)(2,1)S(1)}, bf16[64,2176]{1,0:T(8,128)(2,1)S(1)}, u32[]{:S(2)}, u32[]{:S(2)}) collective-permute-start(bf16[64,2176]{1,0:T(8,128)(2,1)S(1)} %collective-permute-done.20.refs_3_), channel_id=1, source_target_pairs={{0,1},{1,0},{2,3},{3,2},{4,5},{5,4},{6,7},{7,6},{8,9},{9,8},{10,11... | collective-permute-start | bytes 835592 | tf_op jit(solution)/shard_map/ppermute | solution.py:30
  64.2 6.0 %collective-permute-start.23 = (bf16[64,2176]{1,0:T(8,128)(2,1)S(1)}, bf16[64,2176]{1,0:T(8,128)(2,1)S(1)}, u32[]{:S(2)}, u32[]{:S(2)}) collective-permute-start(bf16[64,2176]{1,0:T(8,128)(2,1)S(1)} %collective-permute-done.19.refs_2_), channel_id=1, source_target_pairs={{0,1},{1,0},{2,3},{3,2},{4,5},{5,4},{6,7},{7,6},{8,9},{9,8},{10,11... | collective-permute-start | bytes 835592 | tf_op jit(solution)/shard_map/ppermute | solution.py:30
  66.7 13.8 %collective-permute-start.26 = (bf16[64,2048]{1,0:T(8,128)(2,1)S(1)}, bf16[64,2048]{1,0:T(8,128)(2,1)S(1)}, u32[]{:S(2)}, u32[]{:S(2)}) collective-permute-start(bf16[64,2048]{1,0:T(8,128)(2,1)S(1)} %pad_maximum_fusion.1.refs_0_), channel_id=1, source_target_pairs={{0,2},{1,3},{2,0},{3,1},{4,6},{5,7},{6,4},{7,5},{8,10},{9,11},{10,... | collective-permute-start | bytes 786440 | tf_op jit(solution)/shard_map/ppermute | solution.py:30
  68.4 13.6 %collective-permute-start.25 = (bf16[64,2048]{1,0:T(8,128)(2,1)S(1)}, bf16[64,2048]{1,0:T(8,128)(2,1)S(1)}, u32[]{:S(2)}, u32[]{:S(2)}) collective-permute-start(bf16[64,2048]{1,0:T(8,128)(2,1)S(1)} %pad_maximum_fusion.1.refs_0_), channel_id=1, source_target_pairs={{0,4},{1,5},{2,6},{3,7},{4,0},{5,1},{6,2},{7,3},{8,12},{9,13},{10,... | collective-permute-start | bytes 786440 | tf_op jit(solution)/shard_map/ppermute | solution.py:30
  69.5 12.5 %collective-permute-start.14 = (bf16[64,2048]{1,0:T(8,128)(2,1)S(1)}, bf16[64,2048]{1,0:T(8,128)(2,1)S(1)}, u32[]{:S(2)}, u32[]{:S(2)}) collective-permute-start(bf16[64,2048]{1,0:T(8,128)(2,1)S(1)} %pad_maximum_fusion.1.refs_0_), channel_id=1, source_target_pairs={{0,6},{1,7},{2,4},{3,5},{4,2},{5,3},{6,0},{7,1},{8,14},{9,15},{10,... | collective-permute-start | bytes 786440 | tf_op jit(solution)/shard_map/ppermute | solution.py:30
  70.3 12.2 %collective-permute-start.27 = (bf16[64,2048]{1,0:T(8,128)(2,1)S(1)}, bf16[64,2048]{1,0:T(8,128)(2,1)S(1)}, u32[]{:S(2)}, u32[]{:S(2)}) collective-permute-start(bf16[64,2048]{1,0:T(8,128)(2,1)S(1)} %pad_maximum_fusion.1.refs_0_), channel_id=1, source_target_pairs={{0,1},{1,0},{2,3},{3,2},{4,5},{5,4},{6,7},{7,6},{8,9},{9,8},{10,11... | collective-permute-start | bytes 786440 | tf_op jit(solution)/shard_map/ppermute | solution.py:30
  97.1 8.4 %collective-permute-start.33 = (bf16[64,2048]{1,0:T(8,128)(2,1)S(1)}, bf16[64,2048]{1,0:T(8,128)(2,1)S(1)}, u32[]{:S(2)}, u32[]{:S(2)}) collective-permute-start(bf16[64,2048]{1,0:T(8,128)(2,1)S(1)} %add_convert_fusion.4), channel_id=1, source_target_pairs={{0,2},{1,3},{2,0},{3,1},{4,6},{5,7},{6,4},{7,5},{8,10},{9,11},{10,... | collective-permute-start | bytes 786440 | tf_op jit(solution)/shard_map/ppermute | solution.py:30
  99.4 8.7 %collective-permute-start.34 = (bf16[64,2048]{1,0:T(8,128)(2,1)S(1)}, bf16[64,2048]{1,0:T(8,128)(2,1)S(1)}, u32[]{:S(2)}, u32[]{:S(2)}) collective-permute-start(bf16[64,2048]{1,0:T(8,128)(2,1)S(1)} %get-tuple-element.53), channel_id=1, source_target_pairs={{0,4},{1,5},{2,6},{3,7},{4,0},{5,1},{6,2},{7,3},{8,12},{9,13},{10,... | collective-permute-start | bytes 786440 | tf_op jit(solution)/shard_map/ppermute | solution.py:30
  108.1 7.8 %collective-permute-start.35 = (bf16[64,2048]{1,0:T(8,128)(2,1)S(1)}, bf16[64,2048]{1,0:T(8,128)(2,1)S(1)}, u32[]{:S(2)}, u32[]{:S(2)}) collective-permute-start(bf16[64,2048]{1,0:T(8,128)(2,1)S(1)} %get-tuple-element.43), channel_id=1, source_target_pairs={{0,2},{1,3},{2,0},{3,1},{4,6},{5,7},{6,4},{7,5},{8,10},{9,11},{10,... | collective-permute-start | bytes 786440 | tf_op jit(solution)/shard_map/ppermute | solution.py:30
  109.0 7.5 %collective-permute-start.36 = (bf16[64,2048]{1,0:T(8,128)(2,1)S(1)}, bf16[64,2048]{1,0:T(8,128)(2,1)S(1)}, u32[]{:S(2)}, u32[]{:S(2)}) collective-permute-start(bf16[64,2048]{1,0:T(8,128)(2,1)S(1)} %get-tuple-element.44), channel_id=1, source_target_pairs={{0,4},{1,5},{2,6},{3,7},{4,0},{5,1},{6,2},{7,3},{8,12},{9,13},{10,... | collective-permute-start | bytes 786440 | tf_op jit(solution)/shard_map/ppermute | solution.py:30
  116.6 6.9 %collective-permute-start.40 = (bf16[64,2048]{1,0:T(8,128)(2,1)S(1)}, bf16[64,2048]{1,0:T(8,128)(2,1)S(1)}, u32[]{:S(2)}, u32[]{:S(2)}) collective-permute-start(bf16[64,2048]{1,0:T(8,128)(2,1)S(1)} %add_convert_fusion.1), channel_id=1, source_target_pairs={{0,2},{1,3},{2,0},{3,1},{4,6},{5,7},{6,4},{7,5},{8,10},{9,11},{10,... | collective-permute-start | bytes 786440 | tf_op jit(solution)/shard_map/ppermute | solution.py:30
  117.9 6.4 %collective-permute-start.41 = (bf16[64,2048]{1,0:T(8,128)(2,1)S(1)}, bf16[64,2048]{1,0:T(8,128)(2,1)S(1)}, u32[]{:S(2)}, u32[]{:S(2)}) collective-permute-start(bf16[64,2048]{1,0:T(8,128)(2,1)S(1)} %get-tuple-element.47), channel_id=1, source_target_pairs={{0,4},{1,5},{2,6},{3,7},{4,0},{5,1},{6,2},{7,3},{8,12},{9,13},{10,... | collective-permute-start | bytes 786440 | tf_op jit(solution)/shard_map/ppermute | solution.py:30
  119.0 6.7 %collective-permute-start.37 = (bf16[16,2048]{1,0:T(8,128)(2,1)S(1)}, bf16[16,2048]{1,0:T(8,128)(2,1)S(1)}, u32[]{:S(2)}, u32[]{:S(2)}) collective-permute-start(bf16[16,2048]{1,0:T(8,128)(2,1)S(1)} %get-tuple-element.61), channel_id=1, source_target_pairs={{0,24},{8,16},{16,8},{24,0},{1,25},{9,17},{17,9},{25,1},{2,26},{10... | collective-permute-start | bytes 196616 | tf_op jit(solution)/shard_map/ppermute | solution.py:35
  120.4 8.5 %collective-permute-start.39 = (bf16[16,2048]{1,0:T(8,128)(2,1)S(1)}, bf16[16,2048]{1,0:T(8,128)(2,1)S(1)}, u32[]{:S(2)}, u32[]{:S(2)}) collective-permute-start(bf16[16,2048]{1,0:T(8,128)(2,1)S(1)} %get-tuple-element.62), channel_id=1, source_target_pairs={{0,8},{8,0},{16,24},{24,16},{1,9},{9,1},{17,25},{25,17},{2,10},{10... | collective-permute-start | bytes 196616 | tf_op jit(solution)/shard_map/ppermute | solution.py:35
  120.7 8.3 %collective-permute-start.38 = (bf16[16,2048]{1,0:T(8,128)(2,1)S(1)}, bf16[16,2048]{1,0:T(8,128)(2,1)S(1)}, u32[]{:S(2)}, u32[]{:S(2)}) collective-permute-start(bf16[16,2048]{1,0:T(8,128)(2,1)S(1)} %get-tuple-element.63), channel_id=1, source_target_pairs={{0,16},{8,24},{16,0},{24,8},{1,17},{9,25},{17,1},{25,9},{2,18},{10... | collective-permute-start | bytes 196616 | tf_op jit(solution)/shard_map/ppermute | solution.py:35
  124.5 6.2 %collective-permute-start.42 = (bf16[16,2048]{1,0:T(8,128)(2,1)S(1)}, bf16[16,2048]{1,0:T(8,128)(2,1)S(1)}, u32[]{:S(2)}, u32[]{:S(2)}) collective-permute-start(bf16[16,2048]{1,0:T(8,128)(2,1)S(1)} %get-tuple-element.64), channel_id=1, source_target_pairs={{0,24},{8,16},{16,8},{24,0},{1,25},{9,17},{17,9},{25,1},{2,26},{10... | collective-permute-start | bytes 196616 | tf_op jit(solution)/shard_map/ppermute | solution.py:35
  125.7 5.6 %collective-permute-start.43 = (bf16[16,2048]{1,0:T(8,128)(2,1)S(1)}, bf16[16,2048]{1,0:T(8,128)(2,1)S(1)}, u32[]{:S(2)}, u32[]{:S(2)}) collective-permute-start(bf16[16,2048]{1,0:T(8,128)(2,1)S(1)} %get-tuple-element.66), channel_id=1, source_target_pairs={{0,16},{8,24},{16,0},{24,8},{1,17},{9,25},{17,1},{25,9},{2,18},{10... | collective-permute-start | bytes 196616 | tf_op jit(solution)/shard_map/ppermute | solution.py:35
  (14 other events, 45.4 us)

commit v6 on v5

--- a/solution.py
+++ b/solution.py
@@ -440,15 +440,9 @@
     span = kv_cache.shape[1]
     share = parts // KVH
     lane = kv_cache[0]
-    heads = [
-        lane[:, :, h * DH : (h + 1) * DH].reshape(span, 2 * DH) for h in range(KVH)
-    ]
-
     def head_of(device):
-        pick = heads[0]
-        for h in range(1, KVH):
-            pick = jnp.where(device // share == h, heads[h], pick)
-        return pick
+        first = (device // share) * DH
+        return lax.dynamic_slice_in_dim(lane, first, DH, 2).reshape(span, 2 * DH)
 
     same, other = head_of(here), head_of(here ^ (parts // 2))
     turns = [near[0]] + ([near[i] for i in (2, 3, 1)] if len(near) == 4 else near[1:])

time: 133 us -> 133 us (level)
  other arithmetic: 8.09 us -> 6.61 us
  local copies, waits for them, and re-layouts: 2.21 us -> 3.6 us
    select_n x1 -> x0, other arithmetic: 1.48 us -> none  [head_of(): pick = jnp.where(device // share == h, heads[h], pick)]
    dynamic_slice x0 -> x1, local copies, waits for them, and re-layouts: none -> 1.4 us  [head_of(): return lax.dynamic_slice_in_dim(lane, first, DH, 2).reshape(span, 2 * DH)]
where the time goes in v6:
time: 133 us; the launch traced here: 132 us
  starting transfers between devices  45.1 us (34%)
  waiting for transfers between devices  44.5 us (33%)
  Pallas kernels  28.7 us (22%)
  other arithmetic  6.61 us (5%)
  local copies, waits for them, and re-layouts  3.6 us (3%)
  matrix products  1.84 us (1%)
  between operations  1.61 us (1%)
    ppermute x33, waiting for transfers between devices, hop(): return lax.ppermute(value, 'seq', [(i, i ^ mask) for i in range(count)])  31.5 us
    ppermute x33, starting transfers between devices, hop(): return lax.ppermute(value, 'seq', [(i, i ^ mask) for i in range(count)])  25.1 us
    pallas_call x2, Pallas kernels, expert_call(): pl.pallas_call(functools.partial(expert_kernel, len(rows), experts, seats...  19.4 us
    ppermute x12, starting transfers between devices, turn(): return lax.ppermute(value, 'req', [(i, i ^ step) for i in range(count)])  15.9 us
    ppermute x12, waiting for transfers between devices, turn(): return lax.ppermute(value, 'req', [(i, i ^ step) for i in range(count)])  12.9 us
    pallas_call x1, Pallas kernels, attend(): pl.pallas_call(functools.partial(attend_kernel, parts, mine), out_shape=(...  6.44 us
    all_to_all x1, starting transfers between devices, body(): lax.all_to_all(packed, 'seq', split_axis=0, concat_axis=0, tiled=True)  4.15 us
    pallas_call x1, Pallas kernels, fall_call(): pl.pallas_call(fall_kernel, out_shape=(shape, shape), in_specs=[full, ful...  2.86 us
  transfers between devices with their start and end apart: 46, of which 26 were waited for; matrix products, arithmetic and copies ran while one was open for 6% of the time, Pallas kernels for 10%

profile of v6, /device:TPU:0, one launch (start us, length us, event | category | flops | bytes accessed | tf_op | source)
XLA Modules:
  0.0 132.0 jit_solution(5787486370578888552)
XLA Ops:
  0.7 1.4 %constant_dynamic-slice_fusion = (bf16[1,512,2,128]{3,2,1,0:T(2,128)(2,1)S(1)}, bf16[1,512,2,128]{3,2,1,0:T(2,128)(2,1)S(1)}) fusion(bf16[1,512,2,256]{3,2,1,0:T(2,128)(2,1)} %param.14, s32[]{:T(128)S(6)} %select_n.23, s32[]{:T(128)S(6)} %select_n.21), kind=kLoop, calls=%fused_computation.59 | loop fusion | bytes 1048584 | tf_op jit(solution)/shard_map/dynamic_slice | solution.py:445
  2.6 2.6 %collective-permute-start = (bf16[512,256]{1,0:T(8,128)(2,1)S(1)}, bf16[512,256]{1,0:T(8,128)(2,1)S(1)}, u32[]{:S(2)}, u32[]{:S(2)}) collective-permute-start(bf16[512,256]{1,0:T(8,128)(2,1)S(1)} %bitcast.55), channel_id=1, source_target_pairs={{0,2},{1,3},{2,0},{3,1},{4,6},{5,7},{6,4},{7,5},{8,10},{9,11},{10,... | collective-permute-start | bytes 786440 | tf_op jit(solution)/shard_map/ppermute | solution.py:30
  5.2 1.6 %collective-permute-start.2 = (bf16[512,256]{1,0:T(8,128)(2,1)S(1)}, bf16[512,256]{1,0:T(8,128)(2,1)S(1)}, u32[]{:S(2)}, u32[]{:S(2)}) collective-permute-start(bf16[512,256]{1,0:T(8,128)(2,1)S(1)} %bitcast.62), channel_id=1, source_target_pairs={{0,4},{1,5},{2,6},{3,7},{4,0},{5,1},{6,2},{7,3},{8,12},{9,13},{10,... | collective-permute-start | bytes 786440 | tf_op jit(solution)/shard_map/ppermute | solution.py:30
  9.4 4.2 %all-to-all-start = ((bf16[8,16,768]{2,1,0:T(8,128)(2,1)}), bf16[8,16,768]{2,1,0:T(8,128)(2,1)S(1)}, u32[]{:S(2)}, u32[]{:S(2)}) async-start(bf16[8,16,768]{2,1,0:T(8,128)(2,1)} %pad_maximum_fusion.2), calls=%async_computation | async-start | bytes 393216 | tf_op jit(solution)/shard_map/all_to_all | solution.py:461
  16.2 3.7 %collective-permute-done.2.refs_3_ = bf16[512,256]{1,0:T(8,128)(2,1)S(1)} collective-permute-done((bf16[512,256]{1,0:T(8,128)(2,1)S(1)}, bf16[512,256]{1,0:T(8,128)(2,1)S(1)}, u32[]{:S(2)}, u32[]{:S(2)}) %collective-permute-start.2) | collective-permute-done | bytes 262176 | tf_op jit(solution)/shard_map/ppermute | solution.py:30
  21.8 6.4 %shard_map.140 = (bf16[64,4096]{1,0:T(8,128)(2,1)S(1)}, bf16[64,4096]{1,0:T(8,128)(2,1)S(1)}) custom-call(s32[8]{0:T(128)S(1)} %broadcast_subtract_fusion.valid_ref, bf16[128,128]{1,0:T(8,128)(2,1)S(1)} %fusion.14.perm_ref, bf16[128,768]{1,0:T(8,128)(2,1)S(1)} %bitcast.57, bf16[128,128]{1,0:T(8,128)(2,1)S(1)} %fusion.6.mask_ref, ...), custom_call_target="tpu_custom_call" | custom-call | flops 1644167168 | bytes 7405568 | tf_op jit(solution)/shard_map/pallas_call | solution.py:115
  28.5 1.8 %collective-permute-done.7 = bf16[64,4096]{1,0:T(8,128)(2,1)S(1)} collective-permute-done((bf16[64,4096]{1,0:T(8,128)(2,1)S(1)}, bf16[64,4096]{1,0:T(8,128)(2,1)S(1)}, u32[]{:S(2)}, u32[]{:S(2)}) %collective-permute-start.7) | collective-permute-done | bytes 524320 | tf_op jit(solution)/shard_map/ppermute | solution.py:30
  30.4 2.5 %collective-permute-start.8 = (bf16[16,4096]{1,0:T(8,128)(2,1)S(1)}, bf16[16,4096]{1,0:T(8,128)(2,1)S(1)}, u32[]{:S(2)}, u32[]{:S(2)}) collective-permute-start(bf16[16,4096]{1,0:T(8,128)(2,1)S(1)} %get-tuple-element.56), channel_id=1, source_target_pairs={{0,4},{1,5},{2,6},{3,7},{4,0},{5,1},{6,2},{7,3},{8,12},{9,13},{10,... | collective-permute-start | bytes 393224 | tf_op jit(solution)/shard_map/ppermute | solution.py:30
  32.9 1.5 %collective-permute-start.9 = (bf16[16,4096]{1,0:T(8,128)(2,1)S(1)}, bf16[16,4096]{1,0:T(8,128)(2,1)S(1)}, u32[]{:S(2)}, u32[]{:S(2)}) collective-permute-start(bf16[16,4096]{1,0:T(8,128)(2,1)S(1)} %get-tuple-element.58), channel_id=1, source_target_pairs={{0,2},{1,3},{2,0},{3,1},{4,6},{5,7},{6,4},{7,5},{8,10},{9,11},{10,... | collective-permute-start | bytes 393224 | tf_op jit(solution)/shard_map/ppermute | solution.py:30
  36.7 2.2 %collective-permute-done.8 = bf16[16,4096]{1,0:T(8,128)(2,1)S(1)} collective-permute-done((bf16[16,4096]{1,0:T(8,128)(2,1)S(1)}, bf16[16,4096]{1,0:T(8,128)(2,1)S(1)}, u32[]{:S(2)}, u32[]{:S(2)}) %collective-permute-start.8) | collective-permute-done | bytes 131104 | tf_op jit(solution)/shard_map/ppermute | solution.py:30
  38.8 1.3 %collective-permute-done.10 = bf16[16,4096]{1,0:T(8,128)(2,1)S(1)} collective-permute-done((bf16[16,4096]{1,0:T(8,128)(2,1)S(1)}, bf16[16,4096]{1,0:T(8,128)(2,1)S(1)}, u32[]{:S(2)}, u32[]{:S(2)}) %collective-permute-start.10) | collective-permute-done | bytes 131104 | tf_op jit(solution)/shard_map/ppermute | solution.py:30
  40.8 1.7 %fusion.10 = (bf16[16,4096]{1,0:T(8,128)(2,1)S(1)}, bf16[16,4096]{1,0:T(8,128)(2,1)}) fusion(bf16[1,16,4096]{2,1,0:T(8,128)(2,1)} %param.18, bf16[16,4096]{1,0:T(8,128)(2,1)S(1)} %collective-permute-done.10, bf16[16,4096]{1,0:T(8,128)(2,1)S(1)} %collective-permute-done.9, bf16[16,4096]{1,0:T(8,128)(2,1)S(1)} %collective-permute-done.8, ...), kind=kLoop, calls=%fused_computation.32 | loop fusion | flops 917504 | bytes 1048576 | tf_op jit(solution)/shard_map/convert_element_type | solution.py:483
  42.8 3.7 %collective-permute-start.17 = (bf16[16,2176]{1,0:T(8,128)(2,1)S(1)}, bf16[16,2176]{1,0:T(8,128)(2,1)S(1)}, u32[]{:S(2)}, u32[]{:S(2)}) collective-permute-start(bf16[16,2176]{1,0:T(8,128)(2,1)S(1)} %pad_maximum_fusion.3), channel_id=1, source_target_pairs={{0,24},{8,16},{16,8},{24,0},{1,25},{9,17},{17,9},{25,1},{2,26},{10... | collective-permute-start | bytes 208904 | tf_op jit(solution)/shard_map/ppermute | solution.py:35
  47.2 2.3 %collective-permute-done.17 = bf16[16,2176]{1,0:T(8,128)(2,1)S(1)} collective-permute-done((bf16[16,2176]{1,0:T(8,128)(2,1)S(1)}, bf16[16,2176]{1,0:T(8,128)(2,1)S(1)}, u32[]{:S(2)}, u32[]{:S(2)}) %collective-permute-start.17) | collective-permute-done | bytes 69664 | tf_op jit(solution)/shard_map/ppermute | solution.py:35
  49.6 2.4 %collective-permute-done.16 = bf16[16,2176]{1,0:T(8,128)(2,1)S(1)} collective-permute-done((bf16[16,2176]{1,0:T(8,128)(2,1)S(1)}, bf16[16,2176]{1,0:T(8,128)(2,1)S(1)}, u32[]{:S(2)}, u32[]{:S(2)}) %collective-permute-start.16) | collective-permute-done | bytes 69664 | tf_op jit(solution)/shard_map/ppermute | solution.py:35
  53.8 1.8 %collective-permute-start.18 = (bf16[64,2176]{1,0:T(8,128)(2,1)S(1)}, bf16[64,2176]{1,0:T(8,128)(2,1)S(1)}, u32[]{:S(2)}, u32[]{:S(2)}) collective-permute-start(bf16[64,2176]{1,0:T(8,128)(2,1)S(1)} %pad_maximum_fusion.refs_0_), channel_id=1, source_target_pairs={{0,6},{1,7},{2,4},{3,5},{4,2},{5,3},{6,0},{7,1},{8,14},{9,15},{10,... | collective-permute-start | bytes 835592 | tf_op jit(solution)/shard_map/ppermute | solution.py:30
  55.6 2.5 %collective-permute-start.13 = (bf16[16,2048]{1,0:T(8,128)(2,1)S(1)}, bf16[16,2048]{1,0:T(8,128)(2,1)S(1)}, u32[]{:S(2)}, u32[]{:S(2)}) collective-permute-start(bf16[16,2048]{1,0:T(8,128)(2,1)S(1)} %get-tuple-element.68), channel_id=1, source_target_pairs={{0,24},{8,16},{16,8},{24,0},{1,25},{9,17},{17,9},{25,1},{2,26},{10... | collective-permute-start | bytes 196616 | tf_op jit(solution)/shard_map/ppermute | solution.py:35
  58.1 4.2 %collective-permute-done.13 = bf16[16,2048]{1,0:T(8,128)(2,1)S(1)} collective-permute-done((bf16[16,2048]{1,0:T(8,128)(2,1)S(1)}, bf16[16,2048]{1,0:T(8,128)(2,1)S(1)}, u32[]{:S(2)}, u32[]{:S(2)}) %collective-permute-start.13) | collective-permute-done | bytes 65568 | tf_op jit(solution)/shard_map/ppermute | solution.py:35
  64.2 2.2 %collective-permute-done.18.refs_1_ = bf16[64,2176]{1,0:T(8,128)(2,1)S(1)} collective-permute-done((bf16[64,2176]{1,0:T(8,128)(2,1)S(1)}, bf16[64,2176]{1,0:T(8,128)(2,1)S(1)}, u32[]{:S(2)}, u32[]{:S(2)}) %collective-permute-start.18) | collective-permute-done | bytes 278560 | tf_op jit(solution)/shard_map/ppermute | solution.py:30
  66.6 1.7 %collective-permute-start.26 = (bf16[64,2048]{1,0:T(8,128)(2,1)S(1)}, bf16[64,2048]{1,0:T(8,128)(2,1)S(1)}, u32[]{:S(2)}, u32[]{:S(2)}) collective-permute-start(bf16[64,2048]{1,0:T(8,128)(2,1)S(1)} %pad_maximum_fusion.1.refs_0_), channel_id=1, source_target_pairs={{0,2},{1,3},{2,0},{3,1},{4,6},{5,7},{6,4},{7,5},{8,10},{9,11},{10,... | collective-permute-start | bytes 786440 | tf_op jit(solution)/shard_map/ppermute | solution.py:30
  70.2 10.2 %shard_map.141 = (f32[16,128,128]{2,1,0:T(8,128)S(1)}, f32[16,128,128]{2,1,0:T(8,128)S(1)}, bf16[512,256]{1,0:T(8,128)(2,1)S(1)}, f32[2,128,1]{2,1,0:T(8,128)S(1)}, bf16[12,128,4096]{2,1,0:T(8,128)(2,1)S(1)}) custom-call(bf16[64,2176]{1,0:T(8,128)(2,1)S(1)} %pad_maximum_fusion.refs_0_, bf16[64,2176]{1,0:T(8,128)(2,1)S(1)} %collective-permute-done.18.refs_1_, ...), custom_call_target="tpu_custom_call" | custom-call | flops 2684354560 | bytes 31457280 | tf_op jit(solution)/shard_map/pallas_call | solution.py:401
  80.4 1.5 %collective-permute-done.25.refs_2_ = bf16[64,2048]{1,0:T(8,128)(2,1)S(1)} collective-permute-done((bf16[64,2048]{1,0:T(8,128)(2,1)S(1)}, bf16[64,2048]{1,0:T(8,128)(2,1)S(1)}, u32[]{:S(2)}, u32[]{:S(2)}) %collective-permute-start.25) | collective-permute-done | bytes 262176 | tf_op jit(solution)/shard_map/ppermute | solution.py:30
  84.2 9.3 %shard_map.142 = (bf16[256,2048]{1,0:T(8,128)(2,1)S(1)}, bf16[256,2048]{1,0:T(8,128)(2,1)S(1)}, bf16[256,1024]{1,0:T(8,128)(2,1)S(1)}) custom-call(bf16[64,2048]{1,0:T(8,128)(2,1)S(1)} %pad_maximum_fusion.1.refs_0_, bf16[64,2048]{1,0:T(8,128)(2,1)S(1)} %collective-permute-done.14.refs_1_, bf16[64,2048]{1,0:T(8,128)(2,1)S(1)} %collective-permute-done.25.refs_2_, ...), custom_call_target="tpu_custom_call" | custom-call | flops 4294967296 | bytes 27262976 | tf_op jit(solution)/shard_map/pallas_call | solution.py:401
  93.6 2.9 %shard_map.143 = (bf16[256,2048]{1,0:T(8,128)(2,1)S(1)}, bf16[256,2048]{1,0:T(8,128)(2,1)S(1)}) custom-call(bf16[256,1024]{1,0:T(8,128)(2,1)S(1)} %get-tuple-element.35.hidden_ref, bf16[12,128,4096]{2,1,0:T(8,128)(2,1)S(1)} %get-tuple-element.34.refs_14_.ready_ref, bf16[512,256]{1,0:T(8,128)(2,1)S(1)} %get-tuple-element.32.refs_12_.back_ref, ...), custom_call_target="tpu_custom_call" | custom-call | flops 2684354560 | bytes 2097152 | tf_op jit(solution)/shard_map/pallas_call | solution.py:342
  97.8 1.4 %collective-permute-done.32 = bf16[256,2048]{1,0:T(8,128)(2,1)S(1)} collective-permute-done((bf16[256,2048]{1,0:T(8,128)(2,1)S(1)}, bf16[256,2048]{1,0:T(8,128)(2,1)S(1)}, u32[]{:S(2)}, u32[]{:S(2)}) %collective-permute-start.32) | collective-permute-done | bytes 1048608 | tf_op jit(solution)/shard_map/ppermute | solution.py:30
  100.5 4.9 %collective-permute-done.33 = bf16[64,2048]{1,0:T(8,128)(2,1)S(1)} collective-permute-done((bf16[64,2048]{1,0:T(8,128)(2,1)S(1)}, bf16[64,2048]{1,0:T(8,128)(2,1)S(1)}, u32[]{:S(2)}, u32[]{:S(2)}) %collective-permute-start.33) | collective-permute-done | bytes 262176 | tf_op jit(solution)/shard_map/ppermute | solution.py:30
  105.6 2.4 %collective-permute-done.34 = bf16[64,2048]{1,0:T(8,128)(2,1)S(1)} collective-permute-done((bf16[64,2048]{1,0:T(8,128)(2,1)S(1)}, bf16[64,2048]{1,0:T(8,128)(2,1)S(1)}, u32[]{:S(2)}, u32[]{:S(2)}) %collective-permute-start.34) | collective-permute-done | bytes 262176 | tf_op jit(solution)/shard_map/ppermute | solution.py:30
  109.9 5.9 %collective-permute-done.35 = bf16[64,2048]{1,0:T(8,128)(2,1)S(1)} collective-permute-done((bf16[64,2048]{1,0:T(8,128)(2,1)S(1)}, bf16[64,2048]{1,0:T(8,128)(2,1)S(1)}, u32[]{:S(2)}, u32[]{:S(2)}) %collective-permute-start.35) | collective-permute-done | bytes 262176 | tf_op jit(solution)/shard_map/ppermute | solution.py:30
  118.9 1.4 %collective-permute-start.37 = (bf16[16,2048]{1,0:T(8,128)(2,1)S(1)}, bf16[16,2048]{1,0:T(8,128)(2,1)S(1)}, u32[]{:S(2)}, u32[]{:S(2)}) collective-permute-start(bf16[16,2048]{1,0:T(8,128)(2,1)S(1)} %get-tuple-element.61), channel_id=1, source_target_pairs={{0,24},{8,16},{16,8},{24,0},{1,25},{9,17},{17,9},{25,1},{2,26},{10... | collective-permute-start | bytes 196616 | tf_op jit(solution)/shard_map/ppermute | solution.py:35
  120.6 2.8 %collective-permute-start.38 = (bf16[16,2048]{1,0:T(8,128)(2,1)S(1)}, bf16[16,2048]{1,0:T(8,128)(2,1)S(1)}, u32[]{:S(2)}, u32[]{:S(2)}) collective-permute-start(bf16[16,2048]{1,0:T(8,128)(2,1)S(1)} %get-tuple-element.63), channel_id=1, source_target_pairs={{0,16},{8,24},{16,0},{24,8},{1,17},{9,25},{17,1},{25,9},{2,18},{10... | collective-permute-start | bytes 196616 | tf_op jit(solution)/shard_map/ppermute | solution.py:35
  125.7 3.2 %collective-permute-start.43 = (bf16[16,2048]{1,0:T(8,128)(2,1)S(1)}, bf16[16,2048]{1,0:T(8,128)(2,1)S(1)}, u32[]{:S(2)}, u32[]{:S(2)}) collective-permute-start(bf16[16,2048]{1,0:T(8,128)(2,1)S(1)} %get-tuple-element.66), channel_id=1, source_target_pairs={{0,16},{8,24},{16,0},{24,8},{1,17},{9,25},{17,1},{25,9},{2,18},{10... | collective-permute-start | bytes 196616 | tf_op jit(solution)/shard_map/ppermute | solution.py:35
  128.9 1.7 %collective-permute-done.42 = bf16[16,2048]{1,0:T(8,128)(2,1)S(1)} collective-permute-done((bf16[16,2048]{1,0:T(8,128)(2,1)S(1)}, bf16[16,2048]{1,0:T(8,128)(2,1)S(1)}, u32[]{:S(2)}, u32[]{:S(2)}) %collective-permute-start.42) | collective-permute-done | bytes 65568 | tf_op jit(solution)/shard_map/ppermute | solution.py:35
  (113 shorter events, 31.2 us)
Async XLA Ops:
  2.1 19.3 %collective-permute-start.3 = (bf16[512,256]{1,0:T(8,128)(2,1)S(1)}, bf16[512,256]{1,0:T(8,128)(2,1)S(1)}, u32[]{:S(2)}, u32[]{:S(2)}) collective-permute-start(bf16[512,256]{1,0:T(8,128)(2,1)S(1)} %bitcast.54), channel_id=1, source_target_pairs={{0,1},{1,0},{2,3},{3,2},{4,5},{5,4},{6,7},{7,6},{8,9},{9,8},{10,11... | collective-permute-start | bytes 786440 | tf_op jit(solution)/shard_map/ppermute | solution.py:30
  2.6 13.0 %collective-permute-start = (bf16[512,256]{1,0:T(8,128)(2,1)S(1)}, bf16[512,256]{1,0:T(8,128)(2,1)S(1)}, u32[]{:S(2)}, u32[]{:S(2)}) collective-permute-start(bf16[512,256]{1,0:T(8,128)(2,1)S(1)} %bitcast.55), channel_id=1, source_target_pairs={{0,2},{1,3},{2,0},{3,1},{4,6},{5,7},{6,4},{7,5},{8,10},{9,11},{10,... | collective-permute-start | bytes 786440 | tf_op jit(solution)/shard_map/ppermute | solution.py:30
  5.2 14.7 %collective-permute-start.2 = (bf16[512,256]{1,0:T(8,128)(2,1)S(1)}, bf16[512,256]{1,0:T(8,128)(2,1)S(1)}, u32[]{:S(2)}, u32[]{:S(2)}) collective-permute-start(bf16[512,256]{1,0:T(8,128)(2,1)S(1)} %bitcast.62), channel_id=1, source_target_pairs={{0,4},{1,5},{2,6},{3,7},{4,0},{5,1},{6,2},{7,3},{8,12},{9,13},{10,... | collective-permute-start | bytes 786440 | tf_op jit(solution)/shard_map/ppermute | solution.py:30
  6.8 13.1 %collective-permute-start.1 = (bf16[512,256]{1,0:T(8,128)(2,1)S(1)}, bf16[512,256]{1,0:T(8,128)(2,1)S(1)}, u32[]{:S(2)}, u32[]{:S(2)}) collective-permute-start(bf16[512,256]{1,0:T(8,128)(2,1)S(1)} %bitcast.63), channel_id=1, source_target_pairs={{0,6},{1,7},{2,4},{3,5},{4,2},{5,3},{6,0},{7,1},{8,14},{9,15},{10,... | collective-permute-start | bytes 786440 | tf_op jit(solution)/shard_map/ppermute | solution.py:30
  9.4 12.0 %all-to-all-start = ((bf16[8,16,768]{2,1,0:T(8,128)(2,1)}), bf16[8,16,768]{2,1,0:T(8,128)(2,1)S(1)}, u32[]{:S(2)}, u32[]{:S(2)}) async-start(bf16[8,16,768]{2,1,0:T(8,128)(2,1)} %pad_maximum_fusion.2), calls=%async_computation | async-start | bytes 393216 | tf_op jit(solution)/shard_map/all_to_all | solution.py:461
  15.6 5.8 %collective-permute-start.4 = (bf16[512,256]{1,0:T(8,128)(2,1)S(1)}, bf16[512,256]{1,0:T(8,128)(2,1)S(1)}, u32[]{:S(2)}, u32[]{:S(2)}) collective-permute-start(bf16[512,256]{1,0:T(8,128)(2,1)S(1)} %collective-permute-done.refs_1_), channel_id=1, source_target_pairs={{0,1},{1,0},{2,3},{3,2},{4,5},{5,4},{6,7},{7,6},{8,9},{9,8},{10,11... | collective-permute-start | bytes 786440 | tf_op jit(solution)/shard_map/ppermute | solution.py:30
  30.4 8.5 %collective-permute-start.8 = (bf16[16,4096]{1,0:T(8,128)(2,1)S(1)}, bf16[16,4096]{1,0:T(8,128)(2,1)S(1)}, u32[]{:S(2)}, u32[]{:S(2)}) collective-permute-start(bf16[16,4096]{1,0:T(8,128)(2,1)S(1)} %get-tuple-element.56), channel_id=1, source_target_pairs={{0,4},{1,5},{2,6},{3,7},{4,0},{5,1},{6,2},{7,3},{8,12},{9,13},{10,... | collective-permute-start | bytes 393224 | tf_op jit(solution)/shard_map/ppermute | solution.py:30
  32.9 7.3 %collective-permute-start.10 = (bf16[16,4096]{1,0:T(8,128)(2,1)S(1)}, bf16[16,4096]{1,0:T(8,128)(2,1)S(1)}, u32[]{:S(2)}, u32[]{:S(2)}) collective-permute-start(bf16[16,4096]{1,0:T(8,128)(2,1)S(1)} %get-tuple-element.57), channel_id=1, source_target_pairs={{0,6},{1,7},{2,4},{3,5},{4,2},{5,3},{6,0},{7,1},{8,14},{9,15},{10,... | collective-permute-start | bytes 393224 | tf_op jit(solution)/shard_map/ppermute | solution.py:30
  32.9 7.9 %collective-permute-start.9 = (bf16[16,4096]{1,0:T(8,128)(2,1)S(1)}, bf16[16,4096]{1,0:T(8,128)(2,1)S(1)}, u32[]{:S(2)}, u32[]{:S(2)}) collective-permute-start(bf16[16,4096]{1,0:T(8,128)(2,1)S(1)} %get-tuple-element.58), channel_id=1, source_target_pairs={{0,2},{1,3},{2,0},{3,1},{4,6},{5,7},{6,4},{7,5},{8,10},{9,11},{10,... | collective-permute-start | bytes 393224 | tf_op jit(solution)/shard_map/ppermute | solution.py:30
  42.8 6.8 %collective-permute-start.17 = (bf16[16,2176]{1,0:T(8,128)(2,1)S(1)}, bf16[16,2176]{1,0:T(8,128)(2,1)S(1)}, u32[]{:S(2)}, u32[]{:S(2)}) collective-permute-start(bf16[16,2176]{1,0:T(8,128)(2,1)S(1)} %pad_maximum_fusion.3), channel_id=1, source_target_pairs={{0,24},{8,16},{16,8},{24,0},{1,25},{9,17},{17,9},{25,1},{2,26},{10... | collective-permute-start | bytes 208904 | tf_op jit(solution)/shard_map/ppermute | solution.py:35
  46.5 5.6 %collective-permute-start.15 = (bf16[16,2176]{1,0:T(8,128)(2,1)S(1)}, bf16[16,2176]{1,0:T(8,128)(2,1)S(1)}, u32[]{:S(2)}, u32[]{:S(2)}) collective-permute-start(bf16[16,2176]{1,0:T(8,128)(2,1)S(1)} %pad_maximum_fusion.3), channel_id=1, source_target_pairs={{0,8},{8,0},{16,24},{24,16},{1,9},{9,1},{17,25},{25,17},{2,10},{10... | collective-permute-start | bytes 208904 | tf_op jit(solution)/shard_map/ppermute | solution.py:35
  52.0 11.6 %collective-permute-start.20 = (bf16[64,2176]{1,0:T(8,128)(2,1)S(1)}, bf16[64,2176]{1,0:T(8,128)(2,1)S(1)}, u32[]{:S(2)}, u32[]{:S(2)}) collective-permute-start(bf16[64,2176]{1,0:T(8,128)(2,1)S(1)} %pad_maximum_fusion.refs_0_), channel_id=1, source_target_pairs={{0,2},{1,3},{2,0},{3,1},{4,6},{5,7},{6,4},{7,5},{8,10},{9,11},{10,... | collective-permute-start | bytes 835592 | tf_op jit(solution)/shard_map/ppermute | solution.py:30
  52.6 11.6 %collective-permute-start.19 = (bf16[64,2176]{1,0:T(8,128)(2,1)S(1)}, bf16[64,2176]{1,0:T(8,128)(2,1)S(1)}, u32[]{:S(2)}, u32[]{:S(2)}) collective-permute-start(bf16[64,2176]{1,0:T(8,128)(2,1)S(1)} %pad_maximum_fusion.refs_0_), channel_id=1, source_target_pairs={{0,4},{1,5},{2,6},{3,7},{4,0},{5,1},{6,2},{7,3},{8,12},{9,13},{10,... | collective-permute-start | bytes 835592 | tf_op jit(solution)/shard_map/ppermute | solution.py:30
  53.8 12.7 %collective-permute-start.18 = (bf16[64,2176]{1,0:T(8,128)(2,1)S(1)}, bf16[64,2176]{1,0:T(8,128)(2,1)S(1)}, u32[]{:S(2)}, u32[]{:S(2)}) collective-permute-start(bf16[64,2176]{1,0:T(8,128)(2,1)S(1)} %pad_maximum_fusion.refs_0_), channel_id=1, source_target_pairs={{0,6},{1,7},{2,4},{3,5},{4,2},{5,3},{6,0},{7,1},{8,14},{9,15},{10,... | collective-permute-start | bytes 835592 | tf_op jit(solution)/shard_map/ppermute | solution.py:30
  55.6 6.8 %collective-permute-start.13 = (bf16[16,2048]{1,0:T(8,128)(2,1)S(1)}, bf16[16,2048]{1,0:T(8,128)(2,1)S(1)}, u32[]{:S(2)}, u32[]{:S(2)}) collective-permute-start(bf16[16,2048]{1,0:T(8,128)(2,1)S(1)} %get-tuple-element.68), channel_id=1, source_target_pairs={{0,24},{8,16},{16,8},{24,0},{1,25},{9,17},{17,9},{25,1},{2,26},{10... | collective-permute-start | bytes 196616 | tf_op jit(solution)/shard_map/ppermute | solution.py:35
  63.7 5.7 %collective-permute-start.24 = (bf16[64,2176]{1,0:T(8,128)(2,1)S(1)}, bf16[64,2176]{1,0:T(8,128)(2,1)S(1)}, u32[]{:S(2)}, u32[]{:S(2)}) collective-permute-start(bf16[64,2176]{1,0:T(8,128)(2,1)S(1)} %collective-permute-done.20.refs_3_), channel_id=1, source_target_pairs={{0,1},{1,0},{2,3},{3,2},{4,5},{5,4},{6,7},{7,6},{8,9},{9,8},{10,11... | collective-permute-start | bytes 835592 | tf_op jit(solution)/shard_map/ppermute | solution.py:30
  64.2 6.0 %collective-permute-start.23 = (bf16[64,2176]{1,0:T(8,128)(2,1)S(1)}, bf16[64,2176]{1,0:T(8,128)(2,1)S(1)}, u32[]{:S(2)}, u32[]{:S(2)}) collective-permute-start(bf16[64,2176]{1,0:T(8,128)(2,1)S(1)} %collective-permute-done.19.refs_2_), channel_id=1, source_target_pairs={{0,1},{1,0},{2,3},{3,2},{4,5},{5,4},{6,7},{7,6},{8,9},{9,8},{10,11... | collective-permute-start | bytes 835592 | tf_op jit(solution)/shard_map/ppermute | solution.py:30
  66.6 13.7 %collective-permute-start.26 = (bf16[64,2048]{1,0:T(8,128)(2,1)S(1)}, bf16[64,2048]{1,0:T(8,128)(2,1)S(1)}, u32[]{:S(2)}, u32[]{:S(2)}) collective-permute-start(bf16[64,2048]{1,0:T(8,128)(2,1)S(1)} %pad_maximum_fusion.1.refs_0_), channel_id=1, source_target_pairs={{0,2},{1,3},{2,0},{3,1},{4,6},{5,7},{6,4},{7,5},{8,10},{9,11},{10,... | collective-permute-start | bytes 786440 | tf_op jit(solution)/shard_map/ppermute | solution.py:30
  68.3 13.6 %collective-permute-start.25 = (bf16[64,2048]{1,0:T(8,128)(2,1)S(1)}, bf16[64,2048]{1,0:T(8,128)(2,1)S(1)}, u32[]{:S(2)}, u32[]{:S(2)}) collective-permute-start(bf16[64,2048]{1,0:T(8,128)(2,1)S(1)} %pad_maximum_fusion.1.refs_0_), channel_id=1, source_target_pairs={{0,4},{1,5},{2,6},{3,7},{4,0},{5,1},{6,2},{7,3},{8,12},{9,13},{10,... | collective-permute-start | bytes 786440 | tf_op jit(solution)/shard_map/ppermute | solution.py:30
  69.4 12.5 %collective-permute-start.14 = (bf16[64,2048]{1,0:T(8,128)(2,1)S(1)}, bf16[64,2048]{1,0:T(8,128)(2,1)S(1)}, u32[]{:S(2)}, u32[]{:S(2)}) collective-permute-start(bf16[64,2048]{1,0:T(8,128)(2,1)S(1)} %pad_maximum_fusion.1.refs_0_), channel_id=1, source_target_pairs={{0,6},{1,7},{2,4},{3,5},{4,2},{5,3},{6,0},{7,1},{8,14},{9,15},{10,... | collective-permute-start | bytes 786440 | tf_op jit(solution)/shard_map/ppermute | solution.py:30
  70.2 12.2 %collective-permute-start.27 = (bf16[64,2048]{1,0:T(8,128)(2,1)S(1)}, bf16[64,2048]{1,0:T(8,128)(2,1)S(1)}, u32[]{:S(2)}, u32[]{:S(2)}) collective-permute-start(bf16[64,2048]{1,0:T(8,128)(2,1)S(1)} %pad_maximum_fusion.1.refs_0_), channel_id=1, source_target_pairs={{0,1},{1,0},{2,3},{3,2},{4,5},{5,4},{6,7},{7,6},{8,9},{9,8},{10,11... | collective-permute-start | bytes 786440 | tf_op jit(solution)/shard_map/ppermute | solution.py:30
  97.0 8.4 %collective-permute-start.33 = (bf16[64,2048]{1,0:T(8,128)(2,1)S(1)}, bf16[64,2048]{1,0:T(8,128)(2,1)S(1)}, u32[]{:S(2)}, u32[]{:S(2)}) collective-permute-start(bf16[64,2048]{1,0:T(8,128)(2,1)S(1)} %add_convert_fusion.4), channel_id=1, source_target_pairs={{0,2},{1,3},{2,0},{3,1},{4,6},{5,7},{6,4},{7,5},{8,10},{9,11},{10,... | collective-permute-start | bytes 786440 | tf_op jit(solution)/shard_map/ppermute | solution.py:30
  99.4 8.6 %collective-permute-start.34 = (bf16[64,2048]{1,0:T(8,128)(2,1)S(1)}, bf16[64,2048]{1,0:T(8,128)(2,1)S(1)}, u32[]{:S(2)}, u32[]{:S(2)}) collective-permute-start(bf16[64,2048]{1,0:T(8,128)(2,1)S(1)} %get-tuple-element.53), channel_id=1, source_target_pairs={{0,4},{1,5},{2,6},{3,7},{4,0},{5,1},{6,2},{7,3},{8,12},{9,13},{10,... | collective-permute-start | bytes 786440 | tf_op jit(solution)/shard_map/ppermute | solution.py:30
  108.0 7.8 %collective-permute-start.35 = (bf16[64,2048]{1,0:T(8,128)(2,1)S(1)}, bf16[64,2048]{1,0:T(8,128)(2,1)S(1)}, u32[]{:S(2)}, u32[]{:S(2)}) collective-permute-start(bf16[64,2048]{1,0:T(8,128)(2,1)S(1)} %get-tuple-element.43), channel_id=1, source_target_pairs={{0,2},{1,3},{2,0},{3,1},{4,6},{5,7},{6,4},{7,5},{8,10},{9,11},{10,... | collective-permute-start | bytes 786440 | tf_op jit(solution)/shard_map/ppermute | solution.py:30
  108.9 7.5 %collective-permute-start.36 = (bf16[64,2048]{1,0:T(8,128)(2,1)S(1)}, bf16[64,2048]{1,0:T(8,128)(2,1)S(1)}, u32[]{:S(2)}, u32[]{:S(2)}) collective-permute-start(bf16[64,2048]{1,0:T(8,128)(2,1)S(1)} %get-tuple-element.44), channel_id=1, source_target_pairs={{0,4},{1,5},{2,6},{3,7},{4,0},{5,1},{6,2},{7,3},{8,12},{9,13},{10,... | collective-permute-start | bytes 786440 | tf_op jit(solution)/shard_map/ppermute | solution.py:30
  116.5 6.9 %collective-permute-start.40 = (bf16[64,2048]{1,0:T(8,128)(2,1)S(1)}, bf16[64,2048]{1,0:T(8,128)(2,1)S(1)}, u32[]{:S(2)}, u32[]{:S(2)}) collective-permute-start(bf16[64,2048]{1,0:T(8,128)(2,1)S(1)} %add_convert_fusion.1), channel_id=1, source_target_pairs={{0,2},{1,3},{2,0},{3,1},{4,6},{5,7},{6,4},{7,5},{8,10},{9,11},{10,... | collective-permute-start | bytes 786440 | tf_op jit(solution)/shard_map/ppermute | solution.py:30
  117.9 6.4 %collective-permute-start.41 = (bf16[64,2048]{1,0:T(8,128)(2,1)S(1)}, bf16[64,2048]{1,0:T(8,128)(2,1)S(1)}, u32[]{:S(2)}, u32[]{:S(2)}) collective-permute-start(bf16[64,2048]{1,0:T(8,128)(2,1)S(1)} %get-tuple-element.47), channel_id=1, source_target_pairs={{0,4},{1,5},{2,6},{3,7},{4,0},{5,1},{6,2},{7,3},{8,12},{9,13},{10,... | collective-permute-start | bytes 786440 | tf_op jit(solution)/shard_map/ppermute | solution.py:30
  118.9 6.7 %collective-permute-start.37 = (bf16[16,2048]{1,0:T(8,128)(2,1)S(1)}, bf16[16,2048]{1,0:T(8,128)(2,1)S(1)}, u32[]{:S(2)}, u32[]{:S(2)}) collective-permute-start(bf16[16,2048]{1,0:T(8,128)(2,1)S(1)} %get-tuple-element.61), channel_id=1, source_target_pairs={{0,24},{8,16},{16,8},{24,0},{1,25},{9,17},{17,9},{25,1},{2,26},{10... | collective-permute-start | bytes 196616 | tf_op jit(solution)/shard_map/ppermute | solution.py:35
  120.3 8.5 %collective-permute-start.39 = (bf16[16,2048]{1,0:T(8,128)(2,1)S(1)}, bf16[16,2048]{1,0:T(8,128)(2,1)S(1)}, u32[]{:S(2)}, u32[]{:S(2)}) collective-permute-start(bf16[16,2048]{1,0:T(8,128)(2,1)S(1)} %get-tuple-element.62), channel_id=1, source_target_pairs={{0,8},{8,0},{16,24},{24,16},{1,9},{9,1},{17,25},{25,17},{2,10},{10... | collective-permute-start | bytes 196616 | tf_op jit(solution)/shard_map/ppermute | solution.py:35
  120.6 8.3 %collective-permute-start.38 = (bf16[16,2048]{1,0:T(8,128)(2,1)S(1)}, bf16[16,2048]{1,0:T(8,128)(2,1)S(1)}, u32[]{:S(2)}, u32[]{:S(2)}) collective-permute-start(bf16[16,2048]{1,0:T(8,128)(2,1)S(1)} %get-tuple-element.63), channel_id=1, source_target_pairs={{0,16},{8,24},{16,0},{24,8},{1,17},{9,25},{17,1},{25,9},{2,18},{10... | collective-permute-start | bytes 196616 | tf_op jit(solution)/shard_map/ppermute | solution.py:35
  124.4 6.2 %collective-permute-start.42 = (bf16[16,2048]{1,0:T(8,128)(2,1)S(1)}, bf16[16,2048]{1,0:T(8,128)(2,1)S(1)}, u32[]{:S(2)}, u32[]{:S(2)}) collective-permute-start(bf16[16,2048]{1,0:T(8,128)(2,1)S(1)} %get-tuple-element.64), channel_id=1, source_target_pairs={{0,24},{8,16},{16,8},{24,0},{1,25},{9,17},{17,9},{25,1},{2,26},{10... | collective-permute-start | bytes 196616 | tf_op jit(solution)/shard_map/ppermute | solution.py:35
  125.7 5.7 %collective-permute-start.43 = (bf16[16,2048]{1,0:T(8,128)(2,1)S(1)}, bf16[16,2048]{1,0:T(8,128)(2,1)S(1)}, u32[]{:S(2)}, u32[]{:S(2)}) collective-permute-start(bf16[16,2048]{1,0:T(8,128)(2,1)S(1)} %get-tuple-element.66), channel_id=1, source_target_pairs={{0,16},{8,24},{16,0},{24,8},{1,17},{9,25},{17,1},{25,9},{2,18},{10... | collective-permute-start | bytes 196616 | tf_op jit(solution)/shard_map/ppermute | solution.py:35
  (14 other events, 45.4 us)
